TPU v7x, 32 devices: a whole 2x2x4 slice. The times are simulated.
32 devices in a mesh: dp: 4 (over z), ctx: 4 (over x, core), exp: 2 (over y).
Axes of the slice: x: 2, y: 2, z: 4, core: 2. Of those that a mesh axis runs over, the one named last changes fastest.
Arguments:
- tokens: bfloat16 [8, 1536, 768], P(('dp', 'exp'), 'ctx'), may hold values from -6 to 6
- cotangent: bfloat16 [8, 1536, 768], P(('dp', 'exp'), 'ctx'), may hold values from -6 to 6
- previous: float32 [8, 1536, 12], P(('dp', 'exp'), 'ctx'), may hold values from -6 to 6
- routes: int32 [8, 1536, 2], P(('dp', 'exp'), 'ctx'), may hold values from 0 to 11, all different within a row; in each aligned block of 384 rows (0 to 383, 384 to 767, ..., all dimensions but the last counted through in order) at most 96 rows name the same one
- boundaries: int32 [8, 8], P(('dp', 'exp')), may hold values from 0 to 1535, as said below
- norm_first: bfloat16 [768], replicated, may hold values from 0.5 to 1.5
- query_weight: bfloat16 [768, 768], replicated, may hold values from -0.21875 to 0.21875
- key_weight: bfloat16 [768, 768], replicated, may hold values from -0.21875 to 0.21875
- value_weight: bfloat16 [768, 768], replicated, may hold values from -0.21875 to 0.21875
- output_weight: bfloat16 [768, 768], replicated, may hold values from -1.25 to 1.25
- norm_second: bfloat16 [768], replicated, may hold values from 0.5 to 1.5
- router: bfloat16 [768, 12], replicated, may hold values from -0.125 to 0.125
- gate_carry: bfloat16 [12, 12], replicated, may hold values from -1 to 1
- constant_map: bfloat16 [2, 768, 2], replicated, may hold values from -0.21875 to 0.21875
- constant_vector: bfloat16 [2, 768], replicated, may hold values from -6 to 6
- expert_gate: bfloat16 [8, 768, 2048], P('exp'), may hold values from -0.21875 to 0.21875
- expert_linear: bfloat16 [8, 768, 2048], P('exp'), may hold values from -0.21875 to 0.21875
- expert_down: bfloat16 [8, 2048, 768], P('exp'), may hold values from -0.5 to 0.5
Outputs:
- result: bfloat16 [8, 1536, 768], P(('dp', 'exp'), 'ctx')
- token_grads: float32 [8, 1536, 768], P(('dp', 'exp'), 'ctx')
- first_grads: float32 [768], replicated
- query_grads: float32 [768, 768], replicated
- key_grads: float32 [768, 768], replicated
- value_grads: float32 [768, 768], replicated
- output_grads: float32 [768, 768], replicated
- second_grads: float32 [768], replicated
- router_grads: float32 [768, 12], replicated
- carry_grads: float32 [12, 12], replicated
- map_grads: float32 [2, 768, 2], replicated
- vector_grads: float32 [2, 768], replicated
- gate_grads: float32 [8, 768, 2048], P('exp', None, 'dp')
- linear_grads: float32 [8, 768, 2048], P('exp', None, 'dp')
- down_grads: float32 [8, 2048, 768], P('exp', 'dp')
Inputs may be any that keep to these rules, and one draw needn't show every extreme that they name: `routes`: each position names two different experts; among the 384 positions of one device no expert is named more than 96 times. `boundaries`: each row rises strictly and starts with 0; one document of each stream begins within its first 384 positions and ends within its last 384.
All inputs are finite; a program needn't handle non-finite values.
Results may differ from a plain program's by a relative error of at most 0.025.
Values may be sent and summed in bfloat16 or wider, within the bound.
A program may use at most 320 MiB of HBM per device.

v0:
```python
import math

import jax
import jax.numpy as jnp
from jax import lax
from jax.sharding import PartitionSpec as P

HEAD_DIM = 64
CAP = 96


EPSILON = 1e-06
NEGATIVE = -1e30
HIGH = lax.Precision.HIGHEST


def block_rows(total_rows):
    for candidate in (512, 384, 256, 128):
        return candidate
    return total_rows


def document_ids(positions, starts):
    return jnp.sum((starts[None, :] <= positions[:, None]).astype(jnp.int32), axis=1) - 1


def rotary(values, positions, direction):
    half_dim = values.shape[-1] // 2
    frequency = jnp.exp(
        jnp.arange(half_dim, dtype=jnp.float32) * (-2.0 * math.log(10000.0) / values.shape[-1])
    )
    angles = positions.astype(jnp.float32)[:, None] * frequency[None, :]
    cosine = jnp.cos(angles)[:, None, :]
    sine_part = direction * jnp.sin(angles)[:, None, :]
    leading = values[..., :half_dim]
    trailing = values[..., half_dim:]
    return jnp.concatenate(
        [leading * cosine - trailing * sine_part, trailing * cosine + leading * sine_part], axis=-1
    )


def scores_and_mask(queries, key_block, query_pos, query_doc, key_pos, key_doc):
    scores = jnp.einsum(
        "qhd,khd->qhk", queries, key_block, preferred_element_type=jnp.float32
    ) * HEAD_DIM ** (-0.5)
    allowed = (query_doc[:, None] == key_doc[None, :]) & (key_pos[None, :] <= query_pos[:, None])
    return (scores, allowed[:, None, :])


def pair_grads(
    queries,
    output_grad,
    log_total,
    row_delta,
    query_pos,
    query_doc,
    key_block,
    value_block,
    key_pos,
    key_doc,
):
    scores, allowed = scores_and_mask(queries, key_block, query_pos, query_doc, key_pos, key_doc)
    weights = jnp.where(allowed, jnp.exp(scores - log_total[..., None]), 0.0)
    weight_grad = jnp.einsum(
        "qhd,khd->qhk", output_grad, value_block, preferred_element_type=jnp.float32
    )
    score_grad = (weights * (weight_grad - row_delta[..., None]) * HEAD_DIM ** (-0.5)).astype(
        jnp.bfloat16
    )
    return (weights.astype(jnp.bfloat16), score_grad)


def over_blocks(function, state, total_rows):
    block_size = block_rows(total_rows)

    def advance(carried, block_index):
        return (function(carried, block_index * block_size, block_size), None)

    state, unused = lax.scan(advance, state, jnp.arange(total_rows // block_size, dtype=jnp.int32))
    return state


def local(
    tokens,
    cotangent,
    previous,
    routes,
    boundaries,
    norm_first,
    query_weight,
    key_weight,
    value_weight,
    output_weight,
    norm_second,
    router,
    gate_carry,
    constant_map,
    constant_vector,
    expert_gate,
    expert_linear,
    expert_down,
):
    row_count = tokens.shape[1]
    model_width = tokens.shape[2]
    head_count = model_width // HEAD_DIM
    heads_shape = (row_count, head_count, HEAD_DIM)
    starts = boundaries[0]
    positions = lax.axis_index("ctx") * row_count + jnp.arange(row_count, dtype=jnp.int32)
    documents = document_ids(positions, starts)
    inputs = tokens[0].astype(jnp.float32)
    upstream = cotangent[0].astype(jnp.float32)
    prior = previous[0]
    chosen_routes = routes[0]
    inverse_first = lax.rsqrt(jnp.mean(inputs * inputs, axis=-1, keepdims=True) + EPSILON)
    unit_first = inputs * inverse_first
    gain_first = norm_first.astype(jnp.float32)
    normed = (unit_first * gain_first).astype(jnp.bfloat16)
    query_heads = rotary(
        jnp.dot(normed, query_weight, preferred_element_type=jnp.float32).reshape(heads_shape),
        positions,
        1.0,
    ).astype(jnp.bfloat16)
    key_heads = rotary(
        jnp.dot(normed, key_weight, preferred_element_type=jnp.float32).reshape(heads_shape),
        positions,
        1.0,
    ).astype(jnp.bfloat16)
    value_flat = jnp.dot(normed, value_weight, preferred_element_type=jnp.float32).astype(
        jnp.bfloat16
    )
    key_flat = key_heads.reshape(row_count, model_width)

    def attend(totals, shards):
        key_rows, value_rows = shards
        key_count = key_rows.shape[0]
        key_positions = jnp.arange(key_count, dtype=jnp.int32)

        def visit(state, begin, block_size):
            running_max, running_sum, accumulated = state
            key_block = lax.dynamic_slice_in_dim(key_rows, begin, block_size, 0).reshape(
                block_size, head_count, HEAD_DIM
            )
            value_block = lax.dynamic_slice_in_dim(value_rows, begin, block_size, 0).reshape(
                block_size, head_count, HEAD_DIM
            )
            key_pos = lax.dynamic_slice_in_dim(key_positions, begin, block_size, 0)
            scores, allowed = scores_and_mask(
                query_heads, key_block, positions, documents, key_pos, document_ids(key_pos, starts)
            )
            new_max = jnp.maximum(
                running_max, jnp.max(jnp.where(allowed, scores, NEGATIVE), axis=-1)
            )
            weights = jnp.where(allowed, jnp.exp(scores - new_max[..., None]), 0.0)
            factor = jnp.exp(running_max - new_max)
            running_sum = running_sum * factor + jnp.sum(weights, axis=-1)
            accumulated = accumulated * factor[..., None] + jnp.einsum(
                "qhk,khd->qhd",
                weights.astype(jnp.bfloat16),
                value_block,
                preferred_element_type=jnp.float32,
            )
            return (new_max, running_sum, accumulated)

        return over_blocks(visit, totals, key_count)

    start_state = (
        jnp.full((row_count, head_count), NEGATIVE, jnp.float32),
        jnp.zeros((row_count, head_count), jnp.float32),
        jnp.zeros(heads_shape, jnp.float32),
    )
    running_max, running_sum, accumulated = attend(
        start_state,
        (
            lax.all_gather(key_flat, "ctx", axis=0, tiled=True),
            lax.all_gather(value_flat, "ctx", axis=0, tiled=True),
        ),
    )
    attended = accumulated / running_sum[..., None]
    log_total = running_max + jnp.log(running_sum)
    attended_low = attended.reshape(row_count, model_width).astype(jnp.bfloat16)
    middle = inputs + jnp.dot(attended_low, output_weight, preferred_element_type=jnp.float32)
    inverse_second = lax.rsqrt(jnp.mean(middle * middle, axis=-1, keepdims=True) + EPSILON)
    unit_second = middle * inverse_second
    gain_second = norm_second.astype(jnp.float32)
    second = unit_second * gain_second
    second_low = second.astype(jnp.bfloat16)
    logits = jnp.dot(second_low, router, preferred_element_type=jnp.float32) + jnp.dot(
        prior, gate_carry.astype(jnp.float32), precision=HIGH
    )
    gate_probs = jax.nn.softmax(logits, axis=-1)
    expert_count = gate_probs.shape[1]
    route_hits = (
        chosen_routes[:, :, None] == jnp.arange(expert_count, dtype=jnp.int32)[None, None, :]
    ).astype(jnp.float32)
    chosen_mask = jnp.sum(route_hits, axis=1)
    gate_weights = gate_probs * chosen_mask
    route_weights = jnp.sum(route_hits * gate_probs[:, None, :], axis=-1)
    local_experts = expert_gate.shape[0]
    exchange_count = lax.axis_size("exp")
    ffn_count = local_experts * exchange_count
    ffn_hits = route_hits[:, :, :ffn_count].reshape(row_count * 2, ffn_count)
    earlier = jnp.cumsum(ffn_hits, axis=0) - ffn_hits
    slot_rank = jnp.sum(earlier * ffn_hits, axis=-1).astype(jnp.int32).reshape(row_count, 2)
    is_ffn = chosen_routes < ffn_count
    targets = jnp.where(is_ffn, chosen_routes * CAP + slot_rank, -1)
    safe_targets = jnp.maximum(targets, 0)
    slot_total = ffn_count * CAP
    slot_ids = jnp.arange(slot_total, dtype=jnp.int32)
    dispatch_first = (slot_ids[:, None] == targets[None, :, 0]).astype(jnp.bfloat16)
    dispatch_second = (slot_ids[:, None] == targets[None, :, 1]).astype(jnp.bfloat16)
    slot_shape = (exchange_count, local_experts, CAP, model_width)
    outgoing = (
        jnp.dot(dispatch_first + dispatch_second, second_low, preferred_element_type=jnp.float32)
        .astype(jnp.bfloat16)
        .reshape(slot_shape)
    )
    received = lax.all_to_all(outgoing, "exp", split_axis=0, concat_axis=0, tiled=True)
    gate_part = jnp.einsum(
        "secd,edf->secf", received, expert_gate, preferred_element_type=jnp.float32
    )
    linear_part = jnp.einsum(
        "secd,edf->secf", received, expert_linear, preferred_element_type=jnp.float32
    )
    hidden = (jax.nn.silu(gate_part) * linear_part).astype(jnp.bfloat16)
    partial_out = jnp.einsum(
        "secf,efd->secd", hidden, expert_down, preferred_element_type=jnp.float32
    )
    produced = partial_out.astype(jnp.bfloat16)
    returned = lax.all_to_all(produced, "exp", split_axis=0, concat_axis=0, tiled=True).reshape(
        slot_total, model_width
    )
    route_outputs = jnp.where(is_ffn[:, :, None], returned[safe_targets].astype(jnp.float32), 0.0)
    copy_index = ffn_count + 1
    combined = jnp.sum(route_weights[:, :, None] * route_outputs, axis=1)
    combined = combined + gate_weights[:, copy_index : copy_index + 1] * second
    mixing = jax.nn.softmax(
        jnp.einsum("td,jdc->tjc", second_low, constant_map, preferred_element_type=jnp.float32),
        axis=-1,
    )
    vectors = constant_vector.astype(jnp.float32)
    constant_terms = (
        mixing[:, :, 0:1] * second[:, None, :] + mixing[:, :, 1:2] * vectors[None, :, :]
    )
    constant_gates = gate_weights[:, ffn_count + 2 : ffn_count + 4]
    combined = combined + jnp.sum(constant_gates[:, :, None] * constant_terms, axis=1)
    result = (middle + combined).astype(jnp.bfloat16)
    ffn_weight_grad = jnp.sum(upstream[:, None, :] * route_outputs, axis=-1)
    copy_grad = jnp.sum(upstream * second, axis=-1)
    constant_weight_grad = jnp.sum(upstream[:, None, :] * constant_terms, axis=-1)
    ffn_columns = jnp.sum(route_hits[:, :, :ffn_count] * ffn_weight_grad[:, :, None], axis=1)
    gate_grad = jnp.concatenate(
        [
            ffn_columns,
            jnp.zeros((row_count, 1), jnp.float32),
            copy_grad[:, None],
            constant_weight_grad,
        ],
        axis=1,
    )
    prob_grad = gate_grad * chosen_mask
    logit_grad = gate_probs * (prob_grad - jnp.sum(gate_probs * prob_grad, axis=-1, keepdims=True))
    carry_grad = jnp.dot(prior.T, logit_grad, precision=HIGH)
    logit_low = logit_grad.astype(jnp.bfloat16)
    router_grad = jnp.dot(second_low.T, logit_low, preferred_element_type=jnp.float32)
    second_grad = jnp.dot(logit_low, router.T, preferred_element_type=jnp.float32)
    second_grad = second_grad + gate_weights[:, copy_index : copy_index + 1] * upstream
    term_grad = constant_gates[:, :, None] * upstream[:, None, :]
    second_grad = second_grad + jnp.sum(term_grad * mixing[:, :, 0:1], axis=1)
    vector_grad = jnp.sum(term_grad * mixing[:, :, 1:2], axis=0)
    mixing_grad = jnp.stack(
        [
            jnp.sum(term_grad * second[:, None, :], axis=-1),
            jnp.sum(term_grad * vectors[None, :, :], axis=-1),
        ],
        axis=-1,
    )
    map_low = (
        mixing * (mixing_grad - jnp.sum(mixing * mixing_grad, axis=-1, keepdims=True))
    ).astype(jnp.bfloat16)
    map_grad = jnp.einsum("td,tjc->jdc", second_low, map_low, preferred_element_type=jnp.float32)
    second_grad = second_grad + jnp.einsum(
        "tjc,jdc->td", map_low, constant_map, preferred_element_type=jnp.float32
    )
    route_grads = (route_weights[:, :, None] * upstream[:, None, :]).astype(jnp.bfloat16)
    sending_back = (
        (
            jnp.dot(dispatch_first, route_grads[:, 0], preferred_element_type=jnp.float32)
            + jnp.dot(dispatch_second, route_grads[:, 1], preferred_element_type=jnp.float32)
        )
        .astype(jnp.bfloat16)
        .reshape(slot_shape)
    )
    grads_in = lax.all_to_all(sending_back, "exp", split_axis=0, concat_axis=0, tiled=True)
    hidden_grad = jnp.einsum(
        "secd,efd->secf", grads_in, expert_down, preferred_element_type=jnp.float32
    )
    down_grad = jnp.einsum("secf,secd->efd", hidden, grads_in, preferred_element_type=jnp.float32)
    gate_sigmoid = jax.nn.sigmoid(gate_part)
    gate_low = (
        hidden_grad * linear_part * gate_sigmoid * (1.0 + gate_part * (1.0 - gate_sigmoid))
    ).astype(jnp.bfloat16)
    linear_low = (hidden_grad * gate_part * gate_sigmoid).astype(jnp.bfloat16)
    gate_grad_sum = jnp.einsum(
        "secd,secf->edf", received, gate_low, preferred_element_type=jnp.float32
    )
    linear_grad_sum = jnp.einsum(
        "secd,secf->edf", received, linear_low, preferred_element_type=jnp.float32
    )
    partial_in = jnp.einsum(
        "secf,edf->secd", gate_low, expert_gate, preferred_element_type=jnp.float32
    ) + jnp.einsum("secf,edf->secd", linear_low, expert_linear, preferred_element_type=jnp.float32)
    input_back = partial_in.astype(jnp.bfloat16)
    home_grads = lax.all_to_all(input_back, "exp", split_axis=0, concat_axis=0, tiled=True).reshape(
        slot_total, model_width
    )
    second_grad = second_grad + jnp.sum(
        jnp.where(is_ffn[:, :, None], home_grads[safe_targets].astype(jnp.float32), 0.0), axis=1
    )
    second_unit_grad = second_grad * gain_second
    second_gain_grad = jnp.sum(second_grad * unit_second, axis=0)
    middle_grad = upstream + inverse_second * (
        second_unit_grad
        - unit_second * jnp.mean(second_unit_grad * unit_second, axis=-1, keepdims=True)
    )
    middle_low = middle_grad.astype(jnp.bfloat16)
    output_grad = jnp.dot(attended_low.T, middle_low, preferred_element_type=jnp.float32)
    attended_grad = (
        jnp.dot(middle_low, output_weight.T, preferred_element_type=jnp.float32)
        .astype(jnp.bfloat16)
        .reshape(heads_shape)
    )
    row_delta = jnp.sum(attended_grad.astype(jnp.float32) * attended, axis=-1)
    zero_heads = jnp.zeros(heads_shape, jnp.float32)
    key_rows, value_rows = (
        lax.all_gather(key_flat, "ctx", axis=0, tiled=True),
        lax.all_gather(value_flat, "ctx", axis=0, tiled=True),
    )
    key_count = key_rows.shape[0]
    block_size = block_rows(key_count)
    key_positions = jnp.arange(key_count, dtype=jnp.int32)

    def visit(query_sum, block_index):
        begin = block_index * block_size
        key_block = lax.dynamic_slice_in_dim(key_rows, begin, block_size, 0).reshape(
            block_size, head_count, HEAD_DIM
        )
        value_block = lax.dynamic_slice_in_dim(value_rows, begin, block_size, 0).reshape(
            block_size, head_count, HEAD_DIM
        )
        key_pos = lax.dynamic_slice_in_dim(key_positions, begin, block_size, 0)
        weights_low, score_grad = pair_grads(
            query_heads,
            attended_grad,
            log_total,
            row_delta,
            positions,
            documents,
            key_block,
            value_block,
            key_pos,
            document_ids(key_pos, starts),
        )
        query_sum = query_sum + jnp.einsum(
            "qhk,khd->qhd", score_grad, key_block, preferred_element_type=jnp.float32
        )
        key_part = jnp.einsum(
            "qhk,qhd->khd", score_grad, query_heads, preferred_element_type=jnp.float32
        ).reshape(block_size, model_width)
        value_part = jnp.einsum(
            "qhk,qhd->khd", weights_low, attended_grad, preferred_element_type=jnp.float32
        ).reshape(block_size, model_width)
        return (query_sum, jnp.concatenate([key_part, value_part], axis=1))

    query_grad, key_terms = lax.scan(
        visit, zero_heads, jnp.arange(key_count // block_size, dtype=jnp.int32)
    )
    summed = lax.psum_scatter(
        key_terms.reshape(key_count, 2 * model_width).astype(jnp.bfloat16),
        "ctx",
        scatter_dimension=0,
        tiled=True,
    ).astype(jnp.float32)
    key_grad = summed[:, :model_width].reshape(heads_shape)
    value_grad = summed[:, model_width:].reshape(heads_shape)
    query_low = (
        rotary(query_grad, positions, -1.0).reshape(row_count, model_width).astype(jnp.bfloat16)
    )
    key_low = rotary(key_grad, positions, -1.0).reshape(row_count, model_width).astype(jnp.bfloat16)
    value_low = value_grad.reshape(row_count, model_width).astype(jnp.bfloat16)
    query_sum_grad = jnp.dot(normed.T, query_low, preferred_element_type=jnp.float32)
    key_sum_grad = jnp.dot(normed.T, key_low, preferred_element_type=jnp.float32)
    value_sum_grad = jnp.dot(normed.T, value_low, preferred_element_type=jnp.float32)
    first_grad = (
        jnp.dot(query_low, query_weight.T, preferred_element_type=jnp.float32)
        + jnp.dot(key_low, key_weight.T, preferred_element_type=jnp.float32)
        + jnp.dot(value_low, value_weight.T, preferred_element_type=jnp.float32)
    )
    first_unit_grad = first_grad * gain_first
    first_gain_grad = jnp.sum(first_grad * unit_first, axis=0)
    token_grad = middle_grad + inverse_first * (
        first_unit_grad
        - unit_first * jnp.mean(first_unit_grad * unit_first, axis=-1, keepdims=True)
    )
    dense = lax.psum(
        (
            first_gain_grad,
            query_sum_grad,
            key_sum_grad,
            value_sum_grad,
            output_grad,
            second_gain_grad,
            router_grad,
            carry_grad,
            map_grad,
            vector_grad,
        ),
        ("dp", "ctx", "exp"),
    )
    shares = (
        lax.psum_scatter(
            gate_grad_sum.astype(jnp.bfloat16), "dp", scatter_dimension=2, tiled=True
        ).astype(jnp.float32),
        lax.psum_scatter(
            linear_grad_sum.astype(jnp.bfloat16), "dp", scatter_dimension=2, tiled=True
        ).astype(jnp.float32),
        lax.psum_scatter(
            down_grad.astype(jnp.bfloat16), "dp", scatter_dimension=1, tiled=True
        ).astype(jnp.float32),
    )
    experts = (
        lax.psum(shares[0].astype(jnp.bfloat16), "ctx").astype(jnp.float32),
        lax.psum(shares[1].astype(jnp.bfloat16), "ctx").astype(jnp.float32),
        lax.psum(shares[2].astype(jnp.bfloat16), "ctx").astype(jnp.float32),
    )
    return (
        result[None],
        token_grad[None],
        dense[0],
        dense[1],
        dense[2],
        dense[3],
        dense[4],
        dense[5],
        dense[6],
        dense[7],
        dense[8],
        dense[9],
        experts[0],
        experts[1],
        experts[2],
    )


def solution(mesh):
    return jax.shard_map(
        local,
        mesh=mesh,
        in_specs=(
            P(("dp", "exp"), "ctx", None),
            P(("dp", "exp"), "ctx", None),
            P(("dp", "exp"), "ctx", None),
            P(("dp", "exp"), "ctx", None),
            P(("dp", "exp"), None),
            P(),
            P(),
            P(),
            P(),
            P(),
            P(),
            P(),
            P(),
            P(),
            P(),
            P("exp", None, None),
            P("exp", None, None),
            P("exp", None, None),
        ),
        out_specs=(
            P(("dp", "exp"), "ctx", None),
            P(("dp", "exp"), "ctx", None),
            P(),
            P(),
            P(),
            P(),
            P(),
            P(),
            P(),
            P(),
            P(),
            P(),
            P("exp", None, "dp"),
            P("exp", None, "dp"),
            P("exp", "dp", None),
        ),
        check_vma=False,
    )
```

profile of v0, /device:TPU:0, one launch (start us, length us, event | category | flops | bytes accessed | tf_op | source)
XLA Modules:
  0.0 1260.2 jit_solution(11941271383690279877)
XLA Ops:
  9.3 2.7 convolution_convert_fusion.2
  16.0 2.2 fusion.110
  27.1 11.8 all-gather.5.cloned.1.call-done
  38.9 4.3 copy.151
  43.2 21.9 %all-gather.3.cloned.1.call-done = bf16[1536,768]{0,1:T(8,128)(2,1)} async-done(((bf16[384,768]{0,1:T(8,128)(2,1)}), bf16[1536,768]{0,1:T(8,128)(2,1)}) %all-gather.3.cloned.1.call-update) | async-done | bytes 2359312 | tf_op jit(solution)/shard_map/all_gather | solution.py:174
  65.1 29.7 %while.32 = (s32[]{:T(128)}, f32[384,12]{0,1:T(8,128)S(1)}, f32[384,12]{0,1:T(8,128)S(1)}, f32[384,12,64]{0,2,1:T(8,128)}, s32[384]{0:T(512)S(1)}, /*index=5*/s3...) while((s32[]{:T(128)}, f32[384,12]{0,1:T(8,128)S(1)}, ...), condition=%wide.region_6.7_spmd.clone, body=%wide.region_2.6_spmd.clone.sunk | while | flops 631442304 | bytes 46519108 | solution.py:79
  69.9 1.9 fusion.230
  71.9 2.1 fusion.232
  79.8 1.9 fusion.230
  81.8 2.1 fusion.232
  91.7 2.1 fusion.232
  101.2 3.2 select_reduce_fusion
  106.4 3.6 all-to-all-start
  114.1 11.6 all-to-all-done
  125.7 4.5 all-to-all-start.2
  130.3 9.9 fusion.36
  140.2 9.9 fusion.40
  150.1 13.4 %fusion.48 = (bf16[2,4,96,2048]{3,2,0,1:T(8,128)(2,1)}, bf16[2,4,96,2048]{3,2,0,1:T(8,128)(2,1)}, bf16[2,4,96,2048]{3,2,0,1:T(8,128)(2,1)}) fusion(f32[4,2,96,2048]{3,2,1,0:T(8,128)} %fusion.36, f32[4,2,96,2048]{3,2,1,0:T(8,128)} %fusion.40, bf16[4,2048,768]{2,1,0:T(8,128)(2,1)} %param.39, bf16[2,4,96,768]{3,2,1,0:T(8,128)(2,1)} %all-to-all-done.2), kind=kOutput, calls=%fused_computation.70 | convolution fusion | flops 2441084928 | bytes 35782656 | tf_op jit(solution)/shard_map/secd,efd->secf/dot_general | solution.py:294
  163.5 10.3 bitcast_convert_fusion
  173.8 8.9 bitcast_convert_fusion.2
  182.8 8.5 bitcast_convert_fusion.1
  194.4 8.1 fusion.78
  203.7 3.6 all-to-all-start.1
  207.3 11.5 fusion.34
  218.8 10.6 fusion.81
  229.4 2.4 copy.171
  231.8 4.6 all-to-all-start.3
  238.5 3.6 gather_fusion
  242.2 3.7 reshape.511
  245.8 5.5 all-to-all-done.3
  251.3 5.4 gather_fusion.1
  256.7 3.8 reshape.512
  260.5 7.7 multiply_reduce_fusion.1
  270.3 2.5 multiply_reduce_fusion.9
  278.1 3.2 multiply_reduce_fusion.4
  284.8 2.3 multiply_reduce_fusion.5
  287.8 55.4 %while.33 = (s32[]{:T(128)}, f32[384,12,64]{0,2,1:T(8,128)S(1)}, bf16[3,512,1536]{2,1,0:T(8,128)(2,1)}, s32[3]{0:T(128)S(1)}, bf16[1536,768]{0,1:T(8,128)(2,1)},...) while((s32[]{:T(128)}, f32[384,12,64]{0,2,1:T(8,128)S(1)}, ...), condition=%wide.region_33.34_spmd.clone, body=%wide.region_31.33_spmd.clone.sunk | while | flops 1540239744 | bytes 78670784 | solution.py:374
  293.6 2.0 fusion.246
  295.6 3.6 fusion.244
  303.7 2.8 constant_dynamic-update-slice_fusion.2
  311.9 2.0 fusion.246
  314.0 3.6 fusion.244
  322.0 2.8 constant_dynamic-update-slice_fusion.2
  330.2 2.0 fusion.246
  332.3 3.6 fusion.244
  340.3 2.8 constant_dynamic-update-slice_fusion.2
  343.2 43.1 %reduce-scatter.11.cloned.1.call-done = bf16[4,512,768]{2,1,0:T(8,128)(2,1)} async-done(((bf16[4,2048,768]{2,1,0:T(8,128)(2,1)}), bf16[4,512,768]{2,1,0:T(8,128)(2,1)}) %reduce-scatter.11.cloned.1.call-update) | async-done | bytes 3145744 | tf_op jit(solution)/shard_map/reduce_scatter | solution.py:426
  386.3 215.1 %reduce-scatter.7.cloned.1.call-done = bf16[4,768,512]{2,1,0:T(8,128)(2,1)} async-done(((bf16[4,768,2048]{2,1,0:T(8,128)(2,1)}), bf16[4,768,512]{2,1,0:T(8,128)(2,1)}) %reduce-scatter.7.cloned.1.call-update) | async-done | bytes 3145744 | tf_op jit(solution)/shard_map/reduce_scatter | solution.py:420
  601.4 215.1 %reduce-scatter.9.cloned.1.call-done = bf16[4,768,512]{2,1,0:T(8,128)(2,1)} async-done(((bf16[4,768,2048]{2,1,0:T(8,128)(2,1)}), bf16[4,768,512]{2,1,0:T(8,128)(2,1)}) %reduce-scatter.9.cloned.1.call-update) | async-done | bytes 3145744 | tf_op jit(solution)/shard_map/reduce_scatter | solution.py:423
  817.6 3.4 fusion.128
  821.0 47.3 %reduce-scatter.5.cloned.1.call-done = bf16[384,1536]{1,0:T(8,128)(2,1)} async-done(((bf16[1536,1536]{1,0:T(8,128)(2,1)}), bf16[384,1536]{1,0:T(8,128)(2,1)}) %reduce-scatter.5.cloned.1.call-update) | async-done | bytes 1179664 | tf_op jit(solution)/shard_map/reduce_scatter | solution.py:377
  868.4 2.2 slice_convert_fusion
  870.6 2.7 copy.176
  875.9 2.3 fusion.114
  878.2 2.3 fusion.116
  880.5 2.3 fusion.122
  892.7 42.4 %all-reduce = (f32[768]{0:T(1024)}, f32[768]{0:T(1024)}, f32[768,12]{0,1:T(8,128)}, f32[12,12]{0,1:T(8,128)S(1)}, f32[2,768,2]{1,2,0:T(2,128)}, /*index=5*/f32[2,768]{1,0:T(2,128)}) all-reduce(f32[768]{0:T(1024)S(1)} %get-tuple-element.646, f32[768]{0:T(1024)S(1)} %copy-done.92, ...), channel_id=1, replica_groups=mesh['dp'=4,'ctx'=4,'exp'=2] {'dp','ctx','exp'}, use_global_device_ids=true, to_apply=%region_37.38 | all-reduce | flops 15504 | bytes 124032 | tf_op jit(solution)/shard_map/psum | solution.py:404
  935.8 2.6 fusion.89
  938.4 104.9 %all-reduce.8.cloned.1.call-done = (bf16[4,768,512]{2,1,0:T(8,128)(2,1)}, bf16[4,768,512]{2,1,0:T(8,128)(2,1)}, bf16[4,512,768]{2,1,0:T(8,128)(2,1)}) async-done(((bf16[4,768,512]{2,1,0:T(8,128)(2,1)}, bf16[4,768,512]{2,1,0:T(8,128)(2,1)}, bf16[4,512,768]{2,1,0:T(8,128)(2,1)}), (bf16[4,768,512]{2,1,0:T(8,128)(2,1)}, bf16[4,768,512]{2,1,0:T(8,128)(2,1)}, ...) | async-done | bytes 9437200 | tf_op jit(solution)/shard_map/psum | solution.py:431
  1043.3 5.6 convert_element_type.291
  1049.0 3.6 convert_element_type.293
  1052.5 3.2 convert_element_type.295
  1055.8 187.6 %all-reduce.6.cloned.1.call-done = (f32[768,768]{1,0:T(8,128)}, f32[768,768]{1,0:T(8,128)}, f32[768,768]{1,0:T(8,128)}, f32[768,768]{1,0:T(8,128)}) async-done(((f32[768,768]{1,0:T(8,128)}, f32[768,768]{1,0:T(8,128)}, f32[768,768]{1,0:T(8,128)}, f32[768,768]{1,0:T(8,128)}), (f32[768,768]{1,0:T(8,128)}, f32[768,768]{1,0:T(8,128)}, f32[768,768]{1,0:T(8,128)}, ...) | async-done | bytes 9437200 | tf_op jit(solution)/shard_map/psum | solution.py:404
  1243.4 3.4 copy.288
  (424 shorter events, 109.8 us)
Async XLA Ops:
  7.2 31.7 %all-gather.5.cloned.1.call-start = ((), (), s32[]{:S(2)}) async-start(), calls=%async_computation.9 | async-start | bytes 2949120 | tf_op jit(solution)/shard_map/all_gather | solution.py:175
  8.6 9.6 copy-start.72
  9.3 8.9 copy-start.60
  12.0 53.1 %all-gather.3.cloned.1.call-start = ((), (), s32[]{:S(2)}) async-start(), calls=%async_computation.8 | async-start | bytes 2949120 | tf_op jit(solution)/shard_map/all_gather | solution.py:174
  16.0 3.1 copy-start.51
  21.2 76.2 %copy-start.67 = (f32[768]{0:T(1024)}, f32[768]{0:T(1024)S(1)}, u32[]{:S(2)}) copy-start(f32[768]{0:T(1024)S(1)} %convert_element_type.255) | copy-start | bytes 9220
  21.3 3.6 copy-start.16
  21.3 3.5 copy-start.69
  21.9 3.1 copy-start.19
  97.4 3.8 copy-start.17
  99.3 94.8 %copy-start.6 = (bf16[384,768]{1,0:T(8,128)(2,1)}, bf16[384,768]{1,0:T(8,128)(2,1)S(1)}, u32[]{:S(2)}) copy-start(bf16[384,768]{1,0:T(8,128)(2,1)S(1)} %get-tuple-element.750) | copy-start | bytes 1769476
  99.3 5.3 copy-start.93
  99.3 5.3 copy-start.95
  99.8 6.6 copy-start.45
  104.5 5.5 copy-start.81
  106.4 19.3 %all-to-all-start = ((bf16[2,4,96,768]{3,2,1,0:T(8,128)(2,1)}), bf16[2,4,96,768]{3,2,1,0:T(8,128)(2,1)S(1)}, u32[]{:S(2)}, u32[]{:S(2)}) async-start(bf16[2,4,96,768]{3,2,1,0:T(8,128)(2,1)} %bitcast.407), calls=%async_computation | async-start | bytes 2359296 | tf_op jit(solution)/shard_map/all_to_all | solution.py:217
  125.7 24.4 %all-to-all-start.2 = ((bf16[2,4,96,768]{3,2,1,0:T(8,128)(2,1)}), bf16[2,4,96,768]{3,2,1,0:T(8,128)(2,1)}, u32[]{:S(2)}, u32[]{:S(2)}) async-start(bf16[2,4,96,768]{3,2,1,0:T(8,128)(2,1)} %bitcast.397), calls=%async_computation.2 | async-start | bytes 2359296 | tf_op jit(solution)/shard_map/all_to_all | solution.py:293
  130.2 256.1 %reduce-scatter.11.cloned.1.call-start = ((), (), s32[]{:S(2)}) async-start(), calls=%async_computation.13 | async-start | bytes 15728640 | tf_op jit(solution)/shard_map/reduce_scatter | solution.py:426
  173.8 427.6 %reduce-scatter.7.cloned.1.call-start = ((), (), s32[]{:S(2)}) async-start(), calls=%async_computation.11 | async-start | bytes 15728640 | tf_op jit(solution)/shard_map/reduce_scatter | solution.py:420
  182.8 633.8 %reduce-scatter.9.cloned.1.call-start = ((), (), s32[]{:S(2)}) async-start(), calls=%async_computation.12 | async-start | bytes 15728640 | tf_op jit(solution)/shard_map/reduce_scatter | solution.py:423
  194.4 8.2 copy-start.71
  194.4 8.2 copy-start.83
  194.4 81.6 %copy-start.64 = (f32[384,2,2]{0,2,1:T(2,128)}, f32[384,2,2]{0,2,1:T(2,128)S(1)}, u32[]{:S(2)}) copy-start(f32[384,2,2]{0,2,1:T(2,128)S(1)} %broadcast_divide_fusion.1) | copy-start | bytes 18436
  203.7 28.1 %all-to-all-start.1 = ((bf16[2,4,96,768]{3,2,1,0:T(8,128)(2,1)}), bf16[2,4,96,768]{3,2,1,0:T(8,128)(2,1)S(1)}, u32[]{:S(2)}, u32[]{:S(2)}) async-start(bf16[2,4,96,768]{3,2,1,0:T(8,128)(2,1)} %copy.162), calls=%async_computation.1 | async-start | bytes 2359296 | tf_op jit(solution)/shard_map/all_to_all | solution.py:229
  207.3 11.5 copy-start.10
  231.8 4.7 copy-start.94
  231.8 5.3 copy-start.48
  231.8 5.4 copy-start.46
  231.8 5.4 copy-start.66
  231.8 5.5 copy-start.76
  231.8 6.1 copy-start.30
  231.8 6.1 copy-start.39
  231.8 19.5 %all-to-all-start.3 = ((bf16[2,4,96,768]{3,2,1,0:T(8,128)(2,1)}), bf16[2,4,96,768]{3,2,1,0:T(8,128)(2,1)}, u32[]{:S(2)}, u32[]{:S(2)}) async-start(bf16[2,4,96,768]{3,2,1,0:T(8,128)(2,1)} %copy.171), calls=%async_computation.3 | async-start | bytes 2359296 | tf_op jit(solution)/shard_map/all_to_all | solution.py:313
  236.5 631.9 %reduce-scatter.5.cloned.1.call-start = ((), (), s32[]{:S(2)}) async-start(), calls=%async_computation.10 | async-start | bytes 5898240 | tf_op jit(solution)/shard_map/reduce_scatter | solution.py:377
  237.3 4.9 copy-start.49
  256.7 3.8 copy-start.11
  256.7 3.8 copy-start.82
  256.7 3.8 copy-start.87
  256.7 3.8 copy-start.97
  270.3 7.7 copy-start.13
  270.3 7.7 copy-start.15
  274.4 2.8 copy-start.50
  274.4 2.8 copy-start.56
  274.4 3.6 copy-start.63
  278.0 3.3 copy-start.59
  278.0 3.3 copy-start.20
  278.0 3.3 copy-start.21
  278.0 3.3 copy-start.68
  278.1 3.3 copy-start.79
  278.1 3.3 copy-start.90
  284.8 3.0 copy-start.1
  284.8 3.0 copy-start.70
  288.2 7.5 copy-start.31
  303.7 2.8 copy-start.32
  306.5 7.4 copy-start.31
  322.0 2.8 copy-start.32
  324.8 7.4 copy-start.31
  343.2 700.2 %all-reduce.8.cloned.1.call-start = ((), (), s32[]{:S(2)}) async-start(), calls=%async_computation.15 | async-start | bytes 18874368 | tf_op jit(solution)/shard_map/psum | solution.py:431
  816.6 426.8 %all-reduce.6.cloned.1.call-start = ((), (), s32[]{:S(2)}) async-start(), calls=%async_computation.14 | async-start | bytes 18874368 | tf_op jit(solution)/shard_map/psum | solution.py:404
  883.5 4.7 copy-start.25
  890.9 44.9 %copy-start.5 = (f32[384,768]{1,0:T(8,128)S(1)}, f32[384,768]{1,0:T(8,128)}, u32[]{:S(2)}) copy-start(f32[384,768]{1,0:T(8,128)} %copy-done.4) | copy-start | bytes 3538948
  1043.3 5.6 copy-start.28
  1048.9 3.6 copy-start.27
  1243.4 3.4 copy-start.35
  (66 other events, 115.0 us)
Sparse Core Ops, SparseCore 0:
  12.1 26.7 all-gather.4
  41.0 24.0 all-gather.2
  173.9 212.3 reduce-scatter.10
  388.5 212.8 reduce-scatter.6
  603.6 212.8 reduce-scatter.8
  819.5 48.8 reduce-scatter.4
  871.3 171.9 all-reduce.7
  1051.2 192.1 all-reduce.5
where the time goes:
time: 1280 us; the launch traced here: 1260 us
  waiting for transfers between devices  864 us (68%)
  matrix products  167 us (13%)
  local copies, waits for them, and re-layouts  87.9 us (7%)
  other arithmetic  61.8 us (5%)
  blocking collectives  42.4 us (3%)
  starting transfers between devices  16.8 us (1%)
  between operations  15.5 us (1%)
    reduce_scatter x1, waiting for transfers between devices, local(): lax.psum_scatter(gate_grad_sum.astype(jnp.bfloat16), 'dp', scatter_dimens...  215 us
    reduce_scatter x1, waiting for transfers between devices, local(): lax.psum_scatter(linear_grad_sum.astype(jnp.bfloat16), 'dp', scatter_dime...  215 us
    psum x1, waiting for transfers between devices, local(): lax.psum((first_gain_grad, query_sum_grad, key_sum_grad, value_sum_grad,...  188 us
    psum x1, waiting for transfers between devices, local(): lax.psum(shares[0].astype(jnp.bfloat16), 'ctx').astype(jnp.float32)  105 us
    reduce_scatter x1, waiting for transfers between devices, local(): lax.psum_scatter(key_terms.reshape(key_count, 2 * model_width).astype(jnp...  47.3 us
    reduce_scatter x1, waiting for transfers between devices, local(): lax.psum_scatter(down_grad.astype(jnp.bfloat16), 'dp', scatter_dimension=...  43.1 us
    psum x1, blocking collectives, local(): lax.psum((first_gain_grad, query_sum_grad, key_sum_grad, value_sum_grad,...  42.4 us
  transfers between devices with their start and end apart: 12, of which 10 were waited for; matrix products, arithmetic and copies ran while one was open for 19% of the time, Pallas kernels for 0%

commit v1 on v0

--- a/solution.py
+++ b/solution.py
@@ -3,6 +3,8 @@
 import jax
 import jax.numpy as jnp
 from jax import lax
+from jax.experimental import pallas as pl
+from jax.experimental.pallas import tpu as pltpu
 from jax.sharding import PartitionSpec as P
 
 HEAD_DIM = 64
@@ -78,6 +80,103 @@
 
     state, unused = lax.scan(advance, state, jnp.arange(total_rows // block_size, dtype=jnp.int32))
     return state
+
+
+def bits_of(axis):
+    bits, bit = [], 1
+    while bit < lax.axis_size(axis):
+        bits.append(bit)
+        bit *= 2
+    return bits
+
+
+def swap(values, axis, bit):
+    return lax.ppermute(values, axis, [(i, i ^ bit) for i in range(lax.axis_size(axis))])
+
+
+def halve(values, axis, bit, dim):
+    own = (lax.axis_index(axis) // bit) % 2
+    kept = lax.dynamic_index_in_dim(values, own, dim, keepdims=False)
+    sent = lax.dynamic_index_in_dim(values, 1 - own, dim, keepdims=False)
+    total = kept.astype(jnp.float32) + swap(sent, axis, bit).astype(jnp.float32)
+    return total.astype(jnp.bfloat16)
+
+
+def scatter_sum(values, axis):
+    bits = bits_of(axis)
+    values = values.reshape((2,) * len(bits) + values.shape[1:])
+    for place, bit in enumerate(bits):
+        values = halve(values, axis, bit, len(bits) - 1 - place)
+    return values
+
+
+def exchange(blocks, direction, ranks, name):
+    exchange_size, group_size, spread = ranks
+    count = exchange_size * group_size
+
+    def kernel(*refs):
+        arrays = len(blocks)
+        sources, targets = refs[:arrays], refs[arrays : 2 * arrays]
+        send_sem, recv_sem, local_sem = refs[2 * arrays :]
+        exp_index, ctx_index = lax.axis_index("exp"), lax.axis_index("ctx")
+        inner = lax.rem(ctx_index, spread)
+
+        def member(shift):
+            far, near = shift // group_size, shift % group_size
+            other = lax.rem(exp_index + far, exchange_size)
+            return {
+                "exp": other,
+                "ctx": lax.rem(ctx_index // spread + near, group_size) * spread + inner,
+            }
+
+        def back(shift):
+            far, near = shift // group_size, shift % group_size
+            return (exchange_size - far) % exchange_size * group_size + (
+                group_size - near
+            ) % group_size
+
+        barrier = pltpu.get_barrier_semaphore()
+        for shift in range(1, count):
+            pl.semaphore_signal(
+                barrier, inc=1, device_id=member(shift), device_id_type=pl.DeviceIdType.MESH
+            )
+        pl.semaphore_wait(barrier, count - 1)
+        copies = []
+        for index in range(arrays):
+            for shift in range(1, count):
+                copy = pltpu.make_async_remote_copy(
+                    src_ref=sources[index].at[shift],
+                    dst_ref=targets[index].at[shift],
+                    send_sem=send_sem.at[index, shift],
+                    recv_sem=recv_sem.at[index, shift],
+                    device_id=member(shift if direction > 0 else back(shift)),
+                    device_id_type=pl.DeviceIdType.MESH,
+                )
+                copy.start()
+                copies.append(copy)
+            copy = pltpu.make_async_copy(
+                sources[index].at[0], targets[index].at[0], local_sem.at[index]
+            )
+            copy.start()
+            copies.append(copy)
+        for copy in copies:
+            copy.wait()
+
+    return pl.pallas_call(
+        kernel,
+        out_shape=[jax.ShapeDtypeStruct(block.shape, block.dtype) for block in blocks],
+        in_specs=[pl.BlockSpec(memory_space=pl.ANY)] * len(blocks),
+        out_specs=[pl.BlockSpec(memory_space=pl.ANY)] * len(blocks),
+        scratch_shapes=[
+            pltpu.SemaphoreType.DMA((len(blocks), count)),
+            pltpu.SemaphoreType.DMA((len(blocks), count)),
+            pltpu.SemaphoreType.DMA((len(blocks),)),
+        ],
+        compiler_params=pltpu.CompilerParams(
+            collective_id=0 if direction > 0 else 1, has_side_effects=True
+        ),
+        name=name,
+    )(*blocks)
 
 
 def local(
@@ -198,37 +297,102 @@
     local_experts = expert_gate.shape[0]
     exchange_count = lax.axis_size("exp")
     ffn_count = local_experts * exchange_count
+    group_size = local_experts
+    spread = lax.axis_size("ctx") // group_size
+    ranks = (exchange_count, group_size, spread)
+    ctx_index = lax.axis_index("ctx")
+    far = (chosen_routes // group_size - lax.axis_index("exp")) % exchange_count
+    near = (chosen_routes % group_size - ctx_index // spread) % group_size
+    relative = far * group_size + near
     ffn_hits = route_hits[:, :, :ffn_count].reshape(row_count * 2, ffn_count)
     earlier = jnp.cumsum(ffn_hits, axis=0) - ffn_hits
     slot_rank = jnp.sum(earlier * ffn_hits, axis=-1).astype(jnp.int32).reshape(row_count, 2)
     is_ffn = chosen_routes < ffn_count
-    targets = jnp.where(is_ffn, chosen_routes * CAP + slot_rank, -1)
+    targets = jnp.where(is_ffn, relative * CAP + slot_rank, -1)
     safe_targets = jnp.maximum(targets, 0)
     slot_total = ffn_count * CAP
     slot_ids = jnp.arange(slot_total, dtype=jnp.int32)
     dispatch_first = (slot_ids[:, None] == targets[None, :, 0]).astype(jnp.bfloat16)
     dispatch_second = (slot_ids[:, None] == targets[None, :, 1]).astype(jnp.bfloat16)
-    slot_shape = (exchange_count, local_experts, CAP, model_width)
+    slot_shape = (ffn_count, CAP, model_width)
     outgoing = (
         jnp.dot(dispatch_first + dispatch_second, second_low, preferred_element_type=jnp.float32)
         .astype(jnp.bfloat16)
         .reshape(slot_shape)
     )
-    received = lax.all_to_all(outgoing, "exp", split_axis=0, concat_axis=0, tiled=True)
-    gate_part = jnp.einsum(
-        "secd,edf->secf", received, expert_gate, preferred_element_type=jnp.float32
-    )
-    linear_part = jnp.einsum(
-        "secd,edf->secf", received, expert_linear, preferred_element_type=jnp.float32
-    )
-    hidden = (jax.nn.silu(gate_part) * linear_part).astype(jnp.bfloat16)
-    partial_out = jnp.einsum(
-        "secf,efd->secd", hidden, expert_down, preferred_element_type=jnp.float32
-    )
-    produced = partial_out.astype(jnp.bfloat16)
-    returned = lax.all_to_all(produced, "exp", split_axis=0, concat_axis=0, tiled=True).reshape(
-        slot_total, model_width
-    )
+    route_grads = (route_weights[:, :, None] * upstream[:, None, :]).astype(jnp.bfloat16)
+    sending_back = (
+        (
+            jnp.dot(dispatch_first, route_grads[:, 0], preferred_element_type=jnp.float32)
+            + jnp.dot(dispatch_second, route_grads[:, 1], preferred_element_type=jnp.float32)
+        )
+        .astype(jnp.bfloat16)
+        .reshape(slot_shape)
+    )
+    received, grads_in = exchange((outgoing, sending_back), 1, ranks, "to_experts")
+    received = received.reshape(slot_total, model_width)
+    grads_in = grads_in.reshape(slot_total, model_width)
+    own_expert = ctx_index // spread
+    gate_matrix = lax.dynamic_index_in_dim(expert_gate, own_expert, 0, keepdims=False)
+    linear_matrix = lax.dynamic_index_in_dim(expert_linear, own_expert, 0, keepdims=False)
+    down_matrix = lax.dynamic_index_in_dim(expert_down, own_expert, 0, keepdims=False)
+    gate_part = jnp.dot(received, gate_matrix, preferred_element_type=jnp.float32)
+    linear_part = jnp.dot(received, linear_matrix, preferred_element_type=jnp.float32)
+    hidden_grad = jnp.dot(grads_in, down_matrix.T, preferred_element_type=jnp.float32)
+    gate_sigmoid = jax.nn.sigmoid(gate_part)
+    hidden = (gate_part * gate_sigmoid * linear_part).astype(jnp.bfloat16)
+    gate_low = (
+        hidden_grad * linear_part * gate_sigmoid * (1.0 + gate_part * (1.0 - gate_sigmoid))
+    ).astype(jnp.bfloat16)
+    linear_low = (hidden_grad * gate_part * gate_sigmoid).astype(jnp.bfloat16)
+    dp_size = lax.axis_size("dp")
+    share_width = gate_low.shape[1] // dp_size
+    split = (slot_total, dp_size, share_width)
+    down_terms = jnp.dot(hidden.T, grads_in, preferred_element_type=jnp.float32)
+    down_terms = down_terms.astype(jnp.bfloat16).reshape(dp_size, share_width, model_width)
+    gate_terms = jnp.einsum(
+        "sd,sgf->gdf", received, gate_low.reshape(split), preferred_element_type=jnp.float32
+    ).astype(jnp.bfloat16)
+    linear_terms = jnp.einsum(
+        "sd,sgf->gdf", received, linear_low.reshape(split), preferred_element_type=jnp.float32
+    ).astype(jnp.bfloat16)
+    produced = jnp.dot(hidden, down_matrix, preferred_element_type=jnp.float32)
+    input_back = jnp.dot(
+        gate_low, gate_matrix.T, preferred_element_type=jnp.float32
+    ) + jnp.dot(linear_low, linear_matrix.T, preferred_element_type=jnp.float32)
+    returned, home_grads = exchange(
+        (
+            produced.astype(jnp.bfloat16).reshape(slot_shape),
+            input_back.astype(jnp.bfloat16).reshape(slot_shape),
+        ),
+        -1,
+        ranks,
+        "from_experts",
+    )
+    returned = returned.reshape(slot_total, model_width)
+    home_grads = home_grads.reshape(slot_total, model_width)
+
+    def collect(terms):
+        share = scatter_sum(terms, "dp")
+        bit = 1
+        while bit < spread:
+            share = (
+                share.astype(jnp.float32) + swap(share, "ctx", bit).astype(jnp.float32)
+            ).astype(jnp.bfloat16)
+            bit *= 2
+        parts, order = [share], [0]
+        while bit < lax.axis_size("ctx"):
+            bit *= 2
+        while bit > spread:
+            bit //= 2
+            parts = parts + [swap(part, "ctx", bit) for part in parts]
+            order = order + [place ^ (bit // spread) for place in order]
+        stacked = jnp.stack(parts)
+        places = jnp.array(order, jnp.int32) ^ own_expert
+        inverse = jnp.argsort(places)
+        return stacked[inverse].astype(jnp.float32)
+
+    experts = (collect(gate_terms), collect(linear_terms), collect(down_terms))
     route_outputs = jnp.where(is_ffn[:, :, None], returned[safe_targets].astype(jnp.float32), 0.0)
     copy_index = ffn_count + 1
     combined = jnp.sum(route_weights[:, :, None] * route_outputs, axis=1)
@@ -280,38 +444,6 @@
     map_grad = jnp.einsum("td,tjc->jdc", second_low, map_low, preferred_element_type=jnp.float32)
     second_grad = second_grad + jnp.einsum(
         "tjc,jdc->td", map_low, constant_map, preferred_element_type=jnp.float32
-    )
-    route_grads = (route_weights[:, :, None] * upstream[:, None, :]).astype(jnp.bfloat16)
-    sending_back = (
-        (
-            jnp.dot(dispatch_first, route_grads[:, 0], preferred_element_type=jnp.float32)
-            + jnp.dot(dispatch_second, route_grads[:, 1], preferred_element_type=jnp.float32)
-        )
-        .astype(jnp.bfloat16)
-        .reshape(slot_shape)
-    )
-    grads_in = lax.all_to_all(sending_back, "exp", split_axis=0, concat_axis=0, tiled=True)
-    hidden_grad = jnp.einsum(
-        "secd,efd->secf", grads_in, expert_down, preferred_element_type=jnp.float32
-    )
-    down_grad = jnp.einsum("secf,secd->efd", hidden, grads_in, preferred_element_type=jnp.float32)
-    gate_sigmoid = jax.nn.sigmoid(gate_part)
-    gate_low = (
-        hidden_grad * linear_part * gate_sigmoid * (1.0 + gate_part * (1.0 - gate_sigmoid))
-    ).astype(jnp.bfloat16)
-    linear_low = (hidden_grad * gate_part * gate_sigmoid).astype(jnp.bfloat16)
-    gate_grad_sum = jnp.einsum(
-        "secd,secf->edf", received, gate_low, preferred_element_type=jnp.float32
-    )
-    linear_grad_sum = jnp.einsum(
-        "secd,secf->edf", received, linear_low, preferred_element_type=jnp.float32
-    )
-    partial_in = jnp.einsum(
-        "secf,edf->secd", gate_low, expert_gate, preferred_element_type=jnp.float32
-    ) + jnp.einsum("secf,edf->secd", linear_low, expert_linear, preferred_element_type=jnp.float32)
-    input_back = partial_in.astype(jnp.bfloat16)
-    home_grads = lax.all_to_all(input_back, "exp", split_axis=0, concat_axis=0, tiled=True).reshape(
-        slot_total, model_width
     )
     second_grad = second_grad + jnp.sum(
         jnp.where(is_ffn[:, :, None], home_grads[safe_targets].astype(jnp.float32), 0.0), axis=1
@@ -401,37 +533,40 @@
         first_unit_grad
         - unit_first * jnp.mean(first_unit_grad * unit_first, axis=-1, keepdims=True)
     )
-    dense = lax.psum(
-        (
-            first_gain_grad,
-            query_sum_grad,
-            key_sum_grad,
-            value_sum_grad,
-            output_grad,
-            second_gain_grad,
-            router_grad,
-            carry_grad,
-            map_grad,
-            vector_grad,
-        ),
-        ("dp", "ctx", "exp"),
-    )
-    shares = (
-        lax.psum_scatter(
-            gate_grad_sum.astype(jnp.bfloat16), "dp", scatter_dimension=2, tiled=True
-        ).astype(jnp.float32),
-        lax.psum_scatter(
-            linear_grad_sum.astype(jnp.bfloat16), "dp", scatter_dimension=2, tiled=True
-        ).astype(jnp.float32),
-        lax.psum_scatter(
-            down_grad.astype(jnp.bfloat16), "dp", scatter_dimension=1, tiled=True
-        ).astype(jnp.float32),
-    )
-    experts = (
-        lax.psum(shares[0].astype(jnp.bfloat16), "ctx").astype(jnp.float32),
-        lax.psum(shares[1].astype(jnp.bfloat16), "ctx").astype(jnp.float32),
-        lax.psum(shares[2].astype(jnp.bfloat16), "ctx").astype(jnp.float32),
-    )
+    steps = [(axis, bit) for axis in ("ctx", "exp", "dp") for bit in bits_of(axis)]
+    units = 2 ** len(steps)
+    wide = jnp.concatenate([query_sum_grad, key_sum_grad, value_sum_grad, output_grad], axis=0)
+    small_terms = (first_gain_grad, second_gain_grad, router_grad, carry_grad, map_grad, vector_grad)
+    flat = jnp.concatenate([term.reshape(-1) for term in small_terms])
+    small_rows = -(-flat.size // (units * model_width))
+    wide_rows = wide.shape[0] // units
+    unit_rows = -(-(small_rows + wide_rows) // 16) * 16
+    flat = jnp.pad(flat, (0, units * small_rows * model_width - flat.size))
+    packed = jnp.concatenate(
+        [
+            wide.reshape(units, wide_rows, model_width).astype(jnp.bfloat16),
+            flat.reshape(units, small_rows, model_width).astype(jnp.bfloat16),
+            jnp.zeros((units, unit_rows - wide_rows - small_rows, model_width), jnp.bfloat16),
+        ],
+        axis=1,
+    )
+    for axis, bit in steps:
+        packed = packed.reshape((2, -1) + packed.shape[1:])
+        packed = halve(packed, axis, bit, 0)
+    for axis, bit in steps[::-1]:
+        other = swap(packed, axis, bit)
+        own = (lax.axis_index(axis) // bit) % 2
+        packed = jnp.concatenate(
+            [jnp.where(own == 0, packed, other), jnp.where(own == 0, other, packed)], axis=0
+        )
+    packed = packed.astype(jnp.float32)
+    wide = packed[:, :wide_rows].reshape(4, model_width, model_width)
+    flat = packed[:, wide_rows : wide_rows + small_rows].reshape(-1)
+    smalls, begin = [], 0
+    for term in small_terms:
+        smalls.append(flat[begin : begin + term.size].reshape(term.shape))
+        begin += term.size
+    dense = (smalls[0], wide[0], wide[1], wide[2], wide[3]) + tuple(smalls[1:])
     return (
         result[None],
         token_grad[None],

time: 1280 us -> 766 us (0.60); the launches traced: 1260 us -> 760 us
  waiting for transfers between devices: 864 us -> 270 us
  Pallas kernels: 0 us -> 59.2 us
  local copies, waits for them, and re-layouts: 87.9 us -> 147 us
  other arithmetic: 61.8 us -> 109 us
  blocking collectives: 42.4 us -> 0 us
  matrix products: 167 us -> 129 us
    reduce_scatter x3 -> x0, waiting for transfers between devices: 473 us -> none  [the longest x1 215 us: local(): lax.psum_scatter(gate_grad_sum.astype(jnp.bfloat16), 'dp', scatter_dimens...]
    psum x2 -> x0, waiting for transfers between devices: 292 us -> none  [the longest x1 188 us: local(): lax.psum((first_gain_grad, query_sum_grad, key_sum_grad, value_sum_grad,...]
    ppermute x0 -> x25, waiting for transfers between devices: none -> 205 us  [swap(): lax.ppermute(values, axis, [(i, i ^ bit) for i in range(lax.axis_size(axi...]
    pallas_call x0 -> x2, Pallas kernels: none -> 59.2 us  [exchange(): pl.pallas_call(kernel, out_shape=[jax.ShapeDtypeStruct(block.shape, block...]
    psum x1 -> x0, blocking collectives: 42.4 us -> none  [local(): lax.psum((first_gain_grad, query_sum_grad, key_sum_grad, value_sum_grad,...]
    dot_general x9, matrix products: 91.1 us -> 52.7 us  [the longest x1 8.52 us: local(): jnp.dot(received, gate_matrix, preferred_element_type=jnp.float32)]
    ppermute x0 -> x25, starting transfers between devices: none -> 25.7 us  [swap(): lax.ppermute(values, axis, [(i, i ^ bit) for i in range(lax.axis_size(axi...]
    convert_element_type x3 -> x15, other arithmetic: 12.5 us -> 35.3 us  [the longest x11 17.9 us: halve(): return total.astype(jnp.bfloat16)]
  transfers between devices with their start and end apart: 12 -> 28, of which waited for: 10 -> 14; matrix products, arithmetic and copies ran while one was open for 19% -> 17% of each run, Pallas kernels for 0% -> 0%
where the time goes in v1:
time: 766 us; the launch traced here: 760 us
  waiting for transfers between devices  270 us (35%)
  local copies, waits for them, and re-layouts  147 us (19%)
  matrix products  129 us (17%)
  other arithmetic  109 us (14%)
  Pallas kernels  59.2 us (8%)
  starting transfers between devices  26 us (3%)
  between operations  15.5 us (2%)
    ppermute x25, waiting for transfers between devices, swap(): lax.ppermute(values, axis, [(i, i ^ bit) for i in range(lax.axis_size(axi...  205 us
    pallas_call x2, Pallas kernels, exchange(): pl.pallas_call(kernel, out_shape=[jax.ShapeDtypeStruct(block.shape, block...  59.2 us
    reduce_scatter x1, waiting for transfers between devices, local(): lax.psum_scatter(key_terms.reshape(key_count, 2 * model_width).astype(jnp...  33.7 us
    ppermute x25, starting transfers between devices, swap(): lax.ppermute(values, axis, [(i, i ^ bit) for i in range(lax.axis_size(axi...  25.7 us
    unnamed x232, local copies, waits for them, and re-layouts  24.3 us
    all_gather x1, waiting for transfers between devices, local(): lax.all_gather(key_flat, 'ctx', axis=0, tiled=True)  21.9 us
    convert_element_type x11, other arithmetic, halve(): return total.astype(jnp.bfloat16)  17.9 us
  transfers between devices with their start and end apart: 28, of which 14 were waited for; matrix products, arithmetic and copies ran while one was open for 17% of the time, Pallas kernels for 0%

profile of v1, /device:TPU:0, one launch (start us, length us, event | category | flops | bytes accessed | tf_op | source)
XLA Modules:
  0.0 760.0 jit_solution(12256346730089947125)
XLA Ops:
  9.3 2.7 convolution_convert_fusion.9
  29.7 9.2 %all-gather.5.cloned.1.call-done = bf16[1536,768]{1,0:T(8,128)(2,1)} async-done(((bf16[384,768]{1,0:T(8,128)(2,1)}), bf16[1536,768]{1,0:T(8,128)(2,1)}) %all-gather.5.cloned.1.call-update) | async-done | bytes 2359312 | tf_op jit(solution)/shard_map/all_gather | solution.py:274
  38.9 4.3 copy.174
  43.2 21.9 %all-gather.3.cloned.1.call-done = bf16[1536,768]{0,1:T(8,128)(2,1)} async-done(((bf16[384,768]{0,1:T(8,128)(2,1)}), bf16[1536,768]{0,1:T(8,128)(2,1)}) %all-gather.3.cloned.1.call-update) | async-done | bytes 2359312 | tf_op jit(solution)/shard_map/all_gather | solution.py:273
  65.1 29.7 %while.32 = (s32[]{:T(128)}, f32[384,12]{0,1:T(8,128)S(1)}, f32[384,12]{0,1:T(8,128)S(1)}, f32[384,12,64]{0,2,1:T(8,128)}, s32[384]{0:T(512)S(1)}, /*index=5*/s3...) while((s32[]{:T(128)}, f32[384,12]{0,1:T(8,128)S(1)}, ...), condition=%wide.region_6.7_spmd.clone, body=%wide.region_2.6_spmd.clone.sunk | while | flops 631442304 | bytes 46519108 | solution.py:81
  103.0 4.1 select_reduce_fusion
  119.8 2.6 convolution_convert_fusion.7
  125.0 28.0 %to_experts.1 = (bf16[8,96,768]{2,1,0:T(8,128)(2,1)}, bf16[8,96,768]{2,1,0:T(8,128)(2,1)}) custom-call(bf16[8,96,768]{2,1,0:T(8,128)(2,1)} %bitcast.475, bf16[8,96,768]{2,1,0:T(8,128)(2,1)} %bitcast.447), custom_call_target="tpu_custom_call" | custom-call | tf_op jit(solution)/shard_map/to_experts/pallas_call | solution.py:165
  153.0 7.7 %fusion.44 = f32[768,2048]{1,0:T(8,128)} fusion(bf16[768,768]{1,0:T(8,128)(2,1)} %bitcast.491, bf16[4,768,2048]{2,1,0:T(8,128)(2,1)} %param.41, s32[]{:T(128)S(6)} %select_n.312), kind=kOutput, calls=%fused_computation.83 | convolution fusion | flops 2415919104 | bytes 10616836 | tf_op jit(solution)/shard_map/dot_general | solution.py:340
  160.7 6.6 fusion.38
  167.3 8.5 %multiply_convert_fusion.1 = (bf16[768,2048]{1,0:T(8,128)(2,1)S(1)}, bf16[768,2048]{1,0:T(8,128)(2,1)S(1)}, bf16[768,2048]{1,0:T(8,128)(2,1)S(1)}) fusion(f32[768,2048]{1,0:T(8,128)} %fusion.38, f32[768,2048]{1,0:T(8,128)} %fusion.44, bf16[768,768]{1,0:T(8,128)(2,1)S(1)} %bitcast.493, bf16[4,768,2048]{2,1,0:T(8,128)(2,1)S(1)} %bitcast.490, s32[]{:T(128)S(6)} %select_n.312), kind=kOutput, calls=%fused_computation.55 | convolution fusion | flops 2441084928 | bytes 26345476 | tf_op jit(solution)/shard_map/dot_general | solution.py:339
  175.9 7.9 %fusion.67 = bf16[768,768]{1,0:T(8,128)(2,1)} fusion(bf16[768,2048]{1,0:T(8,128)(2,1)S(1)} %get-tuple-element.727, bf16[4,2048,768]{2,1,0:T(8,128)(2,1)} %param.42, s32[]{:T(128)S(6)} %select_n.312), kind=kOutput, calls=%fused_computation.125 | convolution fusion | flops 2416508928 | bytes 7471108 | tf_op jit(solution)/shard_map/dot_general | solution.py:359
  183.7 4.5 fusion.42
  188.3 3.7 add_convert_fusion
  191.9 31.2 %from_experts.1 = (bf16[8,96,768]{2,1,0:T(8,128)(2,1)}, bf16[8,96,768]{2,1,0:T(8,128)(2,1)}) custom-call(bf16[8,96,768]{2,1,0:T(8,128)(2,1)} %bitcast.476, bf16[8,96,768]{2,1,0:T(8,128)(2,1)} %bitcast.477), custom_call_target="tpu_custom_call" | custom-call | tf_op jit(solution)/shard_map/from_experts/pallas_call | solution.py:165
  223.2 5.5 gather_fusion
  228.7 3.4 gather_fusion.1
  232.1 3.7 reshape.856
  235.8 3.8 reshape.855
  239.7 7.9 %multiply_reduce_fusion.1 = (f32[384,2]{0,1:T(2,128)}, f32[384,768]{1,0:T(8,128)}, f32[384,768]{1,0:T(8,128)}, bf16[2,768]{1,0:T(2,128)(2,1)}, f32[384,2]{0,1:T(...) fusion(f32[384,2,768]{2,1,0:T(2,128)} %reshape.855, ...), kind=kLoop, calls=%fused_computation.109 | loop fusion | flops 12381696 | bytes 11831040 | tf_op jit(solution)/shard_map/reduce_sum | solution.py:411
  258.0 3.2 multiply_reduce_fusion.4
  269.4 55.1 %while.33 = (s32[]{:T(128)}, f32[384,12,64]{0,2,1:T(8,128)S(1)}, bf16[3,512,1536]{2,1,0:T(8,128)(2,1)}, s32[3]{0:T(128)S(1)}, bf16[1536,768]{0,1:T(8,128)(2,1)},...) while((s32[]{:T(128)}, f32[384,12,64]{0,2,1:T(8,128)S(1)}, ...), condition=%wide.region_33.34_spmd.clone, body=%wide.region_31.33_spmd.clone.sunk | while | flops 1540239744 | bytes 78670784 | solution.py:506
  276.9 3.6 fusion.270
  284.9 2.8 constant_dynamic-update-slice_fusion.2
  295.2 3.6 fusion.270
  303.2 2.8 constant_dynamic-update-slice_fusion.2
  313.5 3.6 fusion.270
  321.6 2.8 constant_dynamic-update-slice_fusion.2
  335.7 3.1 convolution_convert_fusion.3
  338.9 33.7 %reduce-scatter.2.cloned.1.call-done = bf16[384,1536]{1,0:T(8,128)(2,1)} async-done(((bf16[1536,1536]{1,0:T(8,128)(2,1)}), bf16[384,1536]{1,0:T(8,128)(2,1)}) %reduce-scatter.2.cloned.1.call-update) | async-done | bytes 1179664 | tf_op jit(solution)/shard_map/reduce_scatter | solution.py:509
  374.8 2.7 copy.193
  394.2 5.4 collective-permute-done
  399.6 3.3 fusion.34
  404.9 32.0 %collective-permute-done.1 = bf16[8,112,768]{2,1,0:T(8,128)(2,1)} collective-permute-done((bf16[8,112,768]{2,1,0:T(8,128)(2,1)S(1)}, bf16[8,112,768]{2,1,0:T(8,128)(2,1)}, u32[]{:S(2)}, u32[]{:S(2)}) %collective-permute-start.1) | collective-permute-done | bytes 1376288 | tf_op jit(solution)/shard_map/ppermute | solution.py:94
  440.6 15.3 %collective-permute-done.2 = bf16[4,112,768]{2,1,0:T(8,128)(2,1)} collective-permute-done((bf16[4,112,768]{2,1,0:T(8,128)(2,1)S(1)}, bf16[4,112,768]{2,1,0:T(8,128)(2,1)}, u32[]{:S(2)}, u32[]{:S(2)}) %collective-permute-start.2) | collective-permute-done | bytes 688160 | tf_op jit(solution)/shard_map/ppermute | solution.py:94
  458.7 6.2 convolution_convert_fusion
  465.0 4.6 copy.211
  469.6 4.6 copy.212
  474.3 2.8 dynamic-slice_bitcast_fusion.1
  480.2 2.8 convolution_convert_fusion.1
  483.1 30.4 %collective-permute-done.4 = bf16[1,112,768]{2,1,0:T(8,128)(2,1)S(1)} collective-permute-done((bf16[1,112,768]{2,1,0:T(8,128)(2,1)S(1)}, bf16[1,112,768]{2,1,0:T(8,128)(2,1)S(1)}, u32[]{:S(2)}, u32[]{:S(2)}) %collective-permute-start.4) | collective-permute-done | bytes 172064 | tf_op jit(solution)/shard_map/ppermute | solution.py:94
  513.5 3.4 collective-permute-start.5
  518.3 2.6 copy.203
  522.3 4.0 collective-permute-start.6
  526.3 4.8 convolution_convert_fusion.2
  531.2 32.0 %collective-permute-done.6 = bf16[2,112,768]{2,1,0:T(8,128)(2,1)S(1)} collective-permute-done((bf16[2,112,768]{2,1,0:T(8,128)(2,1)S(1)}, bf16[2,112,768]{2,1,0:T(8,128)(2,1)S(1)}, u32[]{:S(2)}, u32[]{:S(2)}) %collective-permute-start.6) | collective-permute-done | bytes 344096 | tf_op jit(solution)/shard_map/ppermute | solution.py:94
  567.4 2.7 copy.200
  575.3 3.1 collective-permute-start.21
  588.8 2.6 copy.218
  591.4 42.5 %collective-permute-done.10 = bf16[2,768,512]{2,1,0:T(8,128)(2,1)} collective-permute-done((bf16[2,768,512]{2,1,0:T(8,128)(2,1)}, bf16[2,768,512]{2,1,0:T(8,128)(2,1)}, u32[]{:S(2)}, u32[]{:S(2)}) %collective-permute-start.10) | collective-permute-done | bytes 1572896 | tf_op jit(solution)/shard_map/ppermute | solution.py:94
  638.6 25.4 %collective-permute-done.16 = bf16[768,512]{1,0:T(8,128)(2,1)} collective-permute-done((bf16[768,512]{1,0:T(8,128)(2,1)}, bf16[768,512]{1,0:T(8,128)(2,1)}, u32[]{:S(2)}, u32[]{:S(2)}) %collective-permute-start.16) | collective-permute-done | bytes 786464 | tf_op jit(solution)/shard_map/ppermute | solution.py:94
  670.3 6.8 collective-permute-done.11
  680.9 14.5 %collective-permute-done.12 = bf16[768,512]{1,0:T(8,128)(2,1)} collective-permute-done((bf16[768,512]{1,0:T(8,128)(2,1)}, bf16[768,512]{1,0:T(8,128)(2,1)}, u32[]{:S(2)}, u32[]{:S(2)}) %collective-permute-start.12) | collective-permute-done | bytes 786464 | tf_op jit(solution)/shard_map/ppermute | solution.py:94
  695.9 3.1 pad_maximum_fusion.3
  699.0 4.3 gather_fusion.4
  703.2 3.2 pad_maximum_fusion.2
  706.5 4.3 gather_fusion.3
  710.8 3.2 pad_maximum_fusion.1
  714.0 4.3 gather_fusion.2
  718.3 5.6 convert_element_type.468
  723.9 3.6 convert_element_type.479
  727.5 3.2 convert_element_type.489
  735.7 4.9 maximum_convert_fusion
  745.7 7.6 fusion.169
  (556 shorter events, 211.5 us)
Async XLA Ops:
  7.2 31.7 %all-gather.5.cloned.1.call-start = ((), (), s32[]{:S(2)}) async-start(), calls=%async_computation.2 | async-start | bytes 2949120 | tf_op jit(solution)/shard_map/all_gather | solution.py:274
  8.6 10.1 %copy-start.102 = (f32[384]{0:T(512)}, f32[384]{0:T(512)S(1)}, u32[]{:S(2)}) copy-start(f32[384]{0:T(512)S(1)} %add_rsqrt_fusion.1) | copy-start | bytes 4612
  9.3 9.4 %copy-start.94 = (f32[768]{0:T(1024)}, f32[768]{0:T(1024)S(1)}, u32[]{:S(2)}) copy-start(f32[768]{0:T(1024)S(1)} %convert_element_type.394) | copy-start | bytes 9220
  12.0 53.1 %all-gather.3.cloned.1.call-start = ((), (), s32[]{:S(2)}) async-start(), calls=%async_computation.1 | async-start | bytes 2949120 | tf_op jit(solution)/shard_map/all_gather | solution.py:273
  20.9 351.7 %reduce-scatter.2.cloned.1.call-start = ((), (), s32[]{:S(2)}) async-start(), calls=%async_computation.3 | async-start | bytes 5898240 | tf_op jit(solution)/shard_map/reduce_scatter | solution.py:509
  21.3 7.0 copy-start.22
  25.1 72.4 %copy-start.78 = (f32[768]{0:T(1024)}, f32[768]{0:T(1024)S(1)}, u32[]{:S(2)}) copy-start(f32[768]{0:T(1024)S(1)} %convert_element_type.403) | copy-start | bytes 9220
  29.7 89.3 %copy-start.15 = (f32[384,768]{1,0:T(8,128)}, f32[384,768]{1,0:T(8,128)S(1)}, u32[]{:S(2)}) copy-start(f32[384,768]{1,0:T(8,128)S(1)} %bitcast_convert_fusion) | copy-start | bytes 3538948
  29.7 35.5 %copy-start.47 = (f32[384,12]{0,1:T(8,128)S(1)}, f32[384,12]{0,1:T(8,128)}, u32[]{:S(2)}) copy-start(f32[384,12]{0,1:T(8,128)} %custom-call) | copy-start | bytes 55300
  29.7 35.5 %copy-start.57 = (f32[384,12]{0,1:T(8,128)S(1)}, f32[384,12]{0,1:T(8,128)}, u32[]{:S(2)}) copy-start(f32[384,12]{0,1:T(8,128)} %custom-call.1) | copy-start | bytes 55300
  99.7 20.1 %copy-start.8 = (bf16[384,768]{1,0:T(8,128)(2,1)}, bf16[384,768]{1,0:T(8,128)(2,1)S(1)}, u32[]{:S(2)}) copy-start(bf16[384,768]{1,0:T(8,128)(2,1)S(1)} %get-tuple-element.754) | copy-start | bytes 1769476
  100.2 15.2 %copy-start.75 = (f32[384]{0:T(512)}, f32[384]{0:T(512)S(1)}, u32[]{:S(2)}) copy-start(f32[384]{0:T(512)S(1)} %get-tuple-element.771) | copy-start | bytes 4612
  100.8 14.6 %copy-start.82 = (f32[384]{0:T(512)}, f32[384]{0:T(512)S(1)}, u32[]{:S(2)}) copy-start(f32[384]{0:T(512)S(1)} %fusion.153) | copy-start | bytes 4612
  116.1 140.7 %copy-start.74 = (f32[384,2,2]{0,2,1:T(2,128)}, f32[384,2,2]{0,2,1:T(2,128)S(1)}, u32[]{:S(2)}) copy-start(f32[384,2,2]{0,2,1:T(2,128)S(1)} %broadcast_divide_fusion.1) | copy-start | bytes 18436
  153.0 7.7 %copy-start.112 = (bf16[8,96,768]{2,1,0:T(8,128)(2,1)S(1)}, bf16[8,96,768]{2,1,0:T(8,128)(2,1)}, u32[]{:S(2)}) copy-start(bf16[8,96,768]{2,1,0:T(8,128)(2,1)} %get-tuple-element.350) | copy-start | bytes 3538948
  153.0 14.3 %slice-start = ((s8[12582912]{0:T(1024)(128)(4,1)}), s8[4194304]{0:T(1024)(128)(4,1)S(1)}, s32[]{:S(2)}) async-start(s8[12582912]{0:T(1024)(128)(4,1)} %bitcast.489), calls=%async_computation.4 | async-start | bytes 8388608
  153.0 14.3 %slice-start.1 = ((s8[12582912]{0:T(1024)(128)(4,1)}), s8[4194304]{0:T(1024)(128)(4,1)S(1)}, s32[]{:S(2)}) async-start(s8[12582912]{0:T(1024)(128)(4,1)} %bitcast.489), calls=%async_computation.5 | async-start | bytes 8388608
  160.7 6.6 slice-start.2
  160.7 6.6 copy-start.110
  175.8 7.9 %copy-start.115 = (bf16[768,2048]{1,0:T(8,128)(2,1)}, bf16[768,2048]{1,0:T(8,128)(2,1)S(1)}, u32[]{:S(2)}) copy-start(bf16[768,2048]{1,0:T(8,128)(2,1)S(1)} %get-tuple-element.727) | copy-start | bytes 9437188
  175.9 7.9 %copy-start.40 = (bf16[768,2048]{1,0:T(8,128)(2,1)}, bf16[768,2048]{1,0:T(8,128)(2,1)S(1)}, u32[]{:S(2)}) copy-start(bf16[768,2048]{1,0:T(8,128)(2,1)S(1)} %get-tuple-element.728) | copy-start | bytes 9437188
  175.9 12.4 %copy-start.41 = (bf16[768,2048]{1,0:T(8,128)(2,1)}, bf16[768,2048]{1,0:T(8,128)(2,1)S(1)}, u32[]{:S(2)}) copy-start(bf16[768,2048]{1,0:T(8,128)(2,1)S(1)} %get-tuple-element.726) | copy-start | bytes 9437188
  223.1 5.5 copy-start.1
  239.7 14.6 %copy-start.76 = (f32[384]{0:T(512)S(1)}, f32[384]{0:T(512)}, u32[]{:S(2)}) copy-start(f32[384]{0:T(512)} %copy-done.75) | copy-start | bytes 4612
  247.6 10.3 %copy-start.18 = (f32[384,768]{1,0:T(8,128)S(1)}, f32[384,768]{1,0:T(8,128)}, u32[]{:S(2)}) copy-start(f32[384,768]{1,0:T(8,128)} %copy-done.17) | copy-start | bytes 3538948
  247.6 10.3 %copy-start.21 = (bf16[1,384,768]{2,1,0:T(8,128)(2,1)S(1)}, bf16[1,384,768]{2,1,0:T(8,128)(2,1)}, u32[]{:S(2)}) copy-start(bf16[1,384,768]{2,1,0:T(8,128)(2,1)} %param.26) | copy-start | bytes 1769476
  269.4 7.4 copy-start.49
  287.7 7.4 copy-start.49
  306.0 7.4 copy-start.49
  324.6 11.1 %copy-start.52 = (bf16[384,12,64]{0,2,1:T(8,128)(2,1)S(1)}, bf16[384,12,64]{0,2,1:T(8,128)(2,1)}, u32[]{:S(2)}) copy-start(bf16[384,12,64]{0,2,1:T(8,128)(2,1)} %copy-done.51) | copy-start | bytes 1769476
  394.1 5.4 collective-permute-start
  404.5 32.4 %collective-permute-start.1 = (bf16[8,112,768]{2,1,0:T(8,128)(2,1)S(1)}, bf16[8,112,768]{2,1,0:T(8,128)(2,1)}, u32[]{:S(2)}, u32[]{:S(2)}) collective-permute-start(bf16[8,112,768]{2,1,0:T(8,128)(2,1)S(1)} %dynamic-slice_bitcast_fusion.2), channel_id=1, source_target_pairs={{0,4},{2,6},{4,0},{6,2},{1,5},{3,7},{5,1},{7,3},{8,12},{10,14},{12... | collective-permute-start | bytes 4128776 | tf_op jit(solution)/shard_map/ppermute | solution.py:94
  439.1 16.8 %collective-permute-start.2 = (bf16[4,112,768]{2,1,0:T(8,128)(2,1)S(1)}, bf16[4,112,768]{2,1,0:T(8,128)(2,1)}, u32[]{:S(2)}, u32[]{:S(2)}) collective-permute-start(bf16[4,112,768]{2,1,0:T(8,128)(2,1)S(1)} %dynamic-slice_bitcast_fusion.6), channel_id=1, source_target_pairs={{0,1},{1,0},{2,3},{3,2},{4,5},{5,4},{6,7},{7,6},{8,9},{9,8},{10,11... | collective-permute-start | bytes 2064392 | tf_op jit(solution)/shard_map/ppermute | solution.py:94
  440.6 18.1 %copy-start.113 = (bf16[8,96,768]{2,1,0:T(8,128)(2,1)S(1)}, bf16[8,96,768]{2,1,0:T(8,128)(2,1)}, u32[]{:S(2)}) copy-start(bf16[8,96,768]{2,1,0:T(8,128)(2,1)} %get-tuple-element.350) | copy-start | bytes 3538948
  457.2 20.4 %collective-permute-start.3 = (bf16[2,112,768]{2,1,0:T(8,128)(2,1)S(1)}, bf16[2,112,768]{2,1,0:T(8,128)(2,1)S(1)}, u32[]{:S(2)}, u32[]{:S(2)}) collective-permute-start(bf16[2,112,768]{2,1,0:T(8,128)(2,1)S(1)} %dynamic-slice_bitcast_fusion.7), channel_id=1, source_target_pairs={{0,8},{8,0},{16,24},{24,16},{1,9},{9,1},{17,25},{25,17},{2,10},{10... | collective-permute-start | bytes 1032200 | tf_op jit(solution)/shard_map/ppermute | solution.py:94
  474.2 6.0 copy-start.42
  474.3 6.0 copy-start.111
  477.1 95.0 %collective-permute-start.20 = (bf16[2,512,768]{2,1,0:T(8,128)(2,1)}, bf16[2,512,768]{2,1,0:T(8,128)(2,1)}, u32[]{:S(2)}, u32[]{:S(2)}) collective-permute-start(bf16[2,512,768]{2,1,0:T(8,128)(2,1)} %dynamic-slice_bitcast_fusion.1), channel_id=1, source_target_pairs={{0,8},{8,0},{16,24},{24,16},{1,9},{9,1},{17,25},{25,17},{2,10},{10... | collective-permute-start | bytes 4718600 | tf_op jit(solution)/shard_map/ppermute | solution.py:94
  477.8 35.7 %collective-permute-start.4 = (bf16[1,112,768]{2,1,0:T(8,128)(2,1)S(1)}, bf16[1,112,768]{2,1,0:T(8,128)(2,1)S(1)}, u32[]{:S(2)}, u32[]{:S(2)}) collective-permute-start(bf16[1,112,768]{2,1,0:T(8,128)(2,1)S(1)} %constant_dynamic-slice_fusion.8), channel_id=1, source_target_pairs={{0,16},{8,24},{16,0},{24,8},{1,17},{9,25},{17,1},{25,9},{2,18},{10... | collective-permute-start | bytes 516104 | tf_op jit(solution)/shard_map/ppermute | solution.py:94
  513.5 8.7 %collective-permute-start.5 = (bf16[1,112,768]{2,1,0:T(8,128)(2,1)S(1)}, bf16[1,112,768]{2,1,0:T(8,128)(2,1)S(1)}, u32[]{:S(2)}, u32[]{:S(2)}) collective-permute-start(bf16[1,112,768]{2,1,0:T(8,128)(2,1)S(1)} %add_convert_fusion.5), channel_id=1, source_target_pairs={{0,16},{8,24},{16,0},{24,8},{1,17},{9,25},{17,1},{25,9},{2,18},{10... | collective-permute-start | bytes 516104 | tf_op jit(solution)/shard_map/ppermute | solution.py:94
  520.9 61.0 %collective-permute-start.15 = (bf16[2,768,512]{2,1,0:T(8,128)(2,1)}, bf16[2,768,512]{2,1,0:T(8,128)(2,1)}, u32[]{:S(2)}, u32[]{:S(2)}) collective-permute-start(bf16[2,768,512]{2,1,0:T(8,128)(2,1)} %bitcast.471), channel_id=1, source_target_pairs={{0,8},{8,0},{16,24},{24,16},{1,9},{9,1},{17,25},{25,17},{2,10},{10... | collective-permute-start | bytes 4718600 | tf_op jit(solution)/shard_map/ppermute | solution.py:94
  522.3 40.8 %collective-permute-start.6 = (bf16[2,112,768]{2,1,0:T(8,128)(2,1)S(1)}, bf16[2,112,768]{2,1,0:T(8,128)(2,1)S(1)}, u32[]{:S(2)}, u32[]{:S(2)}) collective-permute-start(bf16[2,112,768]{2,1,0:T(8,128)(2,1)S(1)} %pad_maximum_fusion.9), channel_id=1, source_target_pairs={{0,8},{8,0},{16,24},{24,16},{1,9},{9,1},{17,25},{25,17},{2,10},{10... | collective-permute-start | bytes 1032200 | tf_op jit(solution)/shard_map/ppermute | solution.py:94
  564.1 14.9 %collective-permute-start.7 = (bf16[4,112,768]{2,1,0:T(8,128)(2,1)S(1)}, bf16[4,112,768]{2,1,0:T(8,128)(2,1)}, u32[]{:S(2)}, u32[]{:S(2)}) collective-permute-start(bf16[4,112,768]{2,1,0:T(8,128)(2,1)S(1)} %pad_maximum_fusion.6), channel_id=1, source_target_pairs={{0,1},{1,0},{2,3},{3,2},{4,5},{5,4},{6,7},{7,6},{8,9},{9,8},{10,11... | collective-permute-start | bytes 2064392 | tf_op jit(solution)/shard_map/ppermute | solution.py:94
  570.2 63.8 %collective-permute-start.10 = (bf16[2,768,512]{2,1,0:T(8,128)(2,1)}, bf16[2,768,512]{2,1,0:T(8,128)(2,1)}, u32[]{:S(2)}, u32[]{:S(2)}) collective-permute-start(bf16[2,768,512]{2,1,0:T(8,128)(2,1)} %bitcast.472), channel_id=1, source_target_pairs={{0,8},{8,0},{16,24},{24,16},{1,9},{9,1},{17,25},{25,17},{2,10},{10... | collective-permute-start | bytes 4718600 | tf_op jit(solution)/shard_map/ppermute | solution.py:94
  575.3 61.1 %collective-permute-start.21 = (bf16[512,768]{1,0:T(8,128)(2,1)}, bf16[512,768]{1,0:T(8,128)(2,1)}, u32[]{:S(2)}, u32[]{:S(2)}) collective-permute-start(bf16[512,768]{1,0:T(8,128)(2,1)} %dynamic-slice_bitcast_fusion.3), channel_id=1, source_target_pairs={{0,16},{8,24},{16,0},{24,8},{1,17},{9,25},{17,1},{25,9},{2,18},{10... | collective-permute-start | bytes 2359304 | tf_op jit(solution)/shard_map/ppermute | solution.py:94
  581.5 85.2 %collective-permute-start.8 = (bf16[8,112,768]{2,1,0:T(8,128)(2,1)}, bf16[8,112,768]{2,1,0:T(8,128)(2,1)}, u32[]{:S(2)}, u32[]{:S(2)}) collective-permute-start(bf16[8,112,768]{2,1,0:T(8,128)(2,1)} %pad_maximum_fusion.5), channel_id=1, source_target_pairs={{0,4},{2,6},{4,0},{6,2},{1,5},{3,7},{5,1},{7,3},{8,12},{10,14},{12... | collective-permute-start | bytes 4128776 | tf_op jit(solution)/shard_map/ppermute | solution.py:94
  586.4 77.6 %collective-permute-start.16 = (bf16[768,512]{1,0:T(8,128)(2,1)}, bf16[768,512]{1,0:T(8,128)(2,1)}, u32[]{:S(2)}, u32[]{:S(2)}) collective-permute-start(bf16[768,512]{1,0:T(8,128)(2,1)} %dynamic-slice_bitcast_fusion.4), channel_id=1, source_target_pairs={{0,16},{8,24},{16,0},{24,8},{1,17},{9,25},{17,1},{25,9},{2,18},{10... | collective-permute-start | bytes 2359304 | tf_op jit(solution)/shard_map/ppermute | solution.py:94
  636.3 27.6 %copy-start.24 = (bf16[2,768,512]{2,1,0:T(8,128)(2,1)S(1)}, bf16[2,768,512]{2,1,0:T(8,128)(2,1)}, u32[]{:S(2)}) copy-start(bf16[2,768,512]{2,1,0:T(8,128)(2,1)} %copy-done.23) | copy-start | bytes 4718596
  636.3 40.7 %collective-permute-start.11 = (bf16[768,512]{1,0:T(8,128)(2,1)S(1)}, bf16[768,512]{1,0:T(8,128)(2,1)S(1)}, u32[]{:S(2)}, u32[]{:S(2)}) collective-permute-start(bf16[768,512]{1,0:T(8,128)(2,1)S(1)} %dynamic-slice_bitcast_fusion.5), channel_id=1, source_target_pairs={{0,16},{8,24},{16,0},{24,8},{1,17},{9,25},{17,1},{25,9},{2,18},{10... | collective-permute-start | bytes 2359304 | tf_op jit(solution)/shard_map/ppermute | solution.py:94
  637.9 30.4 %copy-start.38 = (bf16[512,768]{1,0:T(8,128)(2,1)}, bf16[512,768]{1,0:T(8,128)(2,1)S(1)}, u32[]{:S(2)}) copy-start(bf16[512,768]{1,0:T(8,128)(2,1)S(1)} %fusion.62) | copy-start | bytes 2359300
  637.9 28.9 %copy-start.28 = (bf16[4,112,768]{2,1,0:T(8,128)(2,1)S(1)}, bf16[4,112,768]{2,1,0:T(8,128)(2,1)}, u32[]{:S(2)}) copy-start(bf16[4,112,768]{2,1,0:T(8,128)(2,1)} %copy-done.27) | copy-start | bytes 2064388
  637.9 40.8 %collective-permute-start.23 = (bf16[512,768]{1,0:T(8,128)(2,1)S(1)}, bf16[512,768]{1,0:T(8,128)(2,1)S(1)}, u32[]{:S(2)}, u32[]{:S(2)}) collective-permute-start(bf16[512,768]{1,0:T(8,128)(2,1)S(1)} %fusion.62), channel_id=1, source_target_pairs={{0,2},{2,0},{4,6},{6,4},{1,3},{3,1},{5,7},{7,5},{8,10},{10,8},{12,... | collective-permute-start | bytes 2359304 | tf_op jit(solution)/shard_map/ppermute | solution.py:94
  638.0 40.7 %collective-permute-start.22 = (bf16[512,768]{1,0:T(8,128)(2,1)S(1)}, bf16[512,768]{1,0:T(8,128)(2,1)}, u32[]{:S(2)}, u32[]{:S(2)}) collective-permute-start(bf16[512,768]{1,0:T(8,128)(2,1)S(1)} %fusion.62), channel_id=1, source_target_pairs={{0,4},{2,6},{4,0},{6,2},{1,5},{3,7},{5,1},{7,3},{8,12},{10,14},{12... | collective-permute-start | bytes 2359304 | tf_op jit(solution)/shard_map/ppermute | solution.py:94
  666.2 13.9 %collective-permute-start.17 = (bf16[768,512]{1,0:T(8,128)(2,1)}, bf16[768,512]{1,0:T(8,128)(2,1)}, u32[]{:S(2)}, u32[]{:S(2)}) collective-permute-start(bf16[768,512]{1,0:T(8,128)(2,1)} %fusion.63), channel_id=1, source_target_pairs={{0,4},{2,6},{4,0},{6,2},{1,5},{3,7},{5,1},{7,3},{8,12},{10,14},{12... | collective-permute-start | bytes 2359304 | tf_op jit(solution)/shard_map/ppermute | solution.py:94
  670.3 9.8 %copy-start.114 = (s32[4]{0:T(128)S(1)}, s32[4]{0:T(128)}, u32[]{:S(2)}) copy-start(s32[4]{0:T(128)} %constant.390.clone) | copy-start | bytes 52
  670.3 25.6 %copy-start.39 = (bf16[512,768]{1,0:T(8,128)(2,1)S(1)}, bf16[512,768]{1,0:T(8,128)(2,1)}, u32[]{:S(2)}) copy-start(bf16[512,768]{1,0:T(8,128)(2,1)} %copy-done.38) | copy-start | bytes 2359300
  670.3 61.9 %collective-permute-start.9 = (bf16[16,112,768]{2,1,0:T(8,128)(2,1)}, bf16[16,112,768]{2,1,0:T(8,128)(2,1)}, u32[]{:S(2)}, u32[]{:S(2)}) collective-permute-start(bf16[16,112,768]{2,1,0:T(8,128)(2,1)} %pad_maximum_fusion.4), channel_id=1, source_target_pairs={{0,2},{2,0},{4,6},{6,4},{1,3},{3,1},{5,7},{7,5},{8,10},{10,8},{12,... | collective-permute-start | bytes 8257544 | tf_op jit(solution)/shard_map/ppermute | solution.py:94
  678.1 17.2 %collective-permute-start.12 = (bf16[768,512]{1,0:T(8,128)(2,1)}, bf16[768,512]{1,0:T(8,128)(2,1)}, u32[]{:S(2)}, u32[]{:S(2)}) collective-permute-start(bf16[768,512]{1,0:T(8,128)(2,1)} %fusion.64), channel_id=1, source_target_pairs={{0,4},{2,6},{4,0},{6,2},{1,5},{3,7},{5,1},{7,3},{8,12},{10,14},{12... | collective-permute-start | bytes 2359304 | tf_op jit(solution)/shard_map/ppermute | solution.py:94
  678.7 16.6 %collective-permute-start.24 = (bf16[512,768]{1,0:T(8,128)(2,1)}, bf16[512,768]{1,0:T(8,128)(2,1)}, u32[]{:S(2)}, u32[]{:S(2)}) collective-permute-start(bf16[512,768]{1,0:T(8,128)(2,1)} %collective-permute-done.22), channel_id=1, source_target_pairs={{0,2},{2,0},{4,6},{6,4},{1,3},{3,1},{5,7},{7,5},{8,10},{10,8},{12,... | collective-permute-start | bytes 2359304 | tf_op jit(solution)/shard_map/ppermute | solution.py:94
  679.6 23.7 %collective-permute-start.18 = (bf16[768,512]{1,0:T(8,128)(2,1)}, bf16[768,512]{1,0:T(8,128)(2,1)}, u32[]{:S(2)}, u32[]{:S(2)}) collective-permute-start(bf16[768,512]{1,0:T(8,128)(2,1)} %fusion.63), channel_id=1, source_target_pairs={{0,2},{2,0},{4,6},{6,4},{1,3},{3,1},{5,7},{7,5},{8,10},{10,8},{12,... | collective-permute-start | bytes 2359304 | tf_op jit(solution)/shard_map/ppermute | solution.py:94
  680.1 23.2 %collective-permute-start.19 = (bf16[768,512]{1,0:T(8,128)(2,1)}, bf16[768,512]{1,0:T(8,128)(2,1)}, u32[]{:S(2)}, u32[]{:S(2)}) collective-permute-start(bf16[768,512]{1,0:T(8,128)(2,1)} %collective-permute-done.17), channel_id=1, source_target_pairs={{0,2},{2,0},{4,6},{6,4},{1,3},{3,1},{5,7},{7,5},{8,10},{10,8},{12,... | collective-permute-start | bytes 2359304 | tf_op jit(solution)/shard_map/ppermute | solution.py:94
  695.3 15.4 %collective-permute-start.13 = (bf16[768,512]{1,0:T(8,128)(2,1)}, bf16[768,512]{1,0:T(8,128)(2,1)}, u32[]{:S(2)}, u32[]{:S(2)}) collective-permute-start(bf16[768,512]{1,0:T(8,128)(2,1)} %fusion.64), channel_id=1, source_target_pairs={{0,2},{2,0},{4,6},{6,4},{1,3},{3,1},{5,7},{7,5},{8,10},{10,8},{12,... | collective-permute-start | bytes 2359304 | tf_op jit(solution)/shard_map/ppermute | solution.py:94
  695.3 15.4 %collective-permute-start.14 = (bf16[768,512]{1,0:T(8,128)(2,1)}, bf16[768,512]{1,0:T(8,128)(2,1)}, u32[]{:S(2)}, u32[]{:S(2)}) collective-permute-start(bf16[768,512]{1,0:T(8,128)(2,1)} %collective-permute-done.12), channel_id=1, source_target_pairs={{0,2},{2,0},{4,6},{6,4},{1,3},{3,1},{5,7},{7,5},{8,10},{10,8},{12,... | collective-permute-start | bytes 2359304 | tf_op jit(solution)/shard_map/ppermute | solution.py:94
  718.3 5.6 copy-start.11
  (99 other events, 241.6 us)
Sparse Core Ops, SparseCore 0:
  12.1 26.7 all-gather.4
  41.0 24.0 all-gather.2
  324.7 47.8 reduce-scatter.1

commit v2 on v1

--- a/solution.py
+++ b/solution.py
@@ -110,73 +110,291 @@
     return values
 
 
-def exchange(blocks, direction, ranks, name):
+def mesh_id(exp_index, ctx_index):
+    return {"exp": exp_index, "ctx": ctx_index}
+
+
+def dot(left, right):
+    return jnp.dot(left, right, preferred_element_type=jnp.float32)
+
+
+def dot_nt(left, right):
+    return lax.dot_general(
+        left, right, (((1,), (1,)), ((), ())), preferred_element_type=jnp.float32
+    )
+
+
+def dot_tn(left, right):
+    return lax.dot_general(
+        left, right, (((0,), (0,)), ((), ())), preferred_element_type=jnp.float32
+    )
+
+
+def member_of(shift, ranks):
     exchange_size, group_size, spread = ranks
-    count = exchange_size * group_size
-
-    def kernel(*refs):
-        arrays = len(blocks)
-        sources, targets = refs[:arrays], refs[arrays : 2 * arrays]
-        send_sem, recv_sem, local_sem = refs[2 * arrays :]
-        exp_index, ctx_index = lax.axis_index("exp"), lax.axis_index("ctx")
-        inner = lax.rem(ctx_index, spread)
-
-        def member(shift):
-            far, near = shift // group_size, shift % group_size
-            other = lax.rem(exp_index + far, exchange_size)
-            return {
-                "exp": other,
-                "ctx": lax.rem(ctx_index // spread + near, group_size) * spread + inner,
-            }
-
-        def back(shift):
-            far, near = shift // group_size, shift % group_size
-            return (exchange_size - far) % exchange_size * group_size + (
-                group_size - near
-            ) % group_size
-
-        barrier = pltpu.get_barrier_semaphore()
-        for shift in range(1, count):
-            pl.semaphore_signal(
-                barrier, inc=1, device_id=member(shift), device_id_type=pl.DeviceIdType.MESH
-            )
-        pl.semaphore_wait(barrier, count - 1)
-        copies = []
-        for index in range(arrays):
-            for shift in range(1, count):
-                copy = pltpu.make_async_remote_copy(
-                    src_ref=sources[index].at[shift],
-                    dst_ref=targets[index].at[shift],
-                    send_sem=send_sem.at[index, shift],
-                    recv_sem=recv_sem.at[index, shift],
-                    device_id=member(shift if direction > 0 else back(shift)),
-                    device_id_type=pl.DeviceIdType.MESH,
-                )
-                copy.start()
-                copies.append(copy)
-            copy = pltpu.make_async_copy(
-                sources[index].at[0], targets[index].at[0], local_sem.at[index]
-            )
+    exp_index, ctx_index = lax.axis_index("exp"), lax.axis_index("ctx")
+    far, near = shift // group_size, shift % group_size
+    place = jnp.bitwise_xor(ctx_index // spread, near) * spread + lax.rem(ctx_index, spread)
+    return mesh_id(jnp.bitwise_xor(exp_index, far), place)
+
+
+def greet(count, ranks):
+    barrier = pltpu.get_barrier_semaphore()
+    for shift in range(1, count):
+        pl.semaphore_signal(
+            barrier, inc=1, device_id=member_of(shift, ranks), device_id_type=pl.DeviceIdType.MESH
+        )
+    pl.semaphore_wait(barrier, count - 1)
+
+
+def send_block(source, target, shift, ranks, send_sem, recv_sem):
+    return pltpu.make_async_remote_copy(
+        src_ref=source.at[shift],
+        dst_ref=target.at[shift],
+        send_sem=send_sem.at[shift],
+        recv_sem=recv_sem.at[shift],
+        device_id=member_of(shift, ranks),
+        device_id_type=pl.DeviceIdType.MESH,
+    )
+
+
+def exchange(block, ranks, collective_id, name):
+    count = ranks[0] * ranks[1]
+
+    def kernel(source, target, send_sem, recv_sem, local_sem):
+        greet(count, ranks)
+        copies = [
+            send_block(source, target, shift, ranks, send_sem, recv_sem)
+            for shift in range(1, count)
+        ]
+        copies.append(pltpu.make_async_copy(source.at[0], target.at[0], local_sem))
+        for copy in copies:
             copy.start()
-            copies.append(copy)
         for copy in copies:
             copy.wait()
 
     return pl.pallas_call(
         kernel,
-        out_shape=[jax.ShapeDtypeStruct(block.shape, block.dtype) for block in blocks],
-        in_specs=[pl.BlockSpec(memory_space=pl.ANY)] * len(blocks),
-        out_specs=[pl.BlockSpec(memory_space=pl.ANY)] * len(blocks),
+        out_shape=jax.ShapeDtypeStruct(block.shape, block.dtype),
+        in_specs=[pl.BlockSpec(memory_space=pl.ANY)],
+        out_specs=pl.BlockSpec(memory_space=pl.ANY),
         scratch_shapes=[
-            pltpu.SemaphoreType.DMA((len(blocks), count)),
-            pltpu.SemaphoreType.DMA((len(blocks), count)),
-            pltpu.SemaphoreType.DMA((len(blocks),)),
+            pltpu.SemaphoreType.DMA((count,)),
+            pltpu.SemaphoreType.DMA((count,)),
+            pltpu.SemaphoreType.DMA,
+        ],
+        compiler_params=pltpu.CompilerParams(collective_id=collective_id, has_side_effects=True),
+        name=name,
+    )(block)
+
+
+def expert_layer(outgoing, gates, grads, weights, ranks, shares):
+    count, cap, width = outgoing.shape
+    hidden_units = weights[0].shape[2]
+    rows = count * cap
+    share = hidden_units // shares
+    spread = ranks[2]
+
+    def kernel(
+        outgoing_ref,
+        gates_ref,
+        grads_ref,
+        gate_hbm,
+        linear_hbm,
+        down_hbm,
+        back_ref,
+        output_ref,
+        dots_ref,
+        gate_terms,
+        linear_terms,
+        down_terms,
+        received,
+        received_gates,
+        gate_w,
+        linear_w,
+        down_w,
+        hidden_grad,
+        hidden,
+        gate_low,
+        linear_low,
+        rows_t,
+        scaled,
+        gate_column,
+        out_total,
+        in_total,
+        out_send,
+        in_send,
+        dots_send,
+        terms,
+        weight_sem,
+        send_sem,
+        recv_sem,
+        local_sem,
+        terms_sem,
+    ):
+        own = lax.axis_index("ctx") // spread
+        loads = [
+            pltpu.make_async_copy(source.at[own], target, weight_sem.at[index])
+            for index, (source, target) in enumerate(
+                ((down_hbm, down_w), (gate_hbm, gate_w), (linear_hbm, linear_w))
+            )
+        ]
+        for load in loads:
+            load.start()
+        greet(count, ranks)
+
+        def send_all(source, target, index):
+            copies = [
+                send_block(source, target, shift, ranks, send_sem.at[index], recv_sem.at[index])
+                for shift in range(1, count)
+            ]
+            copies.append(
+                pltpu.make_async_copy(source.at[0], target.at[0], local_sem.at[index])
+            )
+            for copy in copies:
+                copy.start()
+            return copies
+
+        incoming = send_all(gates_ref, received_gates, 0) + send_all(outgoing_ref, received, 1)
+        loads[0].wait()
+
+        def backward_in(index, carry):
+            part = pl.ds(pl.multiple_of(index * share, share), share)
+            hidden_grad[:, part] = dot_nt(grads_ref[...], down_w[part, :])
+            return carry
+
+        lax.fori_loop(0, shares, backward_in, 0)
+        for copy in incoming + loads[1:]:
+            copy.wait()
+        for shift in range(count):
+            column = jnp.transpose(received_gates[shift])[:cap, 0:1]
+            block = pl.ds(shift * cap, cap)
+            gate_column[block, :] = jnp.broadcast_to(column, (cap, 128))
+            scaled[block, :] = (column * grads_ref[block, :].astype(jnp.float32)).astype(
+                jnp.bfloat16
+            )
+        tokens = received[...].reshape(rows, width)
+        rows_t[...] = jnp.transpose(tokens)
+
+        def through(index, carry):
+            part = pl.ds(pl.multiple_of(index * share, share), share)
+            tokens = received[...].reshape(rows, width)
+            gate_part = dot(tokens, gate_w[:, part])
+            linear_part = dot(tokens, linear_w[:, part])
+            sigmoid = 1.0 / (1.0 + jnp.exp(-gate_part))
+            silu = gate_part * sigmoid
+            low = (silu * linear_part).astype(jnp.bfloat16)
+            hidden[:, part] = low
+            upper = hidden_grad[:, part] * gate_column[:, 0:1]
+            low_gate = (
+                upper * linear_part * sigmoid * (1.0 + gate_part * (1.0 - sigmoid))
+            ).astype(jnp.bfloat16)
+            gate_low[:, part] = low_gate
+            low_linear = (upper * silu).astype(jnp.bfloat16)
+            linear_low[:, part] = low_linear
+            out = dot(low, down_w[part, :])
+            back = dot_nt(low_gate, gate_w[:, part]) + dot_nt(low_linear, linear_w[:, part])
+
+            @pl.when(index == 0)
+            def _():
+                out_total[...] = out
+                in_total[...] = back
+
+            @pl.when(index > 0)
+            def _():
+                out_total[...] += out
+                in_total[...] += back
+
+            return carry
+
+        lax.fori_loop(0, shares, through, 0)
+        in_send[...] = in_total[...].astype(jnp.bfloat16).reshape(count, cap, width)
+        going = send_all(in_send, back_ref, 2)
+        low = out_total[...].astype(jnp.bfloat16)
+        out_send[...] = low.reshape(count, cap, width)
+        dots = jnp.sum(
+            low.astype(jnp.float32) * grads_ref[...].astype(jnp.float32), axis=1, keepdims=True
+        )
+        for shift in range(count):
+            column = jnp.broadcast_to(dots[shift * cap : (shift + 1) * cap], (cap, 128))
+            dots_send[shift, :, 0:cap] = jnp.transpose(column)[0:8, :]
+            dots_send[shift, :, cap:] = jnp.zeros((8, 128 - cap), jnp.float32)
+        going = going + send_all(dots_send, dots_ref, 3) + send_all(out_send, output_ref, 4)
+
+        def term_copy(which, index):
+            target = (down_terms, gate_terms, linear_terms)[which]
+            return pltpu.make_async_copy(
+                terms[which].at[index], target.at[index], terms_sem.at[which, index]
+            )
+
+        def weigh(index, carry):
+            part = pl.ds(pl.multiple_of(index * share, share), share)
+            terms[0][index] = dot_tn(hidden[:, part], scaled[...]).astype(jnp.bfloat16)
+            term_copy(0, index).start()
+            terms[1][index] = dot(rows_t[...], gate_low[:, part]).astype(jnp.bfloat16)
+            term_copy(1, index).start()
+            terms[2][index] = dot(rows_t[...], linear_low[:, part]).astype(jnp.bfloat16)
+            term_copy(2, index).start()
+            return carry
+
+        lax.fori_loop(0, shares, weigh, 0)
+        for which in range(3):
+            for index in range(shares):
+                term_copy(which, index).wait()
+        for copy in going:
+            copy.wait()
+
+    low, full = jnp.bfloat16, jnp.float32
+    columns, lines = (shares, width, share), (shares, share, width)
+    any_space = pl.BlockSpec(memory_space=pl.ANY)
+    in_vmem = pl.BlockSpec(memory_space=pltpu.VMEM)
+    return pl.pallas_call(
+        kernel,
+        out_shape=[
+            jax.ShapeDtypeStruct(outgoing.shape, low),
+            jax.ShapeDtypeStruct(outgoing.shape, low),
+            jax.ShapeDtypeStruct(gates.shape, full),
+            jax.ShapeDtypeStruct(columns, low),
+            jax.ShapeDtypeStruct(columns, low),
+            jax.ShapeDtypeStruct(lines, low),
+        ],
+        in_specs=[in_vmem, in_vmem, in_vmem, any_space, any_space, any_space],
+        out_specs=[any_space] * 6,
+        scratch_shapes=[
+            pltpu.VMEM(outgoing.shape, low),
+            pltpu.VMEM(gates.shape, full),
+            pltpu.VMEM((width, hidden_units), low),
+            pltpu.VMEM((width, hidden_units), low),
+            pltpu.VMEM((hidden_units, width), low),
+            pltpu.VMEM((rows, hidden_units), full),
+            pltpu.VMEM((rows, hidden_units), low),
+            pltpu.VMEM((rows, hidden_units), low),
+            pltpu.VMEM((rows, hidden_units), low),
+            pltpu.VMEM((width, rows), low),
+            pltpu.VMEM((rows, width), low),
+            pltpu.VMEM((rows, 128), full),
+            pltpu.VMEM((rows, width), full),
+            pltpu.VMEM((rows, width), full),
+            pltpu.VMEM(outgoing.shape, low),
+            pltpu.VMEM(outgoing.shape, low),
+            pltpu.VMEM(gates.shape, full),
+            [pltpu.VMEM(lines, low), pltpu.VMEM(columns, low), pltpu.VMEM(columns, low)],
+            pltpu.SemaphoreType.DMA((3,)),
+            pltpu.SemaphoreType.DMA((5, count)),
+            pltpu.SemaphoreType.DMA((5, count)),
+            pltpu.SemaphoreType.DMA((5,)),
+            pltpu.SemaphoreType.DMA((3, shares)),
         ],
         compiler_params=pltpu.CompilerParams(
-            collective_id=0 if direction > 0 else 1, has_side_effects=True
+            collective_id=1, has_side_effects=True, vmem_limit_bytes=60 * 2**20
         ),
-        name=name,
-    )(*blocks)
+        cost_estimate=pl.CostEstimate(
+            flops=18 * rows * width * hidden_units,
+            bytes_accessed=12 * width * hidden_units + 12 * rows * width,
+            transcendentals=rows * hidden_units,
+        ),
+        name="experts",
+    )(outgoing, gates, grads, *weights)
 
 
 def local(
@@ -301,8 +519,8 @@
     spread = lax.axis_size("ctx") // group_size
     ranks = (exchange_count, group_size, spread)
     ctx_index = lax.axis_index("ctx")
-    far = (chosen_routes // group_size - lax.axis_index("exp")) % exchange_count
-    near = (chosen_routes % group_size - ctx_index // spread) % group_size
+    far = jnp.bitwise_xor(chosen_routes // group_size, lax.axis_index("exp"))
+    near = jnp.bitwise_xor(chosen_routes % group_size, ctx_index // spread)
     relative = far * group_size + near
     ffn_hits = route_hits[:, :, :ffn_count].reshape(row_count * 2, ffn_count)
     earlier = jnp.cumsum(ffn_hits, axis=0) - ffn_hits
@@ -320,57 +538,34 @@
         .astype(jnp.bfloat16)
         .reshape(slot_shape)
     )
-    route_grads = (route_weights[:, :, None] * upstream[:, None, :]).astype(jnp.bfloat16)
-    sending_back = (
-        (
-            jnp.dot(dispatch_first, route_grads[:, 0], preferred_element_type=jnp.float32)
-            + jnp.dot(dispatch_second, route_grads[:, 1], preferred_element_type=jnp.float32)
-        )
+    sending_grads = (
+        jnp.dot(dispatch_first + dispatch_second, cotangent[0], preferred_element_type=jnp.float32)
         .astype(jnp.bfloat16)
         .reshape(slot_shape)
     )
-    received, grads_in = exchange((outgoing, sending_back), 1, ranks, "to_experts")
-    received = received.reshape(slot_total, model_width)
-    grads_in = grads_in.reshape(slot_total, model_width)
+    grads_in = exchange(sending_grads, ranks, 0, "grads_to_experts")
+    weights_first = jnp.where(
+        slot_ids[:, None] == targets[None, :, 0], route_weights[None, :, 0], 0.0
+    )
+    weights_second = jnp.where(
+        slot_ids[:, None] == targets[None, :, 1], route_weights[None, :, 1], 0.0
+    )
+    slot_gates = jnp.sum(weights_first + weights_second, axis=1).reshape(ffn_count, 1, CAP)
+    slot_gates = jnp.broadcast_to(
+        jnp.pad(slot_gates, ((0, 0), (0, 0), (0, 128 - CAP))), (ffn_count, 8, 128)
+    )
     own_expert = ctx_index // spread
-    gate_matrix = lax.dynamic_index_in_dim(expert_gate, own_expert, 0, keepdims=False)
-    linear_matrix = lax.dynamic_index_in_dim(expert_linear, own_expert, 0, keepdims=False)
-    down_matrix = lax.dynamic_index_in_dim(expert_down, own_expert, 0, keepdims=False)
-    gate_part = jnp.dot(received, gate_matrix, preferred_element_type=jnp.float32)
-    linear_part = jnp.dot(received, linear_matrix, preferred_element_type=jnp.float32)
-    hidden_grad = jnp.dot(grads_in, down_matrix.T, preferred_element_type=jnp.float32)
-    gate_sigmoid = jax.nn.sigmoid(gate_part)
-    hidden = (gate_part * gate_sigmoid * linear_part).astype(jnp.bfloat16)
-    gate_low = (
-        hidden_grad * linear_part * gate_sigmoid * (1.0 + gate_part * (1.0 - gate_sigmoid))
-    ).astype(jnp.bfloat16)
-    linear_low = (hidden_grad * gate_part * gate_sigmoid).astype(jnp.bfloat16)
-    dp_size = lax.axis_size("dp")
-    share_width = gate_low.shape[1] // dp_size
-    split = (slot_total, dp_size, share_width)
-    down_terms = jnp.dot(hidden.T, grads_in, preferred_element_type=jnp.float32)
-    down_terms = down_terms.astype(jnp.bfloat16).reshape(dp_size, share_width, model_width)
-    gate_terms = jnp.einsum(
-        "sd,sgf->gdf", received, gate_low.reshape(split), preferred_element_type=jnp.float32
-    ).astype(jnp.bfloat16)
-    linear_terms = jnp.einsum(
-        "sd,sgf->gdf", received, linear_low.reshape(split), preferred_element_type=jnp.float32
-    ).astype(jnp.bfloat16)
-    produced = jnp.dot(hidden, down_matrix, preferred_element_type=jnp.float32)
-    input_back = jnp.dot(
-        gate_low, gate_matrix.T, preferred_element_type=jnp.float32
-    ) + jnp.dot(linear_low, linear_matrix.T, preferred_element_type=jnp.float32)
-    returned, home_grads = exchange(
-        (
-            produced.astype(jnp.bfloat16).reshape(slot_shape),
-            input_back.astype(jnp.bfloat16).reshape(slot_shape),
-        ),
-        -1,
+    home_grads, returned, dots, gate_terms, linear_terms, down_terms = expert_layer(
+        outgoing,
+        slot_gates,
+        grads_in.reshape(slot_total, model_width),
+        (expert_gate, expert_linear, expert_down),
         ranks,
-        "from_experts",
+        lax.axis_size("dp"),
     )
     returned = returned.reshape(slot_total, model_width)
     home_grads = home_grads.reshape(slot_total, model_width)
+    slot_dots = dots[:, 0, :CAP].reshape(slot_total)
 
     def collect(terms):
         share = scatter_sum(terms, "dp")
@@ -408,7 +603,7 @@
     constant_gates = gate_weights[:, ffn_count + 2 : ffn_count + 4]
     combined = combined + jnp.sum(constant_gates[:, :, None] * constant_terms, axis=1)
     result = (middle + combined).astype(jnp.bfloat16)
-    ffn_weight_grad = jnp.sum(upstream[:, None, :] * route_outputs, axis=-1)
+    ffn_weight_grad = jnp.where(is_ffn, slot_dots[safe_targets], 0.0)
     copy_grad = jnp.sum(upstream * second, axis=-1)
     constant_weight_grad = jnp.sum(upstream[:, None, :] * constant_terms, axis=-1)
     ffn_columns = jnp.sum(route_hits[:, :, :ffn_count] * ffn_weight_grad[:, :, None], axis=1)

time: 766 us -> 767 us (level)
  Pallas kernels: 59.2 us -> 87.6 us
  local copies, waits for them, and re-layouts: 147 us -> 119 us
  matrix products: 129 us -> 114 us
  other arithmetic: 109 us -> 121 us
    dot_general x11 -> x1, matrix products: 55.3 us -> 1.85 us  [local(): jnp.dot(dispatch_first + dispatch_second, cotangent[0], preferred_element...]
    pallas_call x2, Pallas kernels: 59.2 us -> 87.6 us  [the longest x1 64.9 us: expert_layer(): pl.pallas_call(kernel, out_shape=[jax.ShapeDtypeStruct(outgoing.shape, lo...]
    ppermute x25, waiting for transfers between devices: 205 us -> 230 us  [swap(): lax.ppermute(values, axis, [(i, i ^ bit) for i in range(lax.axis_size(axi...]
    reduce_sum x3, other arithmetic: 5.77 us -> 17.3 us  [visit(): running_sum = running_sum * factor + jnp.sum(weights, axis=-1)]
    dot_general x3, matrix products: 6.13 us -> 17.2 us  [visit(): jnp.einsum('qhk,qhd->khd', weights_low, attended_grad, preferred_element_...]
    dot_general x6, matrix products: 9.1 us -> 20.1 us  [scores_and_mask(): jnp.einsum('qhd,khd->qhk', queries, key_block, preferred_element_type=jnp...]
    dot_general x3, matrix products: 3.32 us -> 14 us  [visit(): jnp.einsum('qhk,khd->qhd', score_grad, key_block, preferred_element_type=...]
    all_gather x1, waiting for transfers between devices: 21.9 us -> 11.7 us  [local(): lax.all_gather(key_flat, 'ctx', axis=0, tiled=True)]
  transfers between devices with their start and end apart: 28 -> 28, of which waited for: 14 -> 16; matrix products, arithmetic and copies ran while one was open for 17% -> 13% of each run, Pallas kernels for 0% -> 3%
where the time goes in v2:
time: 767 us; the launch traced here: 760 us
  waiting for transfers between devices  277 us (36%)
  other arithmetic  121 us (16%)
  local copies, waits for them, and re-layouts  119 us (16%)
  matrix products  114 us (15%)
  Pallas kernels  87.6 us (11%)
  starting transfers between devices  20.6 us (3%)
  between operations  15.5 us (2%)
    ppermute x25, waiting for transfers between devices, swap(): lax.ppermute(values, axis, [(i, i ^ bit) for i in range(lax.axis_size(axi...  230 us
    pallas_call x1, Pallas kernels, expert_layer(): pl.pallas_call(kernel, out_shape=[jax.ShapeDtypeStruct(outgoing.shape, lo...  64.9 us
    reduce_scatter x1, waiting for transfers between devices, local(): lax.psum_scatter(key_terms.reshape(key_count, 2 * model_width).astype(jnp...  35.6 us
    pallas_call x1, Pallas kernels, exchange(): pl.pallas_call(kernel, out_shape=jax.ShapeDtypeStruct(block.shape, block....  22.8 us
    unnamed x200, local copies, waits for them, and re-layouts  20.5 us
    ppermute x25, starting transfers between devices, swap(): lax.ppermute(values, axis, [(i, i ^ bit) for i in range(lax.axis_size(axi...  20.3 us
    dot_general x6, matrix products, scores_and_mask(): jnp.einsum('qhd,khd->qhk', queries, key_block, preferred_element_type=jnp...  20.1 us
    convert_element_type x11, other arithmetic, halve(): return total.astype(jnp.bfloat16)  19 us
  transfers between devices with their start and end apart: 28, of which 16 were waited for; matrix products, arithmetic and copies ran while one was open for 13% of the time, Pallas kernels for 3%

profile of v2, /device:TPU:0, one launch (start us, length us, event | category | flops | bytes accessed | tf_op | source)
XLA Modules:
  0.0 760.1 jit_solution(17174348198874854458)
XLA Ops:
  9.3 2.7 convolution_convert_fusion.7
  28.2 22.8 %grads_to_experts.1 = bf16[8,96,768]{2,1,0:T(8,128)(2,1)} custom-call(bf16[8,96,768]{2,1,0:T(8,128)(2,1)} %bitcast.433), custom_call_target="tpu_custom_call" | custom-call | tf_op jit(solution)/shard_map/grads_to_experts/pallas_call | solution.py:176
  53.3 4.3 copy.161
  57.6 11.7 %all-gather.3.cloned.1.call-done = bf16[1536,768]{0,1:T(8,128)(2,1)} async-done(((bf16[384,768]{0,1:T(8,128)(2,1)}), bf16[1536,768]{0,1:T(8,128)(2,1)}) %all-gather.3.cloned.1.call-update) | async-done | bytes 2359312 | tf_op jit(solution)/shard_map/all_gather | solution.py:491
  69.3 60.4 %while.32 = (s32[]{:T(128)}, f32[384,12]{0,1:T(8,128)S(1)}, f32[384,12]{0,1:T(8,128)S(1)}, f32[384,12,64]{0,2,1:T(8,128)}, s32[384]{0:T(512)S(1)}, /*index=5*/s3...) while((s32[]{:T(128)}, f32[384,12]{0,1:T(8,128)S(1)}, ...), condition=%wide.region_6.7_spmd.clone, body=%wide.region_2.6_spmd.clone.sunk | while | flops 631442304 | bytes 74830632 | solution.py:81
  73.3 5.3 fusion.214
  78.6 5.8 fusion.215
  84.9 4.2 fusion.217
  93.2 5.3 fusion.214
  98.5 5.8 fusion.215
  104.8 4.6 fusion.217
  113.5 5.3 fusion.214
  118.7 5.8 fusion.215
  125.1 4.6 fusion.217
  136.5 2.5 select_reduce_fusion.1
  140.5 64.9 %experts.1 = (bf16[8,96,768]{2,1,0:T(8,128)(2,1)}, bf16[8,96,768]{2,1,0:T(8,128)(2,1)}, f32[8,8,128]{2,1,0:T(8,128)}, bf16[4,768,512]{2,1,0:T(8,128)(2,1)}, bf16...) custom-call(bf16[8,96,768]{2,1,0:T(8,128)(2,1)} %bitcast.445, f32[8,8,128]{2,1,0:T(8,128)} %broadcast_in_dim.212.gates_ref, ...), custom_call_target="tpu_custom_call" | custom-call | flops 21743271936 | bytes 25952256 | tf_op jit(solution)/shard_map/experts/pallas_call | solution.py:351
  205.4 5.4 gather_fusion.2
  210.8 3.8 reshape.791
  214.5 3.8 gather_fusion
  218.4 3.8 reshape.790
  222.5 4.9 multiply_reduce_fusion
  229.7 3.2 gather_fusion.1
  234.9 8.0 %select_reduce_fusion = (f32[384,768]{1,0:T(8,128)S(1)}, f32[384,768]{1,0:T(8,128)S(1)}) fusion(f32[384,2,768]{2,1,0:T(2,128)} %reshape.791, pred[384,2]{1,0:T(8,128)(4,1)S(1)} %copy-done.63, f32[384,2,768]{2,1,0:T(2,128)} %reshape.790, f32[384,2]{1,0:T(8,128)S(1)} %get-tuple-element.657), kind=kLoop, calls=%fused_computation.83 | loop fusion | flops 2359296 | bytes 7081728 | tf_op jit(solution)/shard_map/reduce_sum | solution.py:643
  252.8 80.5 %while.33 = (s32[]{:T(128)}, f32[384,12,64]{0,2,1:T(8,128)}, bf16[3,512,1536]{2,1,0:T(8,128)(2,1)}, s32[3]{0:T(128)S(1)}, bf16[1536,768]{0,1:T(8,128)(2,1)}, /*i...) while((s32[]{:T(128)}, f32[384,12,64]{0,2,1:T(8,128)}, ...), condition=%wide.region_33.34_spmd.clone, body=%wide.region_31.33_spmd.clone.sunk | while | flops 1540239744 | bytes 121261264 | solution.py:701
  258.3 4.9 fusion.229
  263.2 4.4 fusion.230
  267.7 5.7 fusion.231
  276.7 2.7 constant_dynamic-update-slice_fusion.2
  284.8 4.9 fusion.229
  289.7 4.8 fusion.230
  294.5 5.7 fusion.231
  303.6 2.7 constant_dynamic-update-slice_fusion.2
  311.7 4.9 fusion.229
  316.6 4.8 fusion.230
  321.4 5.7 fusion.231
  330.4 2.7 constant_dynamic-update-slice_fusion.2
  345.8 35.6 %reduce-scatter.2.cloned.1.call-done = bf16[384,1536]{1,0:T(8,128)(2,1)} async-done(((bf16[1536,1536]{1,0:T(8,128)(2,1)}), bf16[384,1536]{1,0:T(8,128)(2,1)}) %reduce-scatter.2.cloned.1.call-update) | async-done | bytes 1179664 | tf_op jit(solution)/shard_map/reduce_scatter | solution.py:704
  383.5 2.7 copy.175
  405.0 5.4 collective-permute-done
  410.4 3.3 fusion.34
  416.0 32.2 %collective-permute-done.1 = bf16[8,112,768]{2,1,0:T(8,128)(2,1)} collective-permute-done((bf16[8,112,768]{2,1,0:T(8,128)(2,1)}, bf16[8,112,768]{2,1,0:T(8,128)(2,1)}, u32[]{:S(2)}, u32[]{:S(2)}) %collective-permute-start.1) | collective-permute-done | bytes 1376288 | tf_op jit(solution)/shard_map/ppermute | solution.py:94
  453.0 15.3 %collective-permute-done.2 = bf16[4,112,768]{2,1,0:T(8,128)(2,1)} collective-permute-done((bf16[4,112,768]{2,1,0:T(8,128)(2,1)S(1)}, bf16[4,112,768]{2,1,0:T(8,128)(2,1)}, u32[]{:S(2)}, u32[]{:S(2)}) %collective-permute-start.2) | collective-permute-done | bytes 688160 | tf_op jit(solution)/shard_map/ppermute | solution.py:94
  471.3 7.0 collective-permute-done.3
  481.9 5.9 collective-permute-done.4
  488.4 2.7 dynamic-slice_bitcast_fusion.3
  491.0 5.2 collective-permute-start.10
  498.5 2.8 dynamic-slice_bitcast_fusion.2
  502.9 36.3 %collective-permute-done.6 = bf16[2,112,768]{2,1,0:T(8,128)(2,1)S(1)} collective-permute-done((bf16[2,112,768]{2,1,0:T(8,128)(2,1)S(1)}, bf16[2,112,768]{2,1,0:T(8,128)(2,1)S(1)}, u32[]{:S(2)}, u32[]{:S(2)}) %collective-permute-start.6) | collective-permute-done | bytes 344096 | tf_op jit(solution)/shard_map/ppermute | solution.py:94
  548.2 6.6 collective-permute-done.7
  557.7 32.1 %collective-permute-done.15 = bf16[2,768,512]{2,1,0:T(8,128)(2,1)} collective-permute-done((bf16[2,768,512]{2,1,0:T(8,128)(2,1)}, bf16[2,768,512]{2,1,0:T(8,128)(2,1)}, u32[]{:S(2)}, u32[]{:S(2)}) %collective-permute-start.15) | collective-permute-done | bytes 1572896 | tf_op jit(solution)/shard_map/ppermute | solution.py:94
  593.8 38.6 %collective-permute-done.20 = bf16[2,512,768]{2,1,0:T(8,128)(2,1)} collective-permute-done((bf16[2,512,768]{2,1,0:T(8,128)(2,1)}, bf16[2,512,768]{2,1,0:T(8,128)(2,1)}, u32[]{:S(2)}, u32[]{:S(2)}) %collective-permute-start.20) | collective-permute-done | bytes 1572896 | tf_op jit(solution)/shard_map/ppermute | solution.py:94
  638.2 27.8 %collective-permute-done.16 = bf16[768,512]{1,0:T(8,128)(2,1)} collective-permute-done((bf16[768,512]{1,0:T(8,128)(2,1)}, bf16[768,512]{1,0:T(8,128)(2,1)}, u32[]{:S(2)}, u32[]{:S(2)}) %collective-permute-start.16) | collective-permute-done | bytes 786464 | tf_op jit(solution)/shard_map/ppermute | solution.py:94
  672.8 6.2 collective-permute-done.21
  682.6 14.9 %collective-permute-done.22 = bf16[512,768]{1,0:T(8,128)(2,1)} collective-permute-done((bf16[512,768]{1,0:T(8,128)(2,1)}, bf16[512,768]{1,0:T(8,128)(2,1)}, u32[]{:S(2)}, u32[]{:S(2)}) %collective-permute-start.22) | collective-permute-done | bytes 786464 | tf_op jit(solution)/shard_map/ppermute | solution.py:94
  698.0 3.1 pad_maximum_fusion.1
  701.1 4.3 gather_fusion.3
  705.4 5.5 convert_element_type.425
  710.9 3.2 pad_maximum_fusion.2
  714.1 4.3 gather_fusion.4
  718.3 5.5 convert_element_type.434
  723.8 3.5 pad_maximum_fusion.3
  727.3 4.3 gather_fusion.5
  731.6 5.3 convert_element_type.443
  743.5 3.8 fusion.140
  (548 shorter events, 174.4 us)
Async XLA Ops:
  7.2 46.1 %all-gather.5.cloned.1.call-start = ((), (), s32[]{:S(2)}) async-start(), calls=%async_computation.2 | async-start | bytes 2949120 | tf_op jit(solution)/shard_map/all_gather | solution.py:492
  8.0 10.1 %copy-start.90 = (f32[768]{0:T(1024)}, f32[768]{0:T(1024)S(1)}, u32[]{:S(2)}) copy-start(f32[768]{0:T(1024)S(1)} %convert_element_type.360) | copy-start | bytes 9220
  9.3 8.8 %copy-start.94 = (f32[384]{0:T(512)}, f32[384]{0:T(512)S(1)}, u32[]{:S(2)}) copy-start(f32[384]{0:T(512)S(1)} %add_rsqrt_fusion.1) | copy-start | bytes 4612
  12.0 57.3 %all-gather.3.cloned.1.call-start = ((), (), s32[]{:S(2)}) async-start(), calls=%async_computation.1 | async-start | bytes 2949120 | tf_op jit(solution)/shard_map/all_gather | solution.py:491
  21.1 360.3 %reduce-scatter.2.cloned.1.call-start = ((), (), s32[]{:S(2)}) async-start(), calls=%async_computation.3 | async-start | bytes 5898240 | tf_op jit(solution)/shard_map/reduce_scatter | solution.py:704
  25.3 107.1 %copy-start.71 = (f32[768]{0:T(1024)}, f32[768]{0:T(1024)S(1)}, u32[]{:S(2)}) copy-start(f32[768]{0:T(1024)S(1)} %convert_element_type.369) | copy-start | bytes 9220
  28.2 23.2 %copy-start.99 = (bf16[2,768]{1,0:T(2,128)(2,1)S(1)}, bf16[2,768]{1,0:T(2,128)(2,1)}, u32[]{:S(2)}) copy-start(bf16[2,768]{1,0:T(2,128)(2,1)} %param.39) | copy-start | bytes 9220
  28.2 23.7 %copy-start.73 = (s32[1,8]{1,0:T(1,128)S(1)}, s32[1,8]{1,0:T(1,128)}, u32[]{:S(2)}) copy-start(s32[1,8]{1,0:T(1,128)} %param.29) | copy-start | bytes 100
  28.2 23.8 %copy-start.54 = (bf16[384,12,32]{0,2,1:T(8,128)(2,1)S(1)}, bf16[384,12,32]{0,2,1:T(8,128)(2,1)}, u32[]{:S(2)}) copy-start(bf16[384,12,32]{0,2,1:T(8,128)(2,1)} %get-tuple-element.741) | copy-start | bytes 884740
  28.2 23.8 %copy-start.55 = (bf16[384,12,32]{0,2,1:T(8,128)(2,1)S(1)}, bf16[384,12,32]{0,2,1:T(8,128)(2,1)}, u32[]{:S(2)}) copy-start(bf16[384,12,32]{0,2,1:T(8,128)(2,1)} %get-tuple-element.742) | copy-start | bytes 884740
  78.6 6.4 copy-start.1
  98.5 6.4 copy-start.1
  118.7 6.4 copy-start.1
  136.4 97.5 %copy-start.74 = (f32[384]{0:T(512)}, f32[384]{0:T(512)S(1)}, u32[]{:S(2)}) copy-start(f32[384]{0:T(512)S(1)} %fusion.130) | copy-start | bytes 4612
  139.1 94.9 %copy-start.61 = (f32[384,12]{0,1:T(8,128)}, f32[384,12]{0,1:T(8,128)S(1)}, u32[]{:S(2)}) copy-start(f32[384,12]{0,1:T(8,128)S(1)} %copy.169) | copy-start | bytes 55300
  227.4 6.6 copy-start.75
  234.0 8.9 %copy-start.89 = (f32[384]{0:T(512)}, f32[384]{0:T(512)S(1)}, u32[]{:S(2)}) copy-start(f32[384]{0:T(512)S(1)} %multiply_reduce_fusion.9) | copy-start | bytes 4612
  234.8 8.1 %copy-start.67 = (bf16[384,12]{0,1:T(8,128)(2,1)}, bf16[384,12]{0,1:T(8,128)(2,1)S(1)}, u32[]{:S(2)}) copy-start(bf16[384,12]{0,1:T(8,128)(2,1)S(1)} %fusion.131) | copy-start | bytes 27652
  234.8 8.1 %copy-start.17 = (f32[384,768]{1,0:T(8,128)S(1)}, f32[384,768]{1,0:T(8,128)}, u32[]{:S(2)}) copy-start(f32[384,768]{1,0:T(8,128)} %copy-done.16) | copy-start | bytes 3538948
  234.8 8.1 %copy-start.20 = (bf16[1,384,768]{2,1,0:T(8,128)(2,1)S(1)}, bf16[1,384,768]{2,1,0:T(8,128)(2,1)}, u32[]{:S(2)}) copy-start(bf16[1,384,768]{2,1,0:T(8,128)(2,1)} %param.26) | copy-start | bytes 1769476
  234.8 8.1 %copy-start.31 = (f32[384,768]{1,0:T(8,128)S(1)}, f32[384,768]{1,0:T(8,128)}, u32[]{:S(2)}) copy-start(f32[384,768]{1,0:T(8,128)} %convolution_bitcast_fusion.1) | copy-start | bytes 3538948
  234.8 8.1 %copy-start.34 = (f32[384,768]{1,0:T(8,128)S(1)}, f32[384,768]{1,0:T(8,128)}, u32[]{:S(2)}) copy-start(f32[384,768]{1,0:T(8,128)} %get-tuple-element.654) | copy-start | bytes 3538948
  234.8 8.1 %copy-start.72 = (f32[768]{0:T(1024)S(1)}, f32[768]{0:T(1024)}, u32[]{:S(2)}) copy-start(f32[768]{0:T(1024)} %copy-done.71) | copy-start | bytes 9220
  234.9 8.1 %copy-start.82 = (f32[384]{0:T(512)S(1)}, f32[384]{0:T(512)}, u32[]{:S(2)}) copy-start(f32[384]{0:T(512)} %copy-done.81) | copy-start | bytes 4612
  257.2 6.1 copy-start.2
  263.2 10.2 %slice-start = ((s8[4718592]{0:T(1024)(128)(4,1)}), s8[4194304]{0:T(1024)(128)(4,1)S(1)}, s32[]{:S(2)}) async-start(s8[4718592]{0:T(1024)(128)(4,1)} %bitcast.386), calls=%async_computation.4 | async-start | bytes 8388608 | tf_op jit(solution)/shard_map/while
  289.7 10.5 %slice-start = ((s8[4718592]{0:T(1024)(128)(4,1)}), s8[4194304]{0:T(1024)(128)(4,1)S(1)}, s32[]{:S(2)}) async-start(s8[4718592]{0:T(1024)(128)(4,1)} %bitcast.386), calls=%async_computation.4 | async-start | bytes 8388608 | tf_op jit(solution)/shard_map/while
  316.6 10.5 %slice-start = ((s8[4718592]{0:T(1024)(128)(4,1)}), s8[4194304]{0:T(1024)(128)(4,1)S(1)}, s32[]{:S(2)}) async-start(s8[4718592]{0:T(1024)(128)(4,1)} %bitcast.386), calls=%async_computation.4 | async-start | bytes 8388608 | tf_op jit(solution)/shard_map/while
  333.3 10.7 %copy-start.7 = (f32[384,768]{1,0:T(8,128)S(1)}, f32[384,768]{1,0:T(8,128)}, u32[]{:S(2)}) copy-start(f32[384,768]{1,0:T(8,128)} %copy-done.6) | copy-start | bytes 3538948
  333.4 10.7 %copy-start.48 = (bf16[384,12,64]{0,2,1:T(8,128)(2,1)S(1)}, bf16[384,12,64]{0,2,1:T(8,128)(2,1)}, u32[]{:S(2)}) copy-start(bf16[384,12,64]{0,2,1:T(8,128)(2,1)} %copy-done.47) | copy-start | bytes 1769476
  405.0 5.4 collective-permute-start
  415.7 32.5 %collective-permute-start.1 = (bf16[8,112,768]{2,1,0:T(8,128)(2,1)}, bf16[8,112,768]{2,1,0:T(8,128)(2,1)}, u32[]{:S(2)}, u32[]{:S(2)}) collective-permute-start(bf16[8,112,768]{2,1,0:T(8,128)(2,1)} %dynamic-slice_bitcast_fusion.4), channel_id=1, source_target_pairs={{0,4},{2,6},{4,0},{6,2},{1,5},{3,7},{5,1},{7,3},{8,12},{10,14},{12... | collective-permute-start | bytes 4128776 | tf_op jit(solution)/shard_map/ppermute | solution.py:94
  451.5 16.8 %collective-permute-start.2 = (bf16[4,112,768]{2,1,0:T(8,128)(2,1)S(1)}, bf16[4,112,768]{2,1,0:T(8,128)(2,1)}, u32[]{:S(2)}, u32[]{:S(2)}) collective-permute-start(bf16[4,112,768]{2,1,0:T(8,128)(2,1)S(1)} %dynamic-slice_bitcast_fusion.8), channel_id=1, source_target_pairs={{0,1},{1,0},{2,3},{3,2},{4,5},{5,4},{6,7},{7,6},{8,9},{9,8},{10,11... | collective-permute-start | bytes 2064392 | tf_op jit(solution)/shard_map/ppermute | solution.py:94
  469.8 8.5 %collective-permute-start.3 = (bf16[2,112,768]{2,1,0:T(8,128)(2,1)S(1)}, bf16[2,112,768]{2,1,0:T(8,128)(2,1)}, u32[]{:S(2)}, u32[]{:S(2)}) collective-permute-start(bf16[2,112,768]{2,1,0:T(8,128)(2,1)S(1)} %dynamic-slice_bitcast_fusion.9), channel_id=1, source_target_pairs={{0,8},{8,0},{16,24},{24,16},{1,9},{9,1},{17,25},{25,17},{2,10},{10... | collective-permute-start | bytes 1032200 | tf_op jit(solution)/shard_map/ppermute | solution.py:94
  479.4 8.4 %collective-permute-start.4 = (bf16[1,112,768]{2,1,0:T(8,128)(2,1)S(1)}, bf16[1,112,768]{2,1,0:T(8,128)(2,1)S(1)}, u32[]{:S(2)}, u32[]{:S(2)}) collective-permute-start(bf16[1,112,768]{2,1,0:T(8,128)(2,1)S(1)} %constant_dynamic-slice_fusion.4), channel_id=1, source_target_pairs={{0,16},{8,24},{16,0},{24,8},{1,17},{9,25},{17,1},{25,9},{2,18},{10... | collective-permute-start | bytes 516104 | tf_op jit(solution)/shard_map/ppermute | solution.py:94
  487.9 10.1 %collective-permute-start.5 = (bf16[1,112,768]{2,1,0:T(8,128)(2,1)S(1)}, bf16[1,112,768]{2,1,0:T(8,128)(2,1)S(1)}, u32[]{:S(2)}, u32[]{:S(2)}) collective-permute-start(bf16[1,112,768]{2,1,0:T(8,128)(2,1)S(1)} %add_convert_fusion.3), channel_id=1, source_target_pairs={{0,16},{8,24},{16,0},{24,8},{1,17},{9,25},{17,1},{25,9},{2,18},{10... | collective-permute-start | bytes 516104 | tf_op jit(solution)/shard_map/ppermute | solution.py:94
  491.0 53.8 %collective-permute-start.10 = (bf16[2,768,512]{2,1,0:T(8,128)(2,1)}, bf16[2,768,512]{2,1,0:T(8,128)(2,1)}, u32[]{:S(2)}, u32[]{:S(2)}) collective-permute-start(bf16[2,768,512]{2,1,0:T(8,128)(2,1)} %dynamic-slice_bitcast_fusion.3), channel_id=1, source_target_pairs={{0,8},{8,0},{16,24},{24,16},{1,9},{9,1},{17,25},{25,17},{2,10},{10... | collective-permute-start | bytes 4718600 | tf_op jit(solution)/shard_map/ppermute | solution.py:94
  498.0 41.2 %collective-permute-start.6 = (bf16[2,112,768]{2,1,0:T(8,128)(2,1)S(1)}, bf16[2,112,768]{2,1,0:T(8,128)(2,1)S(1)}, u32[]{:S(2)}, u32[]{:S(2)}) collective-permute-start(bf16[2,112,768]{2,1,0:T(8,128)(2,1)S(1)} %pad_maximum_fusion.9), channel_id=1, source_target_pairs={{0,8},{8,0},{16,24},{24,16},{1,9},{9,1},{17,25},{25,17},{2,10},{10... | collective-permute-start | bytes 1032200 | tf_op jit(solution)/shard_map/ppermute | solution.py:94
  498.5 43.1 %copy-start.41 = (bf16[4,512,768]{2,1,0:T(8,128)(2,1)S(1)}, bf16[4,512,768]{2,1,0:T(8,128)(2,1)}, u32[]{:S(2)}) copy-start(bf16[4,512,768]{2,1,0:T(8,128)(2,1)} %get-tuple-element.361) | copy-start | bytes 9437188
  501.3 88.5 %collective-permute-start.15 = (bf16[2,768,512]{2,1,0:T(8,128)(2,1)}, bf16[2,768,512]{2,1,0:T(8,128)(2,1)}, u32[]{:S(2)}, u32[]{:S(2)}) collective-permute-start(bf16[2,768,512]{2,1,0:T(8,128)(2,1)} %dynamic-slice_bitcast_fusion.2), channel_id=1, source_target_pairs={{0,8},{8,0},{16,24},{24,16},{1,9},{9,1},{17,25},{25,17},{2,10},{10... | collective-permute-start | bytes 4718600 | tf_op jit(solution)/shard_map/ppermute | solution.py:94
  540.0 14.7 %collective-permute-start.7 = (bf16[4,112,768]{2,1,0:T(8,128)(2,1)S(1)}, bf16[4,112,768]{2,1,0:T(8,128)(2,1)}, u32[]{:S(2)}, u32[]{:S(2)}) collective-permute-start(bf16[4,112,768]{2,1,0:T(8,128)(2,1)S(1)} %pad_maximum_fusion.6), channel_id=1, source_target_pairs={{0,1},{1,0},{2,3},{3,2},{4,5},{5,4},{6,7},{7,6},{8,9},{9,8},{10,11... | collective-permute-start | bytes 2064392 | tf_op jit(solution)/shard_map/ppermute | solution.py:94
  542.8 89.6 %collective-permute-start.20 = (bf16[2,512,768]{2,1,0:T(8,128)(2,1)}, bf16[2,512,768]{2,1,0:T(8,128)(2,1)}, u32[]{:S(2)}, u32[]{:S(2)}) collective-permute-start(bf16[2,512,768]{2,1,0:T(8,128)(2,1)} %dynamic-slice_bitcast_fusion.1), channel_id=1, source_target_pairs={{0,8},{8,0},{16,24},{24,16},{1,9},{9,1},{17,25},{25,17},{2,10},{10... | collective-permute-start | bytes 4718600 | tf_op jit(solution)/shard_map/ppermute | solution.py:94
  547.2 8.9 %copy-start.21 = (bf16[2,768,512]{2,1,0:T(8,128)(2,1)}, bf16[2,768,512]{2,1,0:T(8,128)(2,1)S(1)}, u32[]{:S(2)}) copy-start(bf16[2,768,512]{2,1,0:T(8,128)(2,1)S(1)} %fusion.37) | copy-start | bytes 4718596
  547.2 7.6 copy-start.44
  548.1 86.7 %collective-permute-start.11 = (bf16[768,512]{1,0:T(8,128)(2,1)}, bf16[768,512]{1,0:T(8,128)(2,1)}, u32[]{:S(2)}, u32[]{:S(2)}) collective-permute-start(bf16[768,512]{1,0:T(8,128)(2,1)} %dynamic-slice_bitcast_fusion.7), channel_id=1, source_target_pairs={{0,16},{8,24},{16,0},{24,8},{1,17},{9,25},{17,1},{25,9},{2,18},{10... | collective-permute-start | bytes 2359304 | tf_op jit(solution)/shard_map/ppermute | solution.py:94
  554.8 35.1 %copy-start.42 = (bf16[4,768,512]{2,1,0:T(8,128)(2,1)S(1)}, bf16[4,768,512]{2,1,0:T(8,128)(2,1)}, u32[]{:S(2)}) copy-start(bf16[4,768,512]{2,1,0:T(8,128)(2,1)} %get-tuple-element.359) | copy-start | bytes 9437188
  557.4 111.4 %collective-permute-start.8 = (bf16[8,112,768]{2,1,0:T(8,128)(2,1)}, bf16[8,112,768]{2,1,0:T(8,128)(2,1)}, u32[]{:S(2)}, u32[]{:S(2)}) collective-permute-start(bf16[8,112,768]{2,1,0:T(8,128)(2,1)} %pad_maximum_fusion.5), channel_id=1, source_target_pairs={{0,4},{2,6},{4,0},{6,2},{1,5},{3,7},{5,1},{7,3},{8,12},{10,14},{12... | collective-permute-start | bytes 4128776 | tf_op jit(solution)/shard_map/ppermute | solution.py:94
  593.8 72.3 %collective-permute-start.16 = (bf16[768,512]{1,0:T(8,128)(2,1)}, bf16[768,512]{1,0:T(8,128)(2,1)}, u32[]{:S(2)}, u32[]{:S(2)}) collective-permute-start(bf16[768,512]{1,0:T(8,128)(2,1)} %dynamic-slice_bitcast_fusion.6), channel_id=1, source_target_pairs={{0,16},{8,24},{16,0},{24,8},{1,17},{9,25},{17,1},{25,9},{2,18},{10... | collective-permute-start | bytes 2359304 | tf_op jit(solution)/shard_map/ppermute | solution.py:94
  634.7 31.3 %copy-start.24 = (bf16[2,768,512]{2,1,0:T(8,128)(2,1)S(1)}, bf16[2,768,512]{2,1,0:T(8,128)(2,1)}, u32[]{:S(2)}) copy-start(bf16[2,768,512]{2,1,0:T(8,128)(2,1)} %copy-done.23) | copy-start | bytes 4718596
  634.8 44.2 %collective-permute-start.21 = (bf16[512,768]{1,0:T(8,128)(2,1)S(1)}, bf16[512,768]{1,0:T(8,128)(2,1)S(1)}, u32[]{:S(2)}, u32[]{:S(2)}) collective-permute-start(bf16[512,768]{1,0:T(8,128)(2,1)S(1)} %dynamic-slice_bitcast_fusion.5), channel_id=1, source_target_pairs={{0,16},{8,24},{16,0},{24,8},{1,17},{9,25},{17,1},{25,9},{2,18},{10... | collective-permute-start | bytes 2359304 | tf_op jit(solution)/shard_map/ppermute | solution.py:94
  637.4 32.9 %copy-start.39 = (bf16[768,512]{1,0:T(8,128)(2,1)}, bf16[768,512]{1,0:T(8,128)(2,1)S(1)}, u32[]{:S(2)}) copy-start(bf16[768,512]{1,0:T(8,128)(2,1)S(1)} %fusion.45) | copy-start | bytes 2359300
  637.4 31.4 %copy-start.28 = (bf16[4,112,768]{2,1,0:T(8,128)(2,1)S(1)}, bf16[4,112,768]{2,1,0:T(8,128)(2,1)}, u32[]{:S(2)}) copy-start(bf16[4,112,768]{2,1,0:T(8,128)(2,1)} %copy-done.27) | copy-start | bytes 2064388
  637.4 42.9 %collective-permute-start.12 = (bf16[768,512]{1,0:T(8,128)(2,1)S(1)}, bf16[768,512]{1,0:T(8,128)(2,1)}, u32[]{:S(2)}, u32[]{:S(2)}) collective-permute-start(bf16[768,512]{1,0:T(8,128)(2,1)S(1)} %fusion.45), channel_id=1, source_target_pairs={{0,4},{2,6},{4,0},{6,2},{1,5},{3,7},{5,1},{7,3},{8,12},{10,14},{12... | collective-permute-start | bytes 2359304 | tf_op jit(solution)/shard_map/ppermute | solution.py:94
  638.2 42.1 %collective-permute-start.13 = (bf16[768,512]{1,0:T(8,128)(2,1)S(1)}, bf16[768,512]{1,0:T(8,128)(2,1)S(1)}, u32[]{:S(2)}, u32[]{:S(2)}) collective-permute-start(bf16[768,512]{1,0:T(8,128)(2,1)S(1)} %fusion.45), channel_id=1, source_target_pairs={{0,2},{2,0},{4,6},{6,4},{1,3},{3,1},{5,7},{7,5},{8,10},{10,8},{12,... | collective-permute-start | bytes 2359304 | tf_op jit(solution)/shard_map/ppermute | solution.py:94
  668.2 13.6 %collective-permute-start.17 = (bf16[768,512]{1,0:T(8,128)(2,1)}, bf16[768,512]{1,0:T(8,128)(2,1)}, u32[]{:S(2)}, u32[]{:S(2)}) collective-permute-start(bf16[768,512]{1,0:T(8,128)(2,1)} %fusion.44), channel_id=1, source_target_pairs={{0,4},{2,6},{4,0},{6,2},{1,5},{3,7},{5,1},{7,3},{8,12},{10,14},{12... | collective-permute-start | bytes 2359304 | tf_op jit(solution)/shard_map/ppermute | solution.py:94
  672.8 9.0 %copy-start.104 = (s32[4]{0:T(128)S(1)}, s32[4]{0:T(128)}, u32[]{:S(2)}) copy-start(s32[4]{0:T(128)} %constant.364.clone) | copy-start | bytes 52
  672.8 25.2 %copy-start.40 = (bf16[768,512]{1,0:T(8,128)(2,1)S(1)}, bf16[768,512]{1,0:T(8,128)(2,1)}, u32[]{:S(2)}) copy-start(bf16[768,512]{1,0:T(8,128)(2,1)} %copy-done.39) | copy-start | bytes 2359300
  672.8 65.4 %collective-permute-start.9 = (bf16[16,112,768]{2,1,0:T(8,128)(2,1)}, bf16[16,112,768]{2,1,0:T(8,128)(2,1)}, u32[]{:S(2)}, u32[]{:S(2)}) collective-permute-start(bf16[16,112,768]{2,1,0:T(8,128)(2,1)} %pad_maximum_fusion.4), channel_id=1, source_target_pairs={{0,2},{2,0},{4,6},{6,4},{1,3},{3,1},{5,7},{7,5},{8,10},{10,8},{12,... | collective-permute-start | bytes 8257544 | tf_op jit(solution)/shard_map/ppermute | solution.py:94
  680.1 17.4 %collective-permute-start.22 = (bf16[512,768]{1,0:T(8,128)(2,1)}, bf16[512,768]{1,0:T(8,128)(2,1)}, u32[]{:S(2)}, u32[]{:S(2)}) collective-permute-start(bf16[512,768]{1,0:T(8,128)(2,1)} %fusion.43), channel_id=1, source_target_pairs={{0,4},{2,6},{4,0},{6,2},{1,5},{3,7},{5,1},{7,3},{8,12},{10,14},{12... | collective-permute-start | bytes 2359304 | tf_op jit(solution)/shard_map/ppermute | solution.py:94
  680.3 17.1 %collective-permute-start.14 = (bf16[768,512]{1,0:T(8,128)(2,1)}, bf16[768,512]{1,0:T(8,128)(2,1)}, u32[]{:S(2)}, u32[]{:S(2)}) collective-permute-start(bf16[768,512]{1,0:T(8,128)(2,1)} %collective-permute-done.12), channel_id=1, source_target_pairs={{0,2},{2,0},{4,6},{6,4},{1,3},{3,1},{5,7},{7,5},{8,10},{10,8},{12,... | collective-permute-start | bytes 2359304 | tf_op jit(solution)/shard_map/ppermute | solution.py:94
  681.2 29.6 %collective-permute-start.18 = (bf16[768,512]{1,0:T(8,128)(2,1)}, bf16[768,512]{1,0:T(8,128)(2,1)}, u32[]{:S(2)}, u32[]{:S(2)}) collective-permute-start(bf16[768,512]{1,0:T(8,128)(2,1)} %fusion.44), channel_id=1, source_target_pairs={{0,2},{2,0},{4,6},{6,4},{1,3},{3,1},{5,7},{7,5},{8,10},{10,8},{12,... | collective-permute-start | bytes 2359304 | tf_op jit(solution)/shard_map/ppermute | solution.py:94
  681.8 29.1 %collective-permute-start.19 = (bf16[768,512]{1,0:T(8,128)(2,1)}, bf16[768,512]{1,0:T(8,128)(2,1)}, u32[]{:S(2)}, u32[]{:S(2)}) collective-permute-start(bf16[768,512]{1,0:T(8,128)(2,1)} %collective-permute-done.17), channel_id=1, source_target_pairs={{0,2},{2,0},{4,6},{6,4},{1,3},{3,1},{5,7},{7,5},{8,10},{10,8},{12,... | collective-permute-start | bytes 2359304 | tf_op jit(solution)/shard_map/ppermute | solution.py:94
  697.4 26.4 %collective-permute-start.23 = (bf16[512,768]{1,0:T(8,128)(2,1)}, bf16[512,768]{1,0:T(8,128)(2,1)}, u32[]{:S(2)}, u32[]{:S(2)}) collective-permute-start(bf16[512,768]{1,0:T(8,128)(2,1)} %fusion.43), channel_id=1, source_target_pairs={{0,2},{2,0},{4,6},{6,4},{1,3},{3,1},{5,7},{7,5},{8,10},{10,8},{12,... | collective-permute-start | bytes 2359304 | tf_op jit(solution)/shard_map/ppermute | solution.py:94
  697.4 26.4 %collective-permute-start.24 = (bf16[512,768]{1,0:T(8,128)(2,1)}, bf16[512,768]{1,0:T(8,128)(2,1)}, u32[]{:S(2)}, u32[]{:S(2)}) collective-permute-start(bf16[512,768]{1,0:T(8,128)(2,1)} %collective-permute-done.22), channel_id=1, source_target_pairs={{0,2},{2,0},{4,6},{6,4},{1,3},{3,1},{5,7},{7,5},{8,10},{10,8},{12,... | collective-permute-start | bytes 2359304 | tf_op jit(solution)/shard_map/ppermute | solution.py:94
  (99 other events, 278.9 us)
Sparse Core Ops, SparseCore 0:
  12.1 30.2 all-gather.4
  44.5 24.7 all-gather.2
  333.5 47.8 reduce-scatter.1

commit v3 on v2

v3 whole, which is shorter than its diff:
```python
import math

import jax
import jax.numpy as jnp
import numpy as np
from jax import lax
from jax.experimental import pallas as pl
from jax.experimental.pallas import tpu as pltpu
from jax.sharding import PartitionSpec as P

HEAD_DIM = 64
CAP = 96


EPSILON = 1e-06
NEGATIVE = -1e30
HIGH = lax.Precision.HIGHEST


def bits_of(axis):
    bits, bit = [], 1
    while bit < lax.axis_size(axis):
        bits.append(bit)
        bit *= 2
    return bits


def swap(values, axis, bit):
    return lax.ppermute(values, axis, [(i, i ^ bit) for i in range(lax.axis_size(axis))])


def halve(values, axis, bit, dim):
    own = (lax.axis_index(axis) // bit) % 2
    kept = lax.dynamic_index_in_dim(values, own, dim, keepdims=False)
    sent = lax.dynamic_index_in_dim(values, 1 - own, dim, keepdims=False)
    total = kept.astype(jnp.float32) + swap(sent, axis, bit).astype(jnp.float32)
    return total.astype(jnp.bfloat16)


def scatter_sum(values, axis):
    bits = bits_of(axis)
    values = values.reshape((2,) * len(bits) + values.shape[1:])
    for place, bit in enumerate(bits):
        values = halve(values, axis, bit, len(bits) - 1 - place)
    return values


def mesh_id(exp_index, ctx_index):
    return {"exp": exp_index, "ctx": ctx_index}


def dot(left, right):
    return jnp.dot(left, right, preferred_element_type=jnp.float32)


def dot_nt(left, right):
    return lax.dot_general(
        left, right, (((1,), (1,)), ((), ())), preferred_element_type=jnp.float32
    )


def dot_tn(left, right):
    return lax.dot_general(
        left, right, (((0,), (0,)), ((), ())), preferred_element_type=jnp.float32
    )


def member_of(shift, ranks):
    exchange_size, group_size, spread = ranks
    exp_index, ctx_index = lax.axis_index("exp"), lax.axis_index("ctx")
    far, near = shift // group_size, shift % group_size
    place = jnp.bitwise_xor(ctx_index // spread, near) * spread + lax.rem(ctx_index, spread)
    return mesh_id(jnp.bitwise_xor(exp_index, far), place)


def greet(count, ranks):
    barrier = pltpu.get_barrier_semaphore()
    for shift in range(1, count):
        pl.semaphore_signal(
            barrier, inc=1, device_id=member_of(shift, ranks), device_id_type=pl.DeviceIdType.MESH
        )
    pl.semaphore_wait(barrier, count - 1)


def send_block(source, target, shift, ranks, send_sem, recv_sem):
    return pltpu.make_async_remote_copy(
        src_ref=source.at[shift],
        dst_ref=target.at[shift],
        send_sem=send_sem.at[shift],
        recv_sem=recv_sem.at[shift],
        device_id=member_of(shift, ranks),
        device_id_type=pl.DeviceIdType.MESH,
    )


def expert_layer(outgoing, gates, grads, weights, ranks, shares):
    count, cap, width = outgoing.shape
    hidden_units = weights[0].shape[2]
    rows = count * cap
    share = hidden_units // shares
    spread = ranks[2]

    def kernel(
        outgoing_ref,
        gates_ref,
        grads_ref,
        gate_hbm,
        linear_hbm,
        down_hbm,
        back_ref,
        output_ref,
        dots_ref,
        gate_terms,
        linear_terms,
        down_terms,
        received,
        received_gates,
        gate_w,
        linear_w,
        down_w,
        hidden_grad,
        hidden,
        gate_low,
        linear_low,
        rows_t,
        scaled,
        gate_column,
        out_total,
        in_total,
        out_send,
        in_send,
        dots_send,
        terms,
        weight_sem,
        send_sem,
        recv_sem,
        local_sem,
        terms_sem,
    ):
        own = lax.axis_index("ctx") // spread
        loads = [
            pltpu.make_async_copy(source.at[own], target, weight_sem.at[index])
            for index, (source, target) in enumerate(
                ((down_hbm, down_w), (gate_hbm, gate_w), (linear_hbm, linear_w))
            )
        ]
        for load in loads:
            load.start()
        greet(count, ranks)

        def send_all(source, target, index):
            copies = [
                send_block(source, target, shift, ranks, send_sem.at[index], recv_sem.at[index])
                for shift in range(1, count)
            ]
            copies.append(
                pltpu.make_async_copy(source.at[0], target.at[0], local_sem.at[index])
            )
            for copy in copies:
                copy.start()
            return copies

        incoming = send_all(gates_ref, received_gates, 0) + send_all(outgoing_ref, received, 1)
        loads[0].wait()

        def backward_in(index, carry):
            part = pl.ds(pl.multiple_of(index * share, share), share)
            hidden_grad[:, part] = dot_nt(grads_ref[...], down_w[part, :])
            return carry

        lax.fori_loop(0, shares, backward_in, 0)
        for copy in incoming + loads[1:]:
            copy.wait()
        for shift in range(count):
            column = jnp.transpose(received_gates[shift])[:cap, 0:1]
            block = pl.ds(shift * cap, cap)
            gate_column[block, :] = jnp.broadcast_to(column, (cap, 128))
            scaled[block, :] = (column * grads_ref[block, :].astype(jnp.float32)).astype(
                jnp.bfloat16
            )
        tokens = received[...].reshape(rows, width)
        rows_t[...] = jnp.transpose(tokens)

        def through(index, carry):
            part = pl.ds(pl.multiple_of(index * share, share), share)
            tokens = received[...].reshape(rows, width)
            gate_part = dot(tokens, gate_w[:, part])
            linear_part = dot(tokens, linear_w[:, part])
            sigmoid = 1.0 / (1.0 + jnp.exp(-gate_part))
            silu = gate_part * sigmoid
            low = (silu * linear_part).astype(jnp.bfloat16)
            hidden[:, part] = low
            upper = hidden_grad[:, part] * gate_column[:, 0:1]
            low_gate = (
                upper * linear_part * sigmoid * (1.0 + gate_part * (1.0 - sigmoid))
            ).astype(jnp.bfloat16)
            gate_low[:, part] = low_gate
            low_linear = (upper * silu).astype(jnp.bfloat16)
            linear_low[:, part] = low_linear
            out = dot(low, down_w[part, :])
            back = dot_nt(low_gate, gate_w[:, part]) + dot_nt(low_linear, linear_w[:, part])

            @pl.when(index == 0)
            def _():
                out_total[...] = out
                in_total[...] = back

            @pl.when(index > 0)
            def _():
                out_total[...] += out
                in_total[...] += back

            return carry

        lax.fori_loop(0, shares, through, 0)
        in_send[...] = in_total[...].astype(jnp.bfloat16).reshape(count, cap, width)
        going = send_all(in_send, back_ref, 2)
        low = out_total[...].astype(jnp.bfloat16)
        out_send[...] = low.reshape(count, cap, width)
        dots = jnp.sum(
            low.astype(jnp.float32) * grads_ref[...].astype(jnp.float32), axis=1, keepdims=True
        )
        for shift in range(count):
            column = jnp.broadcast_to(dots[shift * cap : (shift + 1) * cap], (cap, 128))
            dots_send[shift, :, 0:cap] = jnp.transpose(column)[0:8, :]
            dots_send[shift, :, cap:] = jnp.zeros((8, 128 - cap), jnp.float32)
        going = going + send_all(dots_send, dots_ref, 3) + send_all(out_send, output_ref, 4)

        def term_copy(which, index):
            target = (down_terms, gate_terms, linear_terms)[which]
            return pltpu.make_async_copy(
                terms[which].at[index], target.at[index], terms_sem.at[which, index]
            )

        def weigh(index, carry):
            part = pl.ds(pl.multiple_of(index * share, share), share)
            terms[0][index] = dot_tn(hidden[:, part], scaled[...]).astype(jnp.bfloat16)
            term_copy(0, index).start()
            terms[1][index] = dot(rows_t[...], gate_low[:, part]).astype(jnp.bfloat16)
            term_copy(1, index).start()
            terms[2][index] = dot(rows_t[...], linear_low[:, part]).astype(jnp.bfloat16)
            term_copy(2, index).start()
            return carry

        lax.fori_loop(0, shares, weigh, 0)
        for which in range(3):
            for index in range(shares):
                term_copy(which, index).wait()
        for copy in going:
            copy.wait()

    low, full = jnp.bfloat16, jnp.float32
    columns, lines = (shares, width, share), (shares, share, width)
    any_space = pl.BlockSpec(memory_space=pl.ANY)
    in_vmem = pl.BlockSpec(memory_space=pltpu.VMEM)
    return pl.pallas_call(
        kernel,
        out_shape=[
            jax.ShapeDtypeStruct(outgoing.shape, low),
            jax.ShapeDtypeStruct(outgoing.shape, low),
            jax.ShapeDtypeStruct(gates.shape, full),
            jax.ShapeDtypeStruct(columns, low),
            jax.ShapeDtypeStruct(columns, low),
            jax.ShapeDtypeStruct(lines, low),
        ],
        in_specs=[in_vmem, in_vmem, in_vmem, any_space, any_space, any_space],
        out_specs=[any_space] * 6,
        scratch_shapes=[
            pltpu.VMEM(outgoing.shape, low),
            pltpu.VMEM(gates.shape, full),
            pltpu.VMEM((width, hidden_units), low),
            pltpu.VMEM((width, hidden_units), low),
            pltpu.VMEM((hidden_units, width), low),
            pltpu.VMEM((rows, hidden_units), full),
            pltpu.VMEM((rows, hidden_units), low),
            pltpu.VMEM((rows, hidden_units), low),
            pltpu.VMEM((rows, hidden_units), low),
            pltpu.VMEM((width, rows), low),
            pltpu.VMEM((rows, width), low),
            pltpu.VMEM((rows, 128), full),
            pltpu.VMEM((rows, width), full),
            pltpu.VMEM((rows, width), full),
            pltpu.VMEM(outgoing.shape, low),
            pltpu.VMEM(outgoing.shape, low),
            pltpu.VMEM(gates.shape, full),
            [pltpu.VMEM(lines, low), pltpu.VMEM(columns, low), pltpu.VMEM(columns, low)],
            pltpu.SemaphoreType.DMA((3,)),
            pltpu.SemaphoreType.DMA((5, count)),
            pltpu.SemaphoreType.DMA((5, count)),
            pltpu.SemaphoreType.DMA((5,)),
            pltpu.SemaphoreType.DMA((3, shares)),
        ],
        compiler_params=pltpu.CompilerParams(
            collective_id=1, has_side_effects=True, vmem_limit_bytes=60 * 2**20
        ),
        cost_estimate=pl.CostEstimate(
            flops=18 * rows * width * hidden_units,
            bytes_accessed=12 * width * hidden_units + 12 * rows * width,
            transcendentals=rows * hidden_units,
        ),
        name="experts",
    )(outgoing, gates, grads, *weights)


def rope_tables(row_count):
    half = HEAD_DIM // 2
    frequency = np.exp(
        np.arange(half, dtype=np.float32) * np.float32(-2.0 * math.log(10000.0) / HEAD_DIM)
    ).astype(np.float32)
    angles = np.arange(row_count, dtype=np.float32)[:, None] * frequency[None, :]
    cosine, sine = np.cos(angles).astype(np.float32), np.sin(angles).astype(np.float32)
    return (
        np.concatenate([cosine] * 4, axis=1),
        np.concatenate([-sine, sine, -sine, sine], axis=1),
    )


def rotate(values, cosine, sine):
    lane = lax.broadcasted_iota(jnp.int32, cosine.shape, 1)
    leading = jnp.bitwise_and(lane, HEAD_DIM - 1) < HEAD_DIM // 2
    parts = []
    for begin in range(0, values.shape[1], 128):
        part = values[:, begin : begin + 128]
        ahead = pltpu.roll(part, 128 - HEAD_DIM // 2, 1)
        behind = pltpu.roll(part, HEAD_DIM // 2, 1)
        parts.append(part * cosine + jnp.where(leading, ahead, behind) * sine)
    return jnp.concatenate(parts, axis=1)


def inverse_norm(values):
    return lax.rsqrt(jnp.mean(values * values, axis=1, keepdims=True) + EPSILON)


def head_masks(rows):
    first = lax.broadcasted_iota(jnp.int32, (rows, 128), 1) < HEAD_DIM
    return first, jnp.logical_not(first)


def start_of(positions, starts):
    first = jnp.zeros_like(positions)
    for index in range(starts.shape[1]):
        begin = starts[0, index]
        first = jnp.where(begin <= positions, jnp.maximum(first, begin), first)
    return first


def gather_steps(size):
    bits, held, steps = [], [0], []
    bit = size // 2
    while bit >= 1:
        steps.append((bit, list(held)))
        held = held + [place ^ bit for place in held]
        bit //= 2
    return steps


def peer(far, near):
    return {
        "exp": jnp.bitwise_xor(lax.axis_index("exp"), far),
        "ctx": jnp.bitwise_xor(lax.axis_index("ctx"), near),
    }


def greet_all(places):
    barrier = pltpu.get_barrier_semaphore()
    for far, near in places:
        pl.semaphore_signal(
            barrier, inc=1, device_id=peer(far, near), device_id_type=pl.DeviceIdType.MESH
        )
    pl.semaphore_wait(barrier, len(places))


def group_places(ranks):
    return [
        (shift // ranks[1], shift % ranks[1] * ranks[2]) for shift in range(1, ranks[0] * ranks[1])
    ]


def ring_places(size):
    return [(0, bit) for bit, _ in gather_steps(size)]


def places_of(ranks, size):
    places = group_places(ranks)
    return places + [place for place in ring_places(size) if place not in places]


class Gather:
    def __init__(self, buffers, size, send_sem, recv_sem):
        self.buffers, self.size = buffers, size
        self.send_sem, self.recv_sem = send_sem, recv_sem
        self.steps = gather_steps(size)
        self.started = []

    def copy(self, place, bit, index):
        block = jnp.bitwise_xor(lax.axis_index("ctx"), place)
        buffer = self.buffers[index]
        return pltpu.make_async_remote_copy(
            src_ref=buffer.at[block],
            dst_ref=buffer.at[block],
            send_sem=self.send_sem.at[index, place ^ bit],
            recv_sem=self.recv_sem.at[index, place ^ bit],
            device_id=peer(0, bit),
            device_id_type=pl.DeviceIdType.MESH,
        )

    def forward(self, place):
        for bit, held in self.steps:
            if place in held:
                for index in range(len(self.buffers)):
                    copy = self.copy(place, bit, index)
                    copy.start()
                    self.started.append(copy)

    def arrive(self, place):
        bit = place & -place
        for index in range(len(self.buffers)):
            self.copy(place ^ bit, bit, index).wait_recv()
        self.forward(place)

    def finish(self):
        for copy in self.started:
            copy.wait_send()


def slot_targets(routes, ranks, cap):
    exchange_size, group_size, spread = ranks
    rows = routes.shape[1]
    experts = exchange_size * group_size
    expert = lax.broadcasted_iota(jnp.int32, (16, rows), 0)
    hits = [(expert == routes[k : k + 1]).astype(jnp.float32) for k in range(2)]
    before = lax.broadcasted_iota(jnp.int32, (rows, rows), 0) < lax.broadcasted_iota(
        jnp.int32, (rows, rows), 1
    )
    earlier = dot(
        (hits[0] + hits[1]).astype(jnp.bfloat16), before.astype(jnp.float32).astype(jnp.bfloat16)
    )
    targets = []
    for k in range(2):
        route = routes[k : k + 1]
        rank = jnp.sum(hits[k] * earlier, axis=0, keepdims=True)
        far = jnp.bitwise_xor(route // group_size, lax.axis_index("exp"))
        near = jnp.bitwise_xor(route % group_size, lax.axis_index("ctx") // spread)
        place = ((far * group_size + near) * cap).astype(jnp.float32)
        targets.append(jnp.where(route < experts, place + rank, -1.0))
    return targets


def attend_layer(
    tokens, cotangent, previous, routes, starts, weights, norms, heads, carry, ranks, cap, size
):
    rows, width = tokens.shape
    count = ranks[0] * ranks[1]
    slots = count * cap
    pairs = width // 128
    tables = rope_tables(size * rows)
    low, full = jnp.bfloat16, jnp.float32

    def kernel(
        tokens_ref,
        cotangent_ref,
        previous_ref,
        routes_ref,
        starts_ref,
        query_hbm,
        key_hbm,
        value_hbm,
        output_hbm,
        first_ref,
        second_ref,
        heads_ref,
        carry_ref,
        cosine_hbm,
        sine_hbm,
        queries_out,
        keys_out,
        values_out,
        attended_ref,
        lse_ref,
        middle_ref,
        probs_ref,
        targets_ref,
        outgoing_ref,
        gates_ref,
        grads_ref,
        stream,
        queries,
        keys,
        values,
        query_w,
        key_w,
        value_w,
        output_w,
        cosine,
        sine,
        bias,
        totals,
        highest,
        slot_grads,
        load_sem,
        gather_send,
        gather_recv,
        grad_send,
        grad_recv,
        keep_sem,
    ):
        own = lax.axis_index("ctx")
        loads = [
            pltpu.make_async_copy(source, target, load_sem.at[index])
            for index, (source, target) in enumerate(
                (
                    (query_hbm, query_w),
                    (key_hbm, key_w),
                    (value_hbm, value_w),
                    (cosine_hbm, cosine),
                    (sine_hbm, sine),
                    (output_hbm, output_w),
                )
            )
        ]
        for load in loads:
            load.start()
        stream[own] = tokens_ref[...]
        greet_all(places_of(ranks, size))
        gather = Gather([stream], size, gather_send, gather_recv)
        gather.forward(0)

        targets = slot_targets(routes_ref[...], ranks, cap)
        slot = lax.broadcasted_iota(jnp.int32, (slots, rows), 0).astype(full)
        picked = jnp.logical_or(slot == targets[0], slot == targets[1])
        picked = picked.astype(full).astype(low)
        slot_grads[...] = dot(picked, cotangent_ref[...]).astype(low).reshape(count, cap, width)
        grad_copies = [
            send_block(slot_grads, grads_ref, shift, ranks, grad_send, grad_recv)
            for shift in range(1, count)
        ]
        grad_copies.append(pltpu.make_async_copy(slot_grads.at[0], grads_ref.at[0], keep_sem.at[0]))

        for load in loads[:5]:
            load.wait()
        gain = first_ref[...].astype(full)

        def project(block, wanted):
            line = pl.ds(pl.multiple_of(block * rows, rows), rows)
            values_in = stream[block].astype(full)
            normed = (values_in * inverse_norm(values_in) * gain).astype(low)
            if "q" in wanted:
                turned = rotate(dot(normed, query_w[...]), cosine[line, :], sine[line, :])
                queries[block] = (turned.astype(low).astype(full) * HEAD_DIM**-0.5).astype(low)
            if "k" in wanted:
                turned = rotate(dot(normed, key_w[...]), cosine[line, :], sine[line, :])
                keys[block] = turned.astype(low)
                values[block] = dot(normed, value_w[...]).astype(low)

        masks = head_masks(rows)
        query_pos = own * rows + lax.broadcasted_iota(jnp.int32, (rows, rows), 0)
        document_start = start_of(query_pos[:, 0:128], starts_ref)

        def attend(block):
            key_pos = block * rows + lax.broadcasted_iota(jnp.int32, (rows, rows), 1)
            allowed = jnp.logical_and(key_pos >= document_start[:, 0:1], key_pos <= query_pos)
            bias[...] = jnp.where(allowed, 0.0, NEGATIVE)

            def pair(index, carried):
                lanes = pl.ds(pl.multiple_of(index * 128, 128), 128)
                query, key, value = queries[own, :, lanes], keys[block, :, lanes], values[block, :, lanes]
                for head in range(2):
                    scores = dot_nt(jnp.where(masks[head], query, 0), key) + bias[...]
                    old = highest[index, head][:, 0:1]
                    new = jnp.maximum(old, jnp.max(scores, axis=1, keepdims=True))
                    weight = jnp.exp(scores - new).astype(low)
                    factor = jnp.exp(old - new)
                    totals[index, head] = totals[index, head] * factor + dot(
                        weight, jnp.where(masks[head], value, 1)
                    )
                    highest[index, head] = jnp.broadcast_to(new, (rows, 128))
                return carried

            lax.fori_loop(0, pairs, pair, 0)

        totals[...] = jnp.zeros_like(totals)
        highest[...] = jnp.full(highest.shape, NEGATIVE, full)
        project(own, "qk")
        attend(own)
        for place in range(1, size):
            gather.arrive(place)
            if place == size // 2:
                for copy in grad_copies:
                    copy.start()
            block = jnp.bitwise_xor(own, place)

            @pl.when(block < own)
            def _():
                project(block, "k")
                attend(block)

            @pl.when(block > own)
            def _():
                project(block, "q")

        keep = [
            pltpu.make_async_copy(source, target, keep_sem.at[index + 1])
            for index, (source, target) in enumerate(
                ((queries, queries_out), (keys, keys_out), (values, values_out))
            )
        ]
        for copy in keep:
            copy.start()

        lane = lax.broadcasted_iota(jnp.int32, (rows, 128), 1)
        lse_ref[...] = jnp.zeros_like(lse_ref)
        for index in range(pairs):
            halves = []
            for head in range(2):
                total = totals[index, head]
                column = HEAD_DIM if head == 0 else 0
                weight_sum = total[:, column : column + 1]
                halves.append(total / weight_sum)
                lse = highest[index, head][:, 0:1] + jnp.log(weight_sum)
                lse_ref[...] = jnp.where(lane == 2 * index + head, lse, lse_ref[...])
            attended_ref[:, index * 128 : index * 128 + 128] = jnp.where(
                masks[0], halves[0], halves[1]
            )
        loads[5].wait()
        middle = tokens_ref[...].astype(full) + dot(attended_ref[...].astype(low), output_w[...])
        middle_ref[...] = middle
        second = middle * inverse_norm(middle) * second_ref[...].astype(full)
        second_low = second.astype(low)
        outgoing_ref[...] = dot(picked, second_low).astype(low).reshape(count, cap, width)

        experts = previous_ref.shape[1]
        logits = dot(second_low, heads_ref[...])[:, 0:experts] + jnp.dot(
            previous_ref[...], carry_ref[...].astype(full), precision=HIGH
        )
        logits = logits - jnp.max(logits, axis=1, keepdims=True)
        powers = jnp.exp(logits)
        probs_ref[...] = jnp.zeros_like(probs_ref)
        probs_ref[:, 0:experts] = powers / jnp.sum(powers, axis=1, keepdims=True)
        turned = jnp.transpose(probs_ref[...])[0:16]
        expert = lax.broadcasted_iota(jnp.int32, (16, rows), 0)
        weighted = jnp.zeros((slots, rows), full)
        for k in range(2):
            route = routes_ref[k : k + 1, :]
            gate = jnp.sum(jnp.where(expert == route, turned, 0.0), axis=0, keepdims=True)
            weighted = jnp.where(slot == targets[k], gate, weighted)
        gate_column = jnp.sum(weighted, axis=1, keepdims=True)
        for shift in range(count):
            column = jnp.broadcast_to(gate_column[shift * cap : (shift + 1) * cap], (cap, 128))
            gates_ref[shift] = jnp.zeros((8, 128), full)
            gates_ref[shift, :, 0:cap] = jnp.transpose(column)[0:8, :]
        pad = jnp.zeros((6, rows), full)
        target_rows = jnp.concatenate([targets[0], targets[1], pad], axis=0)
        target_rows = jnp.concatenate([target_rows] + [jnp.zeros((120, rows), full)], axis=0)
        targets_ref[...] = jnp.transpose(target_rows)

        gather.finish()
        for copy in keep + grad_copies:
            copy.wait()

    stream_shape = (size, rows, width)
    any_space = pl.BlockSpec(memory_space=pl.ANY)
    in_vmem = pl.BlockSpec(memory_space=pltpu.VMEM)
    square = (width, width)
    return pl.pallas_call(
        kernel,
        out_shape=[
            jax.ShapeDtypeStruct(stream_shape, low),
            jax.ShapeDtypeStruct(stream_shape, low),
            jax.ShapeDtypeStruct(stream_shape, low),
            jax.ShapeDtypeStruct((rows, width), full),
            jax.ShapeDtypeStruct((rows, 128), full),
            jax.ShapeDtypeStruct((rows, width), full),
            jax.ShapeDtypeStruct((rows, 128), full),
            jax.ShapeDtypeStruct((rows, 128), full),
            jax.ShapeDtypeStruct((count, cap, width), low),
            jax.ShapeDtypeStruct((count, 8, 128), full),
            jax.ShapeDtypeStruct((count, cap, width), low),
        ],
        in_specs=[in_vmem] * 4
        + [pl.BlockSpec(memory_space=pltpu.SMEM)]
        + [any_space] * 4
        + [in_vmem] * 4
        + [any_space] * 2,
        out_specs=[any_space] * 3 + [in_vmem] * 7 + [any_space],
        scratch_shapes=[
            pltpu.VMEM(stream_shape, low),
            pltpu.VMEM(stream_shape, low),
            pltpu.VMEM(stream_shape, low),
            pltpu.VMEM(stream_shape, low),
            pltpu.VMEM(square, low),
            pltpu.VMEM(square, low),
            pltpu.VMEM(square, low),
            pltpu.VMEM(square, low),
            pltpu.VMEM((size * rows, 128), full),
            pltpu.VMEM((size * rows, 128), full),
            pltpu.VMEM((rows, rows), full),
            pltpu.VMEM((pairs, 2, rows, 128), full),
            pltpu.VMEM((pairs, 2, rows, 128), full),
            pltpu.VMEM((count, cap, width), low),
            pltpu.SemaphoreType.DMA((6,)),
            pltpu.SemaphoreType.DMA((1, size)),
            pltpu.SemaphoreType.DMA((1, size)),
            pltpu.SemaphoreType.DMA((count,)),
            pltpu.SemaphoreType.DMA((count,)),
            pltpu.SemaphoreType.DMA((4,)),
        ],
        compiler_params=pltpu.CompilerParams(
            collective_id=0, has_side_effects=True, vmem_limit_bytes=60 * 2**20
        ),
        cost_estimate=pl.CostEstimate(
            flops=2 * size * rows * width * width * 3 + 16 * size * rows * rows * width,
            bytes_accessed=20 * 2**20,
            transcendentals=size * rows * rows * 12,
        ),
        name="attend",
    )(
        tokens,
        cotangent,
        previous,
        routes,
        starts,
        *weights,
        *norms,
        heads,
        carry,
        jnp.asarray(tables[0]),
        jnp.asarray(tables[1]),
    )


def column_of(values, index):
    return values[:, index : index + 1]


def backward_layer(
    tokens,
    cotangent,
    previous,
    routes,
    starts,
    forward,
    returns,
    weights,
    norms,
    heads,
    vectors,
    ranks,
    cap,
    size,
):
    rows, width = tokens.shape
    count = ranks[0] * ranks[1]
    slots = count * cap
    pairs = width // 128
    tables = rope_tables(size * rows)
    low, full = jnp.bfloat16, jnp.float32
    experts = previous.shape[1]
    copy_index = count + 1
    stat_rows = 16

    def kernel(
        tokens_ref,
        cotangent_ref,
        previous_ref,
        routes_ref,
        starts_ref,
        attended_ref,
        lse_ref,
        middle_ref,
        probs_ref,
        targets_ref,
        queries_hbm,
        keys_hbm,
        values_hbm,
        back_ref,
        output_ref,
        dots_ref,
        query_hbm,
        key_hbm,
        value_hbm,
        output_hbm,
        first_ref,
        second_ref,
        heads_ref,
        vectors_ref,
        cosine_hbm,
        sine_hbm,
        result_ref,
        token_grads_ref,
        wide_ref,
        small_ref,
        queries,
        keys,
        values,
        query_w,
        key_w,
        value_w,
        output_w,
        cosine,
        sine,
        bias,
        out_grads,
        stats,
        delta,
        middle_grad,
        query_total,
        key_total,
        value_total,
        load_sem,
        gather_send,
        gather_recv,
    ):
        own = lax.axis_index("ctx")
        line = pl.ds(pl.multiple_of(own * rows, rows), rows)
        loads = [
            pltpu.make_async_copy(source, target, load_sem.at[index])
            for index, (source, target) in enumerate(
                (
                    (output_hbm, output_w),
                    (queries_hbm, queries),
                    (keys_hbm, keys),
                    (values_hbm, values),
                    (cosine_hbm.at[line], cosine),
                    (sine_hbm.at[line], sine),
                    (query_hbm, query_w),
                    (key_hbm, key_w),
                    (value_hbm, value_w),
                )
            )
        ]
        for load in loads:
            load.start()
        greet_all(ring_places(size))

        lane = lax.broadcasted_iota(jnp.int32, (rows, 128), 1)
        upstream = cotangent_ref[...].astype(full)
        middle = middle_ref[...]
        inverse_second = inverse_norm(middle)
        unit_second = middle * inverse_second
        gain_second = second_ref[...].astype(full)
        second = unit_second * gain_second
        second_low = second.astype(low)
        heads_in = heads_ref[...]
        mixed = dot(second_low, heads_in)
        probs = probs_ref[...]
        route = [column_of(routes_ref[...], k) for k in range(2)]
        chosen = jnp.logical_or(lane == route[0], lane == route[1])
        gates = jnp.where(chosen, probs, 0.0)
        target = [column_of(targets_ref[...], k) for k in range(2)]

        gate_grad = jnp.zeros((rows, 128), full)
        place = lane.astype(full)
        for k in range(2):
            found = jnp.zeros((rows, 128), full)
            for shift in range(count):
                found = found + jnp.where(
                    jnp.logical_and(target[k] - shift * cap == place, lane < cap),
                    dots_ref[shift, 0:1, :],
                    0.0,
                )
            gate_grad = gate_grad + jnp.where(
                lane == route[k], jnp.sum(found, axis=1, keepdims=True), 0.0
            )
        copy_grad = jnp.sum(upstream * second, axis=1, keepdims=True)
        gate_grad = jnp.where(lane == copy_index, copy_grad, gate_grad)
        direct = column_of(gates, copy_index)
        constants = []
        for index in range(2):
            vector = vectors_ref[index : index + 1, :].astype(full)
            vector_dot = jnp.sum(upstream * vector, axis=1, keepdims=True)
            begin = experts + 2 * index
            spread_of = column_of(mixed, begin + 1) - column_of(mixed, begin)
            mixing = (1.0 / (1.0 + jnp.exp(spread_of)), 1.0 / (1.0 + jnp.exp(-spread_of)))
            gate = column_of(gates, copy_index + 1 + index)
            term = mixing[0] * copy_grad + mixing[1] * vector_dot
            gate_grad = jnp.where(lane == copy_index + 1 + index, term, gate_grad)
            direct = direct + gate * mixing[0]
            constants.append((gate, mixing, vector, vector_dot))
        prob_grad = jnp.where(chosen, gate_grad, 0.0)
        logit_grad = probs * (prob_grad - jnp.sum(probs * prob_grad, axis=1, keepdims=True))
        head_grad = logit_grad
        for index, (gate, mixing, vector, vector_dot) in enumerate(constants):
            mixing_grad = (gate * copy_grad, gate * vector_dot)
            mean = mixing[0] * mixing_grad[0] + mixing[1] * mixing_grad[1]
            for part in range(2):
                head_grad = jnp.where(
                    lane == experts + 2 * index + part,
                    mixing[part] * (mixing_grad[part] - mean),
                    head_grad,
                )
        head_low = head_grad.astype(low)

        slot = lax.broadcasted_iota(jnp.int32, (rows, slots), 1).astype(full)
        picked = [(slot == target[k]).astype(full).astype(low) for k in range(2)]
        second_grad = (
            dot_nt(head_low, heads_in) + direct * upstream + dot(picked[0] + picked[1], back_ref[...])
        )
        normal_grad = second_grad * gain_second
        middle_total = upstream + inverse_second * (
            normal_grad - unit_second * jnp.mean(normal_grad * unit_second, axis=1, keepdims=True)
        )
        middle_grad[...] = middle_total
        middle_low = middle_total.astype(low)
        loads[0].wait()
        out_grad = dot_nt(middle_low, output_w[...]).astype(low)
        out_grads[own] = out_grad
        product = out_grad.astype(full) * attended_ref[...]
        masks = head_masks(rows)
        deltas = jnp.zeros((rows, 128), full)
        for index in range(pairs):
            part = product[:, index * 128 : index * 128 + 128]
            for head in range(2):
                total = jnp.sum(jnp.where(masks[head], part, 0.0), axis=1, keepdims=True)
                deltas = jnp.where(lane == 2 * index + head, total, deltas)
        delta[...] = deltas
        stats[own, 0:stat_rows] = jnp.transpose(lse_ref[...])[0:stat_rows]
        stats[own, stat_rows:] = jnp.transpose(deltas)[0:stat_rows]
        gather = Gather([out_grads, stats], size, gather_send, gather_recv)
        gather.forward(0)

        chosen_out = second * direct
        for k in range(2):
            weight = jnp.sum(jnp.where(lane == route[k], probs, 0.0), axis=1, keepdims=True)
            chosen_out = chosen_out + weight * dot(picked[k], output_ref[...])
        for gate, mixing, vector, vector_dot in constants:
            chosen_out = chosen_out + gate * mixing[1] * vector
        result_ref[...] = (middle + chosen_out).astype(low)
        small_ref[...] = jnp.zeros_like(small_ref)
        small_ref[1:2, :] = jnp.sum(second_grad * unit_second, axis=0, keepdims=True)
        for index, (gate, mixing, vector, vector_dot) in enumerate(constants):
            small_ref[2 + index : 3 + index, :] = jnp.sum(
                gate * mixing[1] * upstream, axis=0, keepdims=True
            )
        small_ref[8:24, :] = dot_tn(head_low, second_low)[0:16]
        carry_grad = lax.dot_general(
            jnp.transpose(logit_grad), previous_ref[...], (((1,), (0,)), ((), ())), precision=HIGH
        )
        small_ref[24:40, 0:experts] = carry_grad[0:16]
        wide_ref[3] = dot_tn(attended_ref[...].astype(low), middle_low).astype(low)

        for load in loads[1:4]:
            load.wait()
        query_total[...] = jnp.zeros_like(query_total)
        key_total[...] = jnp.zeros_like(key_total)
        value_total[...] = jnp.zeros_like(value_total)
        column = lax.broadcasted_iota(jnp.int32, (rows, rows), 0)
        row = lax.broadcasted_iota(jnp.int32, (rows, rows), 1)

        def key_side(block, diagonal):
            key_pos, query_pos = own * rows + column, block * rows + row
            first = start_of(query_pos[0:8], starts_ref)[0:1]
            allowed = jnp.logical_and(key_pos >= first, key_pos <= query_pos)
            bias[...] = jnp.where(allowed, 0.0, NEGATIVE)

            def pair(index, carried):
                lanes = pl.ds(pl.multiple_of(index * 128, 128), 128)
                query, key, value = queries[block, :, lanes], keys[own, :, lanes], values[own, :, lanes]
                grad = out_grads[block, :, lanes]
                key_sum, value_sum = key_total[:, lanes], value_total[:, lanes]
                if diagonal:
                    query_sum = query_total[:, lanes]
                for head in range(2):
                    lse = stats[block, pl.ds(2 * index + head, 1), :]
                    mean = stats[block, pl.ds(stat_rows + 2 * index + head, 1), :]
                    own_key = jnp.where(masks[head], key, 0)
                    weight = jnp.exp(dot_nt(own_key, query) + bias[...] - lse)
                    weight_grad = dot_nt(jnp.where(masks[head], value, 0), grad)
                    score = (weight * (weight_grad - mean)).astype(low)
                    value_sum = value_sum + dot(weight.astype(low), jnp.where(masks[head], grad, 0))
                    key_sum = key_sum + dot(score, jnp.where(masks[head], query, 0))
                    if diagonal:
                        query_sum = query_sum + dot_tn(score, own_key)
                key_total[:, lanes] = key_sum
                value_total[:, lanes] = value_sum
                if diagonal:
                    query_total[:, lanes] = query_sum
                return carried

            lax.fori_loop(0, pairs, pair, 0)

        def query_side(block):
            key_pos, query_pos = block * rows + row, own * rows + column
            first = start_of(query_pos[:, 0:128], starts_ref)[:, 0:1]
            allowed = jnp.logical_and(key_pos >= first, key_pos <= query_pos)
            bias[...] = jnp.where(allowed, 0.0, NEGATIVE)

            def pair(index, carried):
                lanes = pl.ds(pl.multiple_of(index * 128, 128), 128)
                query, key, value = queries[own, :, lanes], keys[block, :, lanes], values[block, :, lanes]
                grad = out_grads[own, :, lanes]
                query_sum = query_total[:, lanes]
                for head in range(2):
                    here = lane == 2 * index + head
                    lse = jnp.sum(jnp.where(here, lse_ref[...], 0.0), axis=1, keepdims=True)
                    mean = jnp.sum(jnp.where(here, delta[...], 0.0), axis=1, keepdims=True)
                    other_key = jnp.where(masks[head], key, 0)
                    weight = jnp.exp(dot_nt(query, other_key) + bias[...] - lse)
                    weight_grad = dot_nt(grad, jnp.where(masks[head], value, 0))
                    score = (weight * (weight_grad - mean)).astype(low)
                    query_sum = query_sum + dot(score, other_key)
                query_total[:, lanes] = query_sum
                return carried

            lax.fori_loop(0, pairs, pair, 0)

        key_side(own, True)
        for place in range(1, size):
            block = jnp.bitwise_xor(own, place)

            @pl.when(block < own)
            def _():
                query_side(block)

        for place in range(1, size):
            gather.arrive(place)
            block = jnp.bitwise_xor(own, place)

            @pl.when(block > own)
            def _():
                key_side(block, False)

        for load in loads[4:]:
            load.wait()
        inputs = tokens_ref[...].astype(full)
        inverse_first = inverse_norm(inputs)
        unit_first = inputs * inverse_first
        gain_first = first_ref[...].astype(full)
        normed = (unit_first * gain_first).astype(low)
        turn = -sine[...]
        query_low = rotate(query_total[...] * HEAD_DIM**-0.5, cosine[...], turn).astype(low)
        key_low = rotate(key_total[...], cosine[...], turn).astype(low)
        value_low = value_total[...].astype(low)
        first_grad = (
            dot_nt(query_low, query_w[...])
            + dot_nt(key_low, key_w[...])
            + dot_nt(value_low, value_w[...])
        )
        for index, part in enumerate((query_low, key_low, value_low)):
            wide_ref[index] = dot_tn(normed, part).astype(low)
        small_ref[0:1, :] = jnp.sum(first_grad * unit_first, axis=0, keepdims=True)
        normal_grad = first_grad * gain_first
        token_grads_ref[...] = middle_grad[...] + inverse_first * (
            normal_grad - unit_first * jnp.mean(normal_grad * unit_first, axis=1, keepdims=True)
        )
        gather.finish()

    stream_shape = (size, rows, width)
    any_space = pl.BlockSpec(memory_space=pl.ANY)
    in_vmem = pl.BlockSpec(memory_space=pltpu.VMEM)
    square = (width, width)
    return pl.pallas_call(
        kernel,
        out_shape=[
            jax.ShapeDtypeStruct((rows, width), low),
            jax.ShapeDtypeStruct((rows, width), full),
            jax.ShapeDtypeStruct((4,) + square, low),
            jax.ShapeDtypeStruct((40, width), full),
        ],
        in_specs=[in_vmem] * 4
        + [pl.BlockSpec(memory_space=pltpu.SMEM)]
        + [in_vmem] * 5
        + [any_space] * 3
        + [in_vmem] * 3
        + [any_space] * 4
        + [in_vmem] * 4
        + [any_space] * 2,
        out_specs=[in_vmem] * 4,
        scratch_shapes=[
            pltpu.VMEM(stream_shape, low),
            pltpu.VMEM(stream_shape, low),
            pltpu.VMEM(stream_shape, low),
            pltpu.VMEM(square, low),
            pltpu.VMEM(square, low),
            pltpu.VMEM(square, low),
            pltpu.VMEM(square, low),
            pltpu.VMEM((rows, 128), full),
            pltpu.VMEM((rows, 128), full),
            pltpu.VMEM((rows, rows), full),
            pltpu.VMEM(stream_shape, low),
            pltpu.VMEM((size, 2 * stat_rows, rows), full),
            pltpu.VMEM((rows, 128), full),
            pltpu.VMEM((rows, width), full),
            pltpu.VMEM((rows, width), full),
            pltpu.VMEM((rows, width), full),
            pltpu.VMEM((rows, width), full),
            pltpu.SemaphoreType.DMA((9,)),
            pltpu.SemaphoreType.DMA((2, size)),
            pltpu.SemaphoreType.DMA((2, size)),
        ],
        compiler_params=pltpu.CompilerParams(
            collective_id=2, has_side_effects=True, vmem_limit_bytes=60 * 2**20
        ),
        cost_estimate=pl.CostEstimate(
            flops=14 * rows * width * width * 2 + 20 * size * rows * rows * width,
            bytes_accessed=30 * 2**20,
            transcendentals=size * rows * rows * 12,
        ),
        name="backward",
    )(
        tokens,
        cotangent,
        previous,
        routes,
        starts,
        *forward,
        *returns,
        *weights,
        *norms,
        heads,
        vectors,
        jnp.asarray(tables[0]),
        jnp.asarray(tables[1]),
    )


def local(
    tokens,
    cotangent,
    previous,
    routes,
    boundaries,
    norm_first,
    query_weight,
    key_weight,
    value_weight,
    output_weight,
    norm_second,
    router,
    gate_carry,
    constant_map,
    constant_vector,
    expert_gate,
    expert_linear,
    expert_down,
):
    model_width = tokens.shape[2]
    ring = lax.axis_size("ctx")
    group_size = expert_gate.shape[0]
    exchange_count = lax.axis_size("exp")
    spread = ring // group_size
    ranks = (exchange_count, group_size, spread)
    slot_total = exchange_count * group_size * CAP
    expert_total = router.shape[1]
    heads = jnp.concatenate([router, constant_map[0], constant_map[1]], axis=1)
    head_count = heads.shape[1]
    heads = jnp.pad(heads, ((0, 0), (0, 128 - head_count)))
    norms = (norm_first[None], norm_second[None])
    weights = (query_weight, key_weight, value_weight, output_weight)
    (
        queries,
        keys,
        values,
        attended,
        lse,
        middle,
        probs,
        targets,
        outgoing,
        slot_gates,
        grads_in,
    ) = attend_layer(
        tokens[0],
        cotangent[0],
        previous[0],
        routes[0].T,
        boundaries,
        weights,
        norms,
        heads,
        gate_carry,
        ranks,
        CAP,
        ring,
    )
    home_grads, returned, dots, gate_terms, linear_terms, down_terms = expert_layer(
        outgoing,
        slot_gates,
        grads_in.reshape(slot_total, model_width),
        (expert_gate, expert_linear, expert_down),
        ranks,
        lax.axis_size("dp"),
    )
    result, token_grads, wide, small = backward_layer(
        tokens[0],
        cotangent[0],
        previous[0],
        routes[0],
        boundaries,
        (attended, lse, middle, probs, targets, queries, keys, values),
        (
            home_grads.reshape(slot_total, model_width),
            returned.reshape(slot_total, model_width),
            dots,
        ),
        weights,
        norms,
        heads,
        constant_vector,
        ranks,
        CAP,
        ring,
    )
    own_expert = lax.axis_index("ctx") // spread

    def collect(terms):
        share = scatter_sum(terms, "dp")
        bit = 1
        while bit < spread:
            share = (
                share.astype(jnp.float32) + swap(share, "ctx", bit).astype(jnp.float32)
            ).astype(jnp.bfloat16)
            bit *= 2
        parts, order = [share], [0]
        while bit < lax.axis_size("ctx"):
            bit *= 2
        while bit > spread:
            bit //= 2
            parts = parts + [swap(part, "ctx", bit) for part in parts]
            order = order + [place ^ (bit // spread) for place in order]
        stacked = jnp.stack(parts)
        places = jnp.array(order, jnp.int32) ^ own_expert
        inverse = jnp.argsort(places)
        return stacked[inverse].astype(jnp.float32)

    experts = (collect(gate_terms), collect(linear_terms), collect(down_terms))
    steps = [(axis, bit) for axis in ("ctx", "exp", "dp") for bit in bits_of(axis)]
    units = 2 ** len(steps)
    wide = wide.reshape(4 * model_width, model_width)
    flat = small.reshape(-1)
    small_rows = -(-flat.size // (units * model_width))
    wide_rows = wide.shape[0] // units
    unit_rows = -(-(small_rows + wide_rows) // 16) * 16
    flat = jnp.pad(flat, (0, units * small_rows * model_width - flat.size))
    packed = jnp.concatenate(
        [
            wide.reshape(units, wide_rows, model_width).astype(jnp.bfloat16),
            flat.reshape(units, small_rows, model_width).astype(jnp.bfloat16),
            jnp.zeros((units, unit_rows - wide_rows - small_rows, model_width), jnp.bfloat16),
        ],
        axis=1,
    )
    for axis, bit in steps:
        packed = packed.reshape((2, -1) + packed.shape[1:])
        packed = halve(packed, axis, bit, 0)
    for axis, bit in steps[::-1]:
        other = swap(packed, axis, bit)
        own = (lax.axis_index(axis) // bit) % 2
        packed = jnp.concatenate(
            [jnp.where(own == 0, packed, other), jnp.where(own == 0, other, packed)], axis=0
        )
    packed = packed.astype(jnp.float32)
    wide = packed[:, :wide_rows].reshape(4, model_width, model_width)
    flat = packed[:, wide_rows : wide_rows + small_rows].reshape(-1)
    small = flat[: small.size].reshape(small.shape)
    head_grads = small[8 : 8 + head_count].T
    return (
        result[None],
        token_grads[None],
        small[0],
        wide[0],
        wide[1],
        wide[2],
        wide[3],
        small[1],
        head_grads[:, :expert_total],
        small[24 : 24 + expert_total, :expert_total].T,
        jnp.stack(
            [head_grads[:, expert_total : expert_total + 2], head_grads[:, expert_total + 2 :]]
        ),
        small[2:4],
        experts[0],
        experts[1],
        experts[2],
    )


def solution(mesh):
    return jax.shard_map(
        local,
        mesh=mesh,
        in_specs=(
            P(("dp", "exp"), "ctx", None),
            P(("dp", "exp"), "ctx", None),
            P(("dp", "exp"), "ctx", None),
            P(("dp", "exp"), "ctx", None),
            P(("dp", "exp"), None),
            P(),
            P(),
            P(),
            P(),
            P(),
            P(),
            P(),
            P(),
            P(),
            P(),
            P("exp", None, None),
            P("exp", None, None),
            P("exp", None, None),
        ),
        out_specs=(
            P(("dp", "exp"), "ctx", None),
            P(("dp", "exp"), "ctx", None),
            P(),
            P(),
            P(),
            P(),
            P(),
            P(),
            P(),
            P(),
            P(),
            P(),
            P("exp", None, "dp"),
            P("exp", None, "dp"),
            P("exp", "dp", None),
        ),
        check_vma=False,
    )
```

time: 767 us -> 533 us (0.69)
  matrix products: 114 us -> 0 us
  local copies, waits for them, and re-layouts: 119 us -> 40.5 us
  Pallas kernels: 87.6 us -> 158 us
  other arithmetic: 121 us -> 60.7 us
  waiting for transfers between devices: 277 us -> 230 us
  between operations: 15.5 us -> 1.54 us
  starting transfers between devices: 20.6 us -> 33.2 us
    dot_general x42 -> x0, matrix products: 114 us -> none  [the longest x6 20.1 us: scores_and_mask(): jnp.einsum('qhd,khd->qhk', queries, key_block, preferred_element_type=jnp...]
    pallas_call x1 -> x2, Pallas kernels: 22.8 us -> 81.6 us  [the longest x1 44.1 us: backward_layer(): pl.pallas_call(kernel, out_shape=[jax.ShapeDtypeStruct((rows, width), low...]
    reduce_sum x22 -> x0, other arithmetic: 41.1 us -> none  [the longest x3 17.3 us: visit(): running_sum = running_sum * factor + jnp.sum(weights, axis=-1)]
    reduce_scatter x1 -> x0, waiting for transfers between devices: 35.6 us -> none  [local(): lax.psum_scatter(key_terms.reshape(key_count, 2 * model_width).astype(jnp...]
    dynamic_slice x18 -> x0, local copies, waits for them, and re-layouts: 15.5 us -> none  [the longest x6 11.6 us: visit(): lax.dynamic_slice_in_dim(value_rows, begin, block_size, 0)]
    ppermute x25, starting transfers between devices: 20.3 us -> 33.2 us  [swap(): lax.ppermute(values, axis, [(i, i ^ bit) for i in range(lax.axis_size(axi...]
    dynamic_update_slice x6 -> x0, local copies, waits for them, and re-layouts: 12.7 us -> none  [local(): lax.scan(visit, zero_heads, jnp.arange(key_count // block_size, dtype=jnp...]
    gather x4 -> x0, local copies, waits for them, and re-layouts: 12.6 us -> none  [the longest x1 5.4 us: local(): home_grads[safe_targets].astype(jnp.float32)]
  transfers between devices with their start and end apart: 28 -> 25, of which waited for: 16 -> 15; matrix products, arithmetic and copies ran while one was open for 13% -> 10% of each run, Pallas kernels for 3% -> 0%
where the time goes in v3:
time: 533 us; the launch traced here: 524 us
  waiting for transfers between devices  230 us (43%)
  Pallas kernels  158 us (30%)
  other arithmetic  60.7 us (11%)
  local copies, waits for them, and re-layouts  40.5 us (8%)
  starting transfers between devices  33.2 us (6%)
    ppermute x25, waiting for transfers between devices, swap(): lax.ppermute(values, axis, [(i, i ^ bit) for i in range(lax.axis_size(axi...  230 us
    pallas_call x1, Pallas kernels, expert_layer(): pl.pallas_call(kernel, out_shape=[jax.ShapeDtypeStruct(outgoing.shape, lo...  76.8 us
    pallas_call x1, Pallas kernels, backward_layer(): pl.pallas_call(kernel, out_shape=[jax.ShapeDtypeStruct((rows, width), low...  44.1 us
    pallas_call x1, Pallas kernels, attend_layer(): pl.pallas_call(kernel, out_shape=[jax.ShapeDtypeStruct(stream_shape, low)...  37.6 us
    ppermute x25, starting transfers between devices, swap(): lax.ppermute(values, axis, [(i, i ^ bit) for i in range(lax.axis_size(axi...  33.2 us
    convert_element_type x11, other arithmetic, halve(): return total.astype(jnp.bfloat16)  17.5 us
    convert_element_type x3, other arithmetic, collect(): return stacked[inverse].astype(jnp.float32)  16.2 us
    unnamed x53, local copies, waits for them, and re-layouts  11.3 us
  transfers between devices with their start and end apart: 25, of which 15 were waited for; matrix products, arithmetic and copies ran while one was open for 10% of the time, Pallas kernels for 0%

profile of v3, /device:TPU:0, one launch (start us, length us, event | category | flops | bytes accessed | tf_op | source)
XLA Modules:
  0.0 524.0 jit_solution(1855233310532068173)
XLA Ops:
  0.7 1.5 copy.57
  3.7 1.3 broadcast_in_dim.24.first_ref
  5.0 1.3 broadcast_in_dim.25.second_ref
  8.6 37.6 %attend.1 = (bf16[4,384,768]{2,1,0:T(8,128)(2,1)}, bf16[4,384,768]{2,1,0:T(8,128)(2,1)}, bf16[4,384,768]{2,1,0:T(8,128)(2,1)}, f32[384,768]{1,0:T(8,128)}, f32[3...) custom-call(bf16[384,768]{1,0:T(8,128)(2,1)} %bitcast.133, ...), custom_call_target="tpu_custom_call" | custom-call | flops 12683575296 | bytes 20971520 | tf_op jit(solution)/shard_map/attend/pallas_call | solution.py:664
  46.2 76.8 %experts.1 = (bf16[8,96,768]{2,1,0:T(8,128)(2,1)}, bf16[8,96,768]{2,1,0:T(8,128)(2,1)}, f32[8,8,128]{2,1,0:T(8,128)}, bf16[4,768,512]{2,1,0:T(8,128)(2,1)}, bf16...) custom-call(bf16[8,96,768]{2,1,0:T(8,128)(2,1)} %get-tuple-element.47.outgoing_ref, ...), custom_call_target="tpu_custom_call" | custom-call | flops 21743271936 | bytes 25952256 | tf_op jit(solution)/shard_map/experts/pallas_call | solution.py:256
  122.9 44.1 %backward.1 = (bf16[384,768]{1,0:T(8,128)(2,1)}, f32[384,768]{1,0:T(8,128)}, bf16[4,768,768]{2,1,0:T(8,128)(2,1)}, f32[40,768]{1,0:T(8,128)}) custom-call(bf16[384,768]{1,0:T(8,128)(2,1)} %bitcast.134, bf16[384,768]{1,0:T(8,128)(2,1)} %bitcast.136, f32[384,12]{1,0:T(8,128)} %bitcast.129, s32[384,2]{1,0:T(8,128)} %bitcast.126, s32[1,8]{1,0:T(1,128)} %starts_ref.3, ...), custom_call_target="tpu_custom_call" | custom-call | flops 15401484288 | bytes 31457280 | tf_op jit(solution)/shard_map/backward/pallas_call | solution.py:1051
  168.2 3.7 maximum_maximum_fusion
  172.1 2.2 copy-done.1
  174.3 5.2 collective-permute-done
  179.5 3.3 fusion
  182.8 1.2 dynamic-slice_bitcast_fusion.4
  184.7 31.9 %collective-permute-done.1 = bf16[8,112,768]{2,1,0:T(8,128)(2,1)} collective-permute-done((bf16[8,112,768]{2,1,0:T(8,128)(2,1)}, bf16[8,112,768]{2,1,0:T(8,128)(2,1)}, u32[]{:S(2)}, u32[]{:S(2)}) %collective-permute-start.1) | collective-permute-done | bytes 1376288 | tf_op jit(solution)/shard_map/ppermute | solution.py:29
  216.5 1.7 fusion.4
  218.2 1.1 copy-done.6
  220.2 1.1 collective-permute-start.2
  221.3 15.9 %collective-permute-done.2 = bf16[4,112,768]{2,1,0:T(8,128)(2,1)} collective-permute-done((bf16[4,112,768]{2,1,0:T(8,128)(2,1)}, bf16[4,112,768]{2,1,0:T(8,128)(2,1)}, u32[]{:S(2)}, u32[]{:S(2)}) %collective-permute-start.2) | collective-permute-done | bytes 688160 | tf_op jit(solution)/shard_map/ppermute | solution.py:29
  237.2 1.5 fusion.8
  239.5 1.6 collective-permute-start.3
  241.2 6.9 %collective-permute-done.3 = bf16[2,112,768]{2,1,0:T(8,128)(2,1)} collective-permute-done((bf16[2,112,768]{2,1,0:T(8,128)(2,1)S(1)}, bf16[2,112,768]{2,1,0:T(8,128)(2,1)}, u32[]{:S(2)}, u32[]{:S(2)}) %collective-permute-start.3) | collective-permute-done | bytes 344096 | tf_op jit(solution)/shard_map/ppermute | solution.py:29
  248.0 1.2 fusion.9
  249.9 2.6 collective-permute-start.4
  252.5 6.1 %collective-permute-done.4 = bf16[1,112,768]{2,1,0:T(8,128)(2,1)} collective-permute-done((bf16[1,112,768]{2,1,0:T(8,128)(2,1)}, bf16[1,112,768]{2,1,0:T(8,128)(2,1)}, u32[]{:S(2)}, u32[]{:S(2)}) %collective-permute-start.4) | collective-permute-done | bytes 172064 | tf_op jit(solution)/shard_map/ppermute | solution.py:29
  258.5 1.6 add_convert_fusion
  260.8 5.9 %collective-permute-done.5 = bf16[1,112,768]{2,1,0:T(8,128)(2,1)S(1)} collective-permute-done((bf16[1,112,768]{2,1,0:T(8,128)(2,1)}, bf16[1,112,768]{2,1,0:T(8,128)(2,1)S(1)}, u32[]{:S(2)}, u32[]{:S(2)}) %collective-permute-start.5) | collective-permute-done | bytes 172064 | tf_op jit(solution)/shard_map/ppermute | solution.py:29
  268.4 3.0 collective-permute-start.6
  271.4 1.2 dynamic-slice_bitcast_fusion.3
  272.7 2.8 dynamic-slice_bitcast_fusion.2
  275.5 2.0 collective-permute-start.15
  277.5 3.0 collective-permute-done.6
  280.5 1.2 broadcast_select_fusion.7
  283.3 1.1 collective-permute-start.7
  284.4 1.2 dynamic-slice_bitcast_fusion.1
  285.6 2.0 collective-permute-start.20
  287.6 6.9 %collective-permute-done.7 = bf16[4,112,768]{2,1,0:T(8,128)(2,1)} collective-permute-done((bf16[4,112,768]{2,1,0:T(8,128)(2,1)}, bf16[4,112,768]{2,1,0:T(8,128)(2,1)}, u32[]{:S(2)}, u32[]{:S(2)}) %collective-permute-start.7) | collective-permute-done | bytes 688160 | tf_op jit(solution)/shard_map/ppermute | solution.py:29
  294.5 1.3 broadcast_select_fusion.5
  295.9 3.5 collective-permute-start.8
  299.5 23.1 %collective-permute-done.10 = bf16[2,768,512]{2,1,0:T(8,128)(2,1)} collective-permute-done((bf16[2,768,512]{2,1,0:T(8,128)(2,1)}, bf16[2,768,512]{2,1,0:T(8,128)(2,1)}, u32[]{:S(2)}, u32[]{:S(2)}) %collective-permute-start.10) | collective-permute-done | bytes 1572896 | tf_op jit(solution)/shard_map/ppermute | solution.py:29
  322.6 1.9 fusion.3
  324.5 2.5 collective-permute-start.11
  327.1 46.1 %collective-permute-done.15 = bf16[2,768,512]{2,1,0:T(8,128)(2,1)} collective-permute-done((bf16[2,768,512]{2,1,0:T(8,128)(2,1)}, bf16[2,768,512]{2,1,0:T(8,128)(2,1)}, u32[]{:S(2)}, u32[]{:S(2)}) %collective-permute-start.15) | collective-permute-done | bytes 1572896 | tf_op jit(solution)/shard_map/ppermute | solution.py:29
  373.2 1.9 fusion.2
  375.1 2.5 collective-permute-start.16
  377.6 27.8 %collective-permute-done.20 = bf16[2,512,768]{2,1,0:T(8,128)(2,1)} collective-permute-done((bf16[2,512,768]{2,1,0:T(8,128)(2,1)}, bf16[2,512,768]{2,1,0:T(8,128)(2,1)}, u32[]{:S(2)}, u32[]{:S(2)}) %collective-permute-start.20) | collective-permute-done | bytes 1572896 | tf_op jit(solution)/shard_map/ppermute | solution.py:29
  405.4 1.8 fusion.1
  408.3 7.4 %collective-permute-start.12 = (bf16[768,512]{1,0:T(8,128)(2,1)S(1)}, bf16[768,512]{1,0:T(8,128)(2,1)S(1)}, u32[]{:S(2)}, u32[]{:S(2)}) collective-permute-start(bf16[768,512]{1,0:T(8,128)(2,1)S(1)} %fusion.7), channel_id=1, source_target_pairs={{0,4},{2,6},{4,0},{6,2},{1,5},{3,7},{5,1},{7,3},{8,12},{10,14},{12... | collective-permute-start | bytes 2359304 | tf_op jit(solution)/shard_map/ppermute | solution.py:29
  415.9 2.0 pad_maximum_fusion.3
  418.9 24.4 %collective-permute-done.16 = bf16[768,512]{1,0:T(8,128)(2,1)S(1)} collective-permute-done((bf16[768,512]{1,0:T(8,128)(2,1)S(1)}, bf16[768,512]{1,0:T(8,128)(2,1)S(1)}, u32[]{:S(2)}, u32[]{:S(2)}) %collective-permute-start.16) | collective-permute-done | bytes 786464 | tf_op jit(solution)/shard_map/ppermute | solution.py:29
  443.3 1.4 fusion.6
  444.6 9.3 %collective-permute-done.21 = bf16[512,768]{1,0:T(8,128)(2,1)S(1)} collective-permute-done((bf16[512,768]{1,0:T(8,128)(2,1)S(1)}, bf16[512,768]{1,0:T(8,128)(2,1)S(1)}, u32[]{:S(2)}, u32[]{:S(2)}) %collective-permute-start.21) | collective-permute-done | bytes 786464 | tf_op jit(solution)/shard_map/ppermute | solution.py:29
  454.0 1.2 fusion.5
  455.7 4.4 collective-permute-done.17
  460.9 12.9 %collective-permute-done.22 = bf16[512,768]{1,0:T(8,128)(2,1)} collective-permute-done((bf16[512,768]{1,0:T(8,128)(2,1)}, bf16[512,768]{1,0:T(8,128)(2,1)}, u32[]{:S(2)}, u32[]{:S(2)}) %collective-permute-start.22) | collective-permute-done | bytes 786464 | tf_op jit(solution)/shard_map/ppermute | solution.py:29
  474.7 2.0 pad_maximum_fusion
  476.7 2.4 gather_fusion
  479.1 5.5 %convert_element_type.181 = f32[4,768,512]{2,1,0:T(8,128)} convert(bf16[4,768,512]{2,1,0:T(8,128)(2,1)} %gather_fusion) | non-fusion elementwise | flops 1572864 | bytes 9437184 | tf_op jit(solution)/shard_map/convert_element_type | solution.py:1223
  484.6 2.1 pad_maximum_fusion.1
  486.7 2.4 gather_fusion.1
  489.1 5.5 %convert_element_type.190 = f32[4,768,512]{2,1,0:T(8,128)} convert(bf16[4,768,512]{2,1,0:T(8,128)(2,1)} %gather_fusion.1) | non-fusion elementwise | flops 1572864 | bytes 9437184 | tf_op jit(solution)/shard_map/convert_element_type | solution.py:1223
  494.6 2.0 pad_maximum_fusion.2
  496.6 2.5 gather_fusion.2
  499.1 5.3 %convert_element_type.199 = f32[4,512,768]{2,1,0:T(8,128)} convert(bf16[4,512,768]{2,1,0:T(8,128)(2,1)} %gather_fusion.2) | non-fusion elementwise | flops 1572864 | bytes 9437184 | tf_op jit(solution)/shard_map/convert_element_type | solution.py:1223
  504.4 2.0 broadcast_select_fusion.1
  506.5 4.9 maximum_convert_fusion
  512.7 7.7 %fusion.10 = (f32[8,96,768]{2,1,0:T(8,128)}, f32[8,96,768]{2,1,0:T(8,128)}, f32[8,96,768]{2,1,0:T(8,128)}, f32[8,96,768]{2,1,0:T(8,128)}) fusion(f32[32,112,768]{2,1,0:T(8,128)} %maximum_convert_fusion), kind=kLoop, calls=%fused_computation.68 | loop fusion | bytes 18874368 | tf_op jit(solution)/shard_map/slice | solution.py:1263
  (112 shorter events, 21.5 us)
Async XLA Ops:
  3.0 43.2 %copy-start.20 = (s32[1,384,2]{2,1,0:T(8,128)}, s32[1,384,2]{2,1,0:T(8,128)S(1)}, u32[]{:S(2)}) copy-start(s32[1,384,2]{2,1,0:T(8,128)S(1)} %copy.58) | copy-start | bytes 9220
  171.9 2.4 copy-start.1
  174.3 5.2 collective-permute-start
  184.0 32.5 %collective-permute-start.1 = (bf16[8,112,768]{2,1,0:T(8,128)(2,1)}, bf16[8,112,768]{2,1,0:T(8,128)(2,1)}, u32[]{:S(2)}, u32[]{:S(2)}) collective-permute-start(bf16[8,112,768]{2,1,0:T(8,128)(2,1)} %dynamic-slice_bitcast_fusion.4), channel_id=1, source_target_pairs={{0,4},{2,6},{4,0},{6,2},{1,5},{3,7},{5,1},{7,3},{8,12},{10,14},{12... | collective-permute-start | bytes 4128776 | tf_op jit(solution)/shard_map/ppermute | solution.py:29
  218.2 1.1 copy-start.6
  220.2 17.0 %collective-permute-start.2 = (bf16[4,112,768]{2,1,0:T(8,128)(2,1)}, bf16[4,112,768]{2,1,0:T(8,128)(2,1)}, u32[]{:S(2)}, u32[]{:S(2)}) collective-permute-start(bf16[4,112,768]{2,1,0:T(8,128)(2,1)} %dynamic-slice_bitcast_fusion.8), channel_id=1, source_target_pairs={{0,1},{1,0},{2,3},{3,2},{4,5},{5,4},{6,7},{7,6},{8,9},{9,8},{10,11... | collective-permute-start | bytes 2064392 | tf_op jit(solution)/shard_map/ppermute | solution.py:29
  221.3 50.1 %copy-start.10 = (bf16[4,768,512]{2,1,0:T(8,128)(2,1)S(1)}, bf16[4,768,512]{2,1,0:T(8,128)(2,1)}, u32[]{:S(2)}) copy-start(bf16[4,768,512]{2,1,0:T(8,128)(2,1)} %get-tuple-element.57) | copy-start | bytes 9437188
  238.6 0.8 copy-start.13
  239.5 8.5 %collective-permute-start.3 = (bf16[2,112,768]{2,1,0:T(8,128)(2,1)S(1)}, bf16[2,112,768]{2,1,0:T(8,128)(2,1)}, u32[]{:S(2)}, u32[]{:S(2)}) collective-permute-start(bf16[2,112,768]{2,1,0:T(8,128)(2,1)S(1)} %dynamic-slice_bitcast_fusion.9), channel_id=1, source_target_pairs={{0,8},{8,0},{16,24},{24,16},{1,9},{9,1},{17,25},{25,17},{2,10},{10... | collective-permute-start | bytes 1032200 | tf_op jit(solution)/shard_map/ppermute | solution.py:29
  249.9 8.6 %collective-permute-start.4 = (bf16[1,112,768]{2,1,0:T(8,128)(2,1)}, bf16[1,112,768]{2,1,0:T(8,128)(2,1)}, u32[]{:S(2)}, u32[]{:S(2)}) collective-permute-start(bf16[1,112,768]{2,1,0:T(8,128)(2,1)} %constant_dynamic-slice_fusion), channel_id=1, source_target_pairs={{0,16},{8,24},{16,0},{24,8},{1,17},{9,25},{17,1},{25,9},{2,18},{10... | collective-permute-start | bytes 516104 | tf_op jit(solution)/shard_map/ppermute | solution.py:29
  260.2 6.5 %collective-permute-start.5 = (bf16[1,112,768]{2,1,0:T(8,128)(2,1)}, bf16[1,112,768]{2,1,0:T(8,128)(2,1)S(1)}, u32[]{:S(2)}, u32[]{:S(2)}) collective-permute-start(bf16[1,112,768]{2,1,0:T(8,128)(2,1)} %add_convert_fusion), channel_id=1, source_target_pairs={{0,16},{8,24},{16,0},{24,8},{1,17},{9,25},{17,1},{25,9},{2,18},{10... | collective-permute-start | bytes 516104 | tf_op jit(solution)/shard_map/ppermute | solution.py:29
  267.6 0.7 copy-start.14
  267.7 0.7 copy-start.15
  268.4 12.1 %collective-permute-start.6 = (bf16[2,112,768]{2,1,0:T(8,128)(2,1)S(1)}, bf16[2,112,768]{2,1,0:T(8,128)(2,1)}, u32[]{:S(2)}, u32[]{:S(2)}) collective-permute-start(bf16[2,112,768]{2,1,0:T(8,128)(2,1)S(1)} %pad_maximum_fusion.6), channel_id=1, source_target_pairs={{0,8},{8,0},{16,24},{24,16},{1,9},{9,1},{17,25},{25,17},{2,10},{10... | collective-permute-start | bytes 1032200 | tf_op jit(solution)/shard_map/ppermute | solution.py:29
  272.6 50.0 %collective-permute-start.10 = (bf16[2,768,512]{2,1,0:T(8,128)(2,1)}, bf16[2,768,512]{2,1,0:T(8,128)(2,1)}, u32[]{:S(2)}, u32[]{:S(2)}) collective-permute-start(bf16[2,768,512]{2,1,0:T(8,128)(2,1)} %dynamic-slice_bitcast_fusion.3), channel_id=1, source_target_pairs={{0,8},{8,0},{16,24},{24,16},{1,9},{9,1},{17,25},{25,17},{2,10},{10... | collective-permute-start | bytes 4718600 | tf_op jit(solution)/shard_map/ppermute | solution.py:29
  272.7 11.7 %copy-start.8 = (bf16[4,512,768]{2,1,0:T(8,128)(2,1)S(1)}, bf16[4,512,768]{2,1,0:T(8,128)(2,1)}, u32[]{:S(2)}) copy-start(bf16[4,512,768]{2,1,0:T(8,128)(2,1)} %get-tuple-element.61) | copy-start | bytes 9437188
  275.5 97.7 %collective-permute-start.15 = (bf16[2,768,512]{2,1,0:T(8,128)(2,1)}, bf16[2,768,512]{2,1,0:T(8,128)(2,1)}, u32[]{:S(2)}, u32[]{:S(2)}) collective-permute-start(bf16[2,768,512]{2,1,0:T(8,128)(2,1)} %dynamic-slice_bitcast_fusion.2), channel_id=1, source_target_pairs={{0,8},{8,0},{16,24},{24,16},{1,9},{9,1},{17,25},{25,17},{2,10},{10... | collective-permute-start | bytes 4718600 | tf_op jit(solution)/shard_map/ppermute | solution.py:29
  281.6 0.7 copy-start.12
  283.3 11.3 %collective-permute-start.7 = (bf16[4,112,768]{2,1,0:T(8,128)(2,1)}, bf16[4,112,768]{2,1,0:T(8,128)(2,1)}, u32[]{:S(2)}, u32[]{:S(2)}) collective-permute-start(bf16[4,112,768]{2,1,0:T(8,128)(2,1)} %pad_maximum_fusion.5), channel_id=1, source_target_pairs={{0,1},{1,0},{2,3},{3,2},{4,5},{5,4},{6,7},{7,6},{8,9},{9,8},{10,11... | collective-permute-start | bytes 2064392 | tf_op jit(solution)/shard_map/ppermute | solution.py:29
  285.6 119.8 %collective-permute-start.20 = (bf16[2,512,768]{2,1,0:T(8,128)(2,1)}, bf16[2,512,768]{2,1,0:T(8,128)(2,1)}, u32[]{:S(2)}, u32[]{:S(2)}) collective-permute-start(bf16[2,512,768]{2,1,0:T(8,128)(2,1)} %dynamic-slice_bitcast_fusion.1), channel_id=1, source_target_pairs={{0,8},{8,0},{16,24},{24,16},{1,9},{9,1},{17,25},{25,17},{2,10},{10... | collective-permute-start | bytes 4718600 | tf_op jit(solution)/shard_map/ppermute | solution.py:29
  287.6 35.0 %copy-start.11 = (bf16[4,768,512]{2,1,0:T(8,128)(2,1)S(1)}, bf16[4,768,512]{2,1,0:T(8,128)(2,1)}, u32[]{:S(2)}) copy-start(bf16[4,768,512]{2,1,0:T(8,128)(2,1)} %get-tuple-element.57) | copy-start | bytes 9437188
  295.9 77.2 %copy-start.9 = (bf16[4,768,512]{2,1,0:T(8,128)(2,1)S(1)}, bf16[4,768,512]{2,1,0:T(8,128)(2,1)}, u32[]{:S(2)}) copy-start(bf16[4,768,512]{2,1,0:T(8,128)(2,1)} %get-tuple-element.59) | copy-start | bytes 9437188
  295.9 119.8 %collective-permute-start.8 = (bf16[8,112,768]{2,1,0:T(8,128)(2,1)S(1)}, bf16[8,112,768]{2,1,0:T(8,128)(2,1)S(1)}, u32[]{:S(2)}, u32[]{:S(2)}) collective-permute-start(bf16[8,112,768]{2,1,0:T(8,128)(2,1)S(1)} %pad_maximum_fusion.4), channel_id=1, source_target_pairs={{0,4},{2,6},{4,0},{6,2},{1,5},{3,7},{5,1},{7,3},{8,12},{10,14},{12... | collective-permute-start | bytes 4128776 | tf_op jit(solution)/shard_map/ppermute | solution.py:29
  324.5 83.6 %collective-permute-start.11 = (bf16[768,512]{1,0:T(8,128)(2,1)S(1)}, bf16[768,512]{1,0:T(8,128)(2,1)S(1)}, u32[]{:S(2)}, u32[]{:S(2)}) collective-permute-start(bf16[768,512]{1,0:T(8,128)(2,1)S(1)} %dynamic-slice_bitcast_fusion.7), channel_id=1, source_target_pairs={{0,16},{8,24},{16,0},{24,8},{1,17},{9,25},{17,1},{25,9},{2,18},{10... | collective-permute-start | bytes 2359304 | tf_op jit(solution)/shard_map/ppermute | solution.py:29
  375.1 68.2 %collective-permute-start.16 = (bf16[768,512]{1,0:T(8,128)(2,1)S(1)}, bf16[768,512]{1,0:T(8,128)(2,1)S(1)}, u32[]{:S(2)}, u32[]{:S(2)}) collective-permute-start(bf16[768,512]{1,0:T(8,128)(2,1)S(1)} %dynamic-slice_bitcast_fusion.6), channel_id=1, source_target_pairs={{0,16},{8,24},{16,0},{24,8},{1,17},{9,25},{17,1},{25,9},{2,18},{10... | collective-permute-start | bytes 2359304 | tf_op jit(solution)/shard_map/ppermute | solution.py:29
  407.3 46.7 %collective-permute-start.21 = (bf16[512,768]{1,0:T(8,128)(2,1)S(1)}, bf16[512,768]{1,0:T(8,128)(2,1)S(1)}, u32[]{:S(2)}, u32[]{:S(2)}) collective-permute-start(bf16[512,768]{1,0:T(8,128)(2,1)S(1)} %dynamic-slice_bitcast_fusion.5), channel_id=1, source_target_pairs={{0,16},{8,24},{16,0},{24,8},{1,17},{9,25},{17,1},{25,9},{2,18},{10... | collective-permute-start | bytes 2359304 | tf_op jit(solution)/shard_map/ppermute | solution.py:29
  408.3 10.0 %copy-start.7 = (bf16[768,512]{1,0:T(8,128)(2,1)}, bf16[768,512]{1,0:T(8,128)(2,1)S(1)}, u32[]{:S(2)}) copy-start(bf16[768,512]{1,0:T(8,128)(2,1)S(1)} %fusion.7) | copy-start | bytes 2359300
  408.3 46.8 %collective-permute-start.12 = (bf16[768,512]{1,0:T(8,128)(2,1)S(1)}, bf16[768,512]{1,0:T(8,128)(2,1)S(1)}, u32[]{:S(2)}, u32[]{:S(2)}) collective-permute-start(bf16[768,512]{1,0:T(8,128)(2,1)S(1)} %fusion.7), channel_id=1, source_target_pairs={{0,4},{2,6},{4,0},{6,2},{1,5},{3,7},{5,1},{7,3},{8,12},{10,14},{12... | collective-permute-start | bytes 2359304 | tf_op jit(solution)/shard_map/ppermute | solution.py:29
  415.9 2.0 copy-start.2
  415.9 2.4 copy-start.4
  418.4 41.8 %copy-start.23 = (s32[4]{0:T(128)S(1)}, s32[4]{0:T(128)}, u32[]{:S(2)}) copy-start(s32[4]{0:T(128)} %constant.212.clone) | copy-start | bytes 52
  418.4 86.1 %collective-permute-start.9 = (bf16[16,112,768]{2,1,0:T(8,128)(2,1)}, bf16[16,112,768]{2,1,0:T(8,128)(2,1)}, u32[]{:S(2)}, u32[]{:S(2)}) collective-permute-start(bf16[16,112,768]{2,1,0:T(8,128)(2,1)} %pad_maximum_fusion.3), channel_id=1, source_target_pairs={{0,2},{2,0},{4,6},{6,4},{1,3},{3,1},{5,7},{7,5},{8,10},{10,8},{12,... | collective-permute-start | bytes 8257544 | tf_op jit(solution)/shard_map/ppermute | solution.py:29
  418.4 36.9 %collective-permute-start.13 = (bf16[768,512]{1,0:T(8,128)(2,1)S(1)}, bf16[768,512]{1,0:T(8,128)(2,1)S(1)}, u32[]{:S(2)}, u32[]{:S(2)}) collective-permute-start(bf16[768,512]{1,0:T(8,128)(2,1)S(1)} %fusion.7), channel_id=1, source_target_pairs={{0,2},{2,0},{4,6},{6,4},{1,3},{3,1},{5,7},{7,5},{8,10},{10,8},{12,... | collective-permute-start | bytes 2359304 | tf_op jit(solution)/shard_map/ppermute | solution.py:29
  444.6 15.5 %collective-permute-start.17 = (bf16[768,512]{1,0:T(8,128)(2,1)}, bf16[768,512]{1,0:T(8,128)(2,1)}, u32[]{:S(2)}, u32[]{:S(2)}) collective-permute-start(bf16[768,512]{1,0:T(8,128)(2,1)} %fusion.6), channel_id=1, source_target_pairs={{0,4},{2,6},{4,0},{6,2},{1,5},{3,7},{5,1},{7,3},{8,12},{10,14},{12... | collective-permute-start | bytes 2359304 | tf_op jit(solution)/shard_map/ppermute | solution.py:29
  455.1 18.6 %collective-permute-start.22 = (bf16[512,768]{1,0:T(8,128)(2,1)}, bf16[512,768]{1,0:T(8,128)(2,1)}, u32[]{:S(2)}, u32[]{:S(2)}) collective-permute-start(bf16[512,768]{1,0:T(8,128)(2,1)} %fusion.5), channel_id=1, source_target_pairs={{0,4},{2,6},{4,0},{6,2},{1,5},{3,7},{5,1},{7,3},{8,12},{10,14},{12... | collective-permute-start | bytes 2359304 | tf_op jit(solution)/shard_map/ppermute | solution.py:29
  455.1 19.2 %copy-start.17 = (bf16[768,512]{1,0:T(8,128)(2,1)}, bf16[768,512]{1,0:T(8,128)(2,1)S(1)}, u32[]{:S(2)}) copy-start(bf16[768,512]{1,0:T(8,128)(2,1)S(1)} %collective-permute-done.12) | copy-start | bytes 2359300
  455.1 18.6 %collective-permute-start.14 = (bf16[768,512]{1,0:T(8,128)(2,1)S(1)}, bf16[768,512]{1,0:T(8,128)(2,1)S(1)}, u32[]{:S(2)}, u32[]{:S(2)}) collective-permute-start(bf16[768,512]{1,0:T(8,128)(2,1)S(1)} %collective-permute-done.12), channel_id=1, source_target_pairs={{0,2},{2,0},{4,6},{6,4},{1,3},{3,1},{5,7},{7,5},{8,10},{10,8},{12,... | collective-permute-start | bytes 2359304 | tf_op jit(solution)/shard_map/ppermute | solution.py:29
  455.2 19.1 %copy-start.18 = (bf16[768,512]{1,0:T(8,128)(2,1)}, bf16[768,512]{1,0:T(8,128)(2,1)S(1)}, u32[]{:S(2)}) copy-start(bf16[768,512]{1,0:T(8,128)(2,1)S(1)} %collective-permute-done.13) | copy-start | bytes 2359300
  455.2 29.4 %collective-permute-start.18 = (bf16[768,512]{1,0:T(8,128)(2,1)}, bf16[768,512]{1,0:T(8,128)(2,1)}, u32[]{:S(2)}, u32[]{:S(2)}) collective-permute-start(bf16[768,512]{1,0:T(8,128)(2,1)} %fusion.6), channel_id=1, source_target_pairs={{0,2},{2,0},{4,6},{6,4},{1,3},{3,1},{5,7},{7,5},{8,10},{10,8},{12,... | collective-permute-start | bytes 2359304 | tf_op jit(solution)/shard_map/ppermute | solution.py:29
  460.1 24.5 %collective-permute-start.19 = (bf16[768,512]{1,0:T(8,128)(2,1)}, bf16[768,512]{1,0:T(8,128)(2,1)}, u32[]{:S(2)}, u32[]{:S(2)}) collective-permute-start(bf16[768,512]{1,0:T(8,128)(2,1)} %collective-permute-done.17), channel_id=1, source_target_pairs={{0,2},{2,0},{4,6},{6,4},{1,3},{3,1},{5,7},{7,5},{8,10},{10,8},{12,... | collective-permute-start | bytes 2359304 | tf_op jit(solution)/shard_map/ppermute | solution.py:29
  473.8 20.8 %collective-permute-start.23 = (bf16[512,768]{1,0:T(8,128)(2,1)}, bf16[512,768]{1,0:T(8,128)(2,1)}, u32[]{:S(2)}, u32[]{:S(2)}) collective-permute-start(bf16[512,768]{1,0:T(8,128)(2,1)} %fusion.5), channel_id=1, source_target_pairs={{0,2},{2,0},{4,6},{6,4},{1,3},{3,1},{5,7},{7,5},{8,10},{10,8},{12,... | collective-permute-start | bytes 2359304 | tf_op jit(solution)/shard_map/ppermute | solution.py:29
  473.8 0.9 copy-start.19
  473.8 20.8 %collective-permute-start.24 = (bf16[512,768]{1,0:T(8,128)(2,1)}, bf16[512,768]{1,0:T(8,128)(2,1)}, u32[]{:S(2)}, u32[]{:S(2)}) collective-permute-start(bf16[512,768]{1,0:T(8,128)(2,1)} %collective-permute-done.22), channel_id=1, source_target_pairs={{0,2},{2,0},{4,6},{6,4},{1,3},{3,1},{5,7},{7,5},{8,10},{10,8},{12,... | collective-permute-start | bytes 2359304 | tf_op jit(solution)/shard_map/ppermute | solution.py:29
  499.1 5.3 %copy-start.3 = (bf16[8,112,768]{2,1,0:T(8,128)(2,1)S(1)}, bf16[8,112,768]{2,1,0:T(8,128)(2,1)}, u32[]{:S(2)}) copy-start(bf16[8,112,768]{2,1,0:T(8,128)(2,1)} %copy-done.2) | copy-start | bytes 4128772
  499.1 5.3 %copy-start.5 = (bf16[8,112,768]{2,1,0:T(8,128)(2,1)S(1)}, bf16[8,112,768]{2,1,0:T(8,128)(2,1)}, u32[]{:S(2)}) copy-start(bf16[8,112,768]{2,1,0:T(8,128)(2,1)} %copy-done.4) | copy-start | bytes 4128772
  506.5 4.9 copy-start
  512.7 9.1 %copy-start.21 = (bf16[384,768]{1,0:T(8,128)(2,1)S(1)}, bf16[384,768]{1,0:T(8,128)(2,1)}, u32[]{:S(2)}) copy-start(bf16[384,768]{1,0:T(8,128)(2,1)} %get-tuple-element.53) | copy-start | bytes 1769476
  512.7 9.9 %copy-start.16 = (f32[384,768]{1,0:T(8,128)S(1)}, f32[384,768]{1,0:T(8,128)}, u32[]{:S(2)}) copy-start(f32[384,768]{1,0:T(8,128)} %get-tuple-element.54) | copy-start | bytes 3538948
  520.5 3.1 copy-start.22
